TPU v7x, 512 devices: a whole 4x8x8 slice. The times are simulated.
512 devices in a mesh: dom: 512 (over x, y, z, core).
Axes of the slice: x: 4, y: 8, z: 8, core: 2. Of those that a mesh axis runs over, the one named last changes fastest.
Arguments:
- saved_states: float32 [4, 3, 28, 65536], P(None, None, None, 'dom'), may hold values from -3.375 to 3.75, as said below
- adjoint_final: float32 [3, 28, 65536], P(None, None, 'dom'), may hold values from -6 to 6
- bathymetry: float32 [28, 65536], P(None, 'dom'), may hold values from 0.7 to 3.9
- wind_speed: float32 [28, 65536], P(None, 'dom'), may hold values from 0.5 to 1.5
- wind_angle: float32 [28, 65536], P(None, 'dom'), may hold values from -3.140625 to 3.140625
- drag_rate: float32 [1], replicated, may hold values from 2 to 8
- metrics: float32 [4, 65536], P(None, 'dom'), may hold values from -0.42 to 1.82
- face_link: int32 [3, 65536], P(None, 'dom'), may hold values from 0 to 511, as said below
- face_tag: int32 [3, 65536], P(None, 'dom'), may hold values from 0 to 2, as said below
- send_faces: int32 [8, 8192], P(None, 'dom'), may hold values from -1 to 383, as said below
Outputs:
- initial_adjoint: float32 [3, 28, 65536], P(None, None, 'dom')
- depth_gradient: float32 [28, 65536], P(None, 'dom')
- speed_gradient: float32 [28, 65536], P(None, 'dom')
- angle_gradient: float32 [28, 65536], P(None, 'dom')
- drag_gradient: float32 [1], replicated
Inputs may be any that keep to these rules, and one draw needn't show every extreme that they name: `send_faces`: row j lists the faces (local index f * 128 + e) that this device shares with the device at offset j + 1 (j < 4) or 4 - j - 1 (otherwise), in slots 0 to n - 1, and -1 in the other slots; that neighbor's row toward this device has the same n, and slot c of both names the two sides of one face. n is at most 16, equals 16 for some pair in every draw, and some device has n = 16 in all 8 rows. No face is listed twice and no row leads past the ends of the axis. `face_link`: A value below 384 names the partner face on the same device, which links back; 384 + j * 16 + c means the face stands in slot c of row j of send_faces; a face with face_tag 1 or 2 links to itself. `face_tag`: 0 for faces with a partner, 1 for walls, 2 for open boundaries. `saved_states`: heights (component 0) lie between 0.75 and 3.75.
All inputs are finite; a program needn't handle non-finite values.
Results may differ from a plain program's by a relative error of at most 0.0003.
Values sent between devices are 32-bit elements; how exact they have to be, the bound alone decides.
No kernel may reach another device: no remote copies, remote signals or barrier semaphores. Data moves between devices by JAX's collectives and lax.ppermute only.
A program may use at most 64 MiB of HBM per device.

v0:
```python
import math

import jax
import jax.numpy as jnp
import numpy as np
from jax import lax
from jax.sharding import PartitionSpec as P

GRAVITY = 1.0
PENALTY = 3.0
WIND_COEF = 5.0
TIME_STEP = 0.01


def passed_along(x, axis, by):
    devices = lax.axis_size(axis)
    pairs = [(i, i + by) for i in range(devices) if 0 <= i + by < devices]
    return lax.ppermute(x, axis, pairs)


def solve_dense(matrix, right):
    system = np.array(matrix) + 0.0
    result = np.array(right) + 0.0
    extent = system.shape[0]
    for column in range(extent):
        pivot_index = column + int(np.argmax(np.abs(system[column:, column])))
        system[[column, pivot_index]] = system[[pivot_index, column]]
        result[[column, pivot_index]] = result[[pivot_index, column]]
        for target in range(column + 1, extent):
            factor = system[target, column] / system[column, column]
            system[target] = system[target] - factor * system[column]
            result[target] = result[target] - factor * result[column]
    solution = np.zeros(result.shape)
    for column in range(extent - 1, -1, -1):
        solution[column] = (
            result[column] - system[column, column + 1 :] @ solution[column + 1 :]
        ) / system[column, column]
    return solution


def element_tables():
    degree = 6
    nodes = [
        (column, row_index)
        for row_index in range(degree + 1)
        for column in range(degree + 1 - row_index)
    ]
    node_total = len(nodes)
    coord_x = np.array([node[0] / degree for node in nodes])
    coord_y = np.array([node[1] / degree for node in nodes])
    vander = np.zeros((node_total, node_total))
    vander_r = np.zeros((node_total, node_total))
    vander_s = np.zeros((node_total, node_total))
    grams = np.zeros((node_total, node_total))
    for column_index, power in enumerate(nodes):
        first, second = power
        vander[:, column_index] = coord_x**first * coord_y**second
        if first > 0:
            vander_r[:, column_index] = 0.5 * first * coord_x ** (first - 1) * coord_y**second
        if second > 0:
            vander_s[:, column_index] = 0.5 * second * coord_x**first * coord_y ** (second - 1)
        for other_index, other_power in enumerate(nodes):
            sum_x = first + other_power[0]
            sum_y = second + other_power[1]
            grams[column_index, other_index] = (
                4.0
                * math.factorial(sum_x)
                * math.factorial(sum_y)
                / math.factorial(sum_x + sum_y + 2)
            )
    deriv_r = solve_dense(vander.T, vander_r.T).T
    deriv_s = solve_dense(vander.T, vander_s.T).T
    mass_inverse = vander @ solve_dense(grams, vander.T)
    points = np.arange(degree + 1) / degree
    line_vander = np.stack([points**power for power in range(degree + 1)], axis=1)
    line_grams = np.array(
        [
            [2.0 / (first + second + 1) for second in range(degree + 1)]
            for first in range(degree + 1)
        ]
    )
    line_inverse = solve_dense(line_vander, np.eye(degree + 1))
    line_mass = line_inverse.T @ line_grams @ line_inverse
    lookup = {node: number for number, node in enumerate(nodes)}
    face_nodes = [
        [lookup[step, 0] for step in range(degree + 1)],
        [lookup[degree - step, step] for step in range(degree + 1)],
        [lookup[0, degree - step] for step in range(degree + 1)],
    ]
    embed = np.zeros((node_total, 3 * (degree + 1)))
    extract = np.zeros((3 * (degree + 1), node_total))
    for face_index in range(3):
        for step in range(degree + 1):
            extract[face_index * (degree + 1) + step, face_nodes[face_index][step]] = 1.0
            for other_step in range(degree + 1):
                embed[
                    face_nodes[face_index][other_step], face_index * (degree + 1) + step
                ] += line_mass[other_step, step]
    lifting = mass_inverse @ embed
    return (
        jnp.asarray(deriv_r, jnp.float32),
        jnp.asarray(deriv_s, jnp.float32),
        jnp.asarray(lifting, jnp.float32),
        jnp.asarray(extract, jnp.float32),
    )


def face_fluxes(values):
    height = values[0]
    velocity_x = values[1] / height
    velocity_y = values[2] / height
    pressure = 0.5 * GRAVITY * height * height
    flux_x = jnp.stack([values[1], values[1] * velocity_x + pressure, values[2] * velocity_x])
    flux_y = jnp.stack([values[2], values[1] * velocity_y, values[2] * velocity_y + pressure])
    return (flux_x, flux_y)


def face_values(state_now, extract):
    elements = state_now.shape[-1]
    face_rows = jnp.einsum("ij,cjk->cik", extract, state_now, precision=lax.Precision.HIGHEST)
    return face_rows.reshape(3, 3, 7, elements).transpose(0, 2, 1, 3).reshape(3, 7, 3 * elements)


def node_values(faces_in, extract):
    elements = faces_in.shape[-1] // 3
    face_rows = faces_in.reshape(3, 7, 3, elements).transpose(0, 2, 1, 3).reshape(3, 21, elements)
    return jnp.einsum("ji,cjk->cik", extract, face_rows, precision=lax.Precision.HIGHEST)


def tendency(
    state_now, outer, depth_field, speed_field, angle_field, drag_rate, metrics, face_tag, tables
):
    deriv_r, deriv_s, lifting, extract = tables
    highest = lax.Precision.HIGHEST
    elements = state_now.shape[-1]
    height = state_now[0]
    velocity_x = state_now[1] / height
    velocity_y = state_now[2] / height
    flux_x, flux_y = face_fluxes(state_now)
    fields = jnp.concatenate([flux_x, flux_y, depth_field[None]], axis=0)
    along_r = jnp.einsum("ij,cjk->cik", deriv_r, fields, precision=highest)
    along_s = jnp.einsum("ij,cjk->cik", deriv_s, fields, precision=highest)
    r_wrt_x, r_wrt_y, s_wrt_x, s_wrt_y = (metrics[0], metrics[1], metrics[2], metrics[3])
    gradient_x = r_wrt_x * along_r + s_wrt_x * along_s
    gradient_y = r_wrt_y * along_r + s_wrt_y * along_s
    divergence = gradient_x[0:3] + gradient_y[3:6]
    stress = WIND_COEF * speed_field * speed_field
    source_x = (
        GRAVITY * height * gradient_x[6] + stress * jnp.cos(angle_field) - drag_rate[0] * velocity_x
    )
    source_y = (
        GRAVITY * height * gradient_y[6] + stress * jnp.sin(angle_field) - drag_rate[0] * velocity_y
    )
    inner = jnp.einsum("ij,cjk->cik", extract, state_now, precision=highest).reshape(
        3, 3, 7, elements
    )
    depth_face = jnp.dot(extract, depth_field, precision=highest).reshape(3, 7, elements)
    given = jnp.flip(outer.reshape(3, 7, 3, elements), axis=1).transpose(0, 2, 1, 3)
    normal_x = jnp.stack([-s_wrt_x, r_wrt_x + s_wrt_x, -r_wrt_x])[:, None, :]
    normal_y = jnp.stack([-s_wrt_y, r_wrt_y + s_wrt_y, -r_wrt_y])[:, None, :]
    face_scale = jnp.sqrt(normal_x * normal_x + normal_y * normal_y)
    unit_x = normal_x / face_scale
    unit_y = normal_y / face_scale
    wall_mask = (face_tag == 1)[:, None, :]
    open_mask = (face_tag == 2)[:, None, :]
    normal_momentum = inner[1] * unit_x + inner[2] * unit_y
    outside_height = jnp.where(wall_mask, inner[0], jnp.where(open_mask, depth_face, given[0]))
    outside_first = jnp.where(
        wall_mask,
        inner[1] - 2.0 * normal_momentum * unit_x,
        jnp.where(open_mask, inner[1], given[1]),
    )
    outside_second = jnp.where(
        wall_mask,
        inner[2] - 2.0 * normal_momentum * unit_y,
        jnp.where(open_mask, inner[2], given[2]),
    )
    outside = jnp.stack([outside_height, outside_first, outside_second])
    inner_fx, inner_fy = face_fluxes(inner)
    outer_fx, outer_fy = face_fluxes(outside)
    flux_jump = 0.5 * (
        normal_x * (inner_fx - outer_fx) + normal_y * (inner_fy - outer_fy)
    ) - 0.5 * PENALTY * face_scale * (inner - outside)
    lifted = jnp.einsum(
        "ij,cjk->cik", lifting, flux_jump.reshape(3, 21, elements), precision=highest
    )
    sources = jnp.stack([jnp.zeros_like(height), source_x, source_y])
    return lifted - divergence + sources


def section_adjoint(
    state_now,
    outer,
    depth_field,
    speed_field,
    angle_field,
    drag_rate,
    metrics,
    face_tag,
    tables,
    weight,
):

    def local_map(state_in, outer_in, depth_in, speed_in, angle_in, drag_in):
        return tendency(
            state_in, outer_in, depth_in, speed_in, angle_in, drag_in, metrics, face_tag, tables
        )

    unused, pullback = jax.vjp(
        local_map, state_now, outer, depth_field, speed_field, angle_field, drag_rate
    )
    return pullback(weight)


def offset_of(direction, reach_count):
    if direction < reach_count:
        return direction + 1
    return reach_count - direction - 1


def pack_slots(values, send_faces):
    safe_index = jnp.where(send_faces < 0, 0, send_faces).reshape(-1)
    packed = jnp.take(values, safe_index, axis=-1)
    return packed.reshape(values.shape[:-1] + send_faces.shape)


def local(
    saved_states,
    adjoint_final,
    bathymetry,
    wind_speed,
    wind_angle,
    drag_rate,
    metrics,
    face_link,
    face_tag,
    send_faces,
):
    tables = element_tables()
    extract = tables[3]
    directions = send_faces.shape[0]
    reach_count = directions // 2
    links = face_link.reshape(-1)
    interior = face_tag.reshape(-1) == 0

    def drag_part(drag_term):
        return lax.psum(drag_term, "dom")

    def one_section(section_index, weight):
        state_now = saved_states[section_index]
        own = face_values(state_now, extract)
        slot_boxes = pack_slots(own, send_faces)
        pieces = []
        for direction in range(directions):
            facing = (direction + reach_count) % directions
            pieces.append(
                passed_along(slot_boxes[..., facing, :], "dom", -offset_of(direction, reach_count))
            )
        received = jnp.concatenate(pieces, axis=-1)
        outer = jnp.take(jnp.concatenate([own, received], axis=-1), links, axis=-1)
        terms = section_adjoint(
            state_now,
            outer,
            bathymetry,
            wind_speed,
            wind_angle,
            drag_rate,
            metrics,
            face_tag,
            tables,
            weight,
        )
        back_boxes = pack_slots(terms[1], send_faces)
        back_pieces = []
        for direction in range(directions):
            facing = (direction + reach_count) % directions
            back_pieces.append(
                passed_along(back_boxes[..., facing, :], "dom", -offset_of(direction, reach_count))
            )
        back_pool = jnp.concatenate([terms[1]] + back_pieces, axis=-1)
        gathered = jnp.where(interior, jnp.take(back_pool, links, axis=-1), 0.0)
        state_term = terms[0] + node_values(gathered, extract)
        return (state_term, terms[2], terms[3], terms[4], drag_part(terms[5]))

    half_step = 0.5 * TIME_STEP
    adjoint = adjoint_final
    state_term, depth_sum, speed_sum, angle_sum, drag_sum = one_section(3, half_step * adjoint)
    adjoint = adjoint + state_term
    state_term, depth_term, speed_term, angle_term, drag_term = one_section(
        2, TIME_STEP / 6.0 * adjoint
    )
    kept = 2.0 / 3.0 * adjoint
    adjoint = adjoint / 3.0 + state_term
    depth_sum, speed_sum, angle_sum, drag_sum = (
        depth_sum + depth_term,
        speed_sum + speed_term,
        angle_sum + angle_term,
        drag_sum + drag_term,
    )
    state_term, depth_term, speed_term, angle_term, drag_term = one_section(1, half_step * adjoint)
    adjoint = adjoint + state_term
    depth_sum, speed_sum, angle_sum, drag_sum = (
        depth_sum + depth_term,
        speed_sum + speed_term,
        angle_sum + angle_term,
        drag_sum + drag_term,
    )
    state_term, depth_term, speed_term, angle_term, drag_term = one_section(0, half_step * adjoint)
    adjoint = kept + adjoint + state_term
    depth_sum, speed_sum, angle_sum, drag_sum = (
        depth_sum + depth_term,
        speed_sum + speed_term,
        angle_sum + angle_term,
        drag_sum + drag_term,
    )
    return (adjoint, depth_sum, speed_sum, angle_sum, drag_sum)


def solution(mesh):
    return jax.shard_map(
        local,
        mesh=mesh,
        in_specs=(
            P(None, None, None, "dom"),
            P(None, None, "dom"),
            P(None, "dom"),
            P(None, "dom"),
            P(None, "dom"),
            P(),
            P(None, "dom"),
            P(None, "dom"),
            P(None, "dom"),
            P(None, "dom"),
        ),
        out_specs=(P(None, None, "dom"), P(None, "dom"), P(None, "dom"), P(None, "dom"), P()),
        check_vma=False,
    )
```

profile of v0, /device:TPU:2, one launch (start us, length us, event | category | flops | bytes accessed | tf_op | source)
XLA Modules:
  0.0 497.8 jit_solution(8471316597688078849)
XLA Ops:
  13.0 13.3 %collective-permute-start = (f32[3,7,16]{1,0,2:T(4,128)}, f32[3,7,16]{1,0,2:T(4,128)}, u32[]{:S(2)}, u32[]{:S(2)}) collective-permute-start(f32[3,7,16]{1,0,2:T(4,128)} %get-tuple-element.190), channel_id=1, source_target_pairs={{1,0},{2,1},{3,2},{4,3},{5,4},{6,5},{7,6},{8,7},{9,8},{10,9},{11,1... | collective-permute-start | bytes 4040 | tf_op jit(solution)/shard_map/ppermute | solution.py:18
  71.1 4.4 collective-permute-start.6
  76.9 4.4 collective-permute-start.7
  82.8 7.4 %collective-permute-start.32 = (f32[3,7,16]{1,0,2:T(4,128)S(1)}, f32[3,7,16]{1,0,2:T(4,128)S(1)}, u32[]{:S(2)}, u32[]{:S(2)}) collective-permute-start(f32[3,7,16]{1,0,2:T(4,128)S(1)} %copy-done.106), channel_id=1, source_target_pairs={{1,0},{2,1},{3,2},{4,3},{5,4},{6,5},{7,6},{8,7},{9,8},{10,9},{11,1... | collective-permute-start | bytes 4040 | tf_op jit(solution)/shard_map/ppermute | solution.py:18
  107.7 4.2 collective-permute-start.38
  112.6 4.6 collective-permute-start.39
  117.8 7.3 %collective-permute-start.16 = (f32[3,7,16]{1,0,2:T(4,128)S(1)}, f32[3,7,16]{1,0,2:T(4,128)S(1)}, u32[]{:S(2)}, u32[]{:S(2)}) collective-permute-start(f32[3,7,16]{1,0,2:T(4,128)S(1)} %get-tuple-element.174), channel_id=1, source_target_pairs={{1,0},{2,1},{3,2},{4,3},{5,4},{6,5},{7,6},{8,7},{9,8},{10,9},{11,1... | collective-permute-start | bytes 4040 | tf_op jit(solution)/shard_map/ppermute | solution.py:18
  141.1 4.2 collective-permute-start.22
  146.0 4.6 collective-permute-start.23
  151.2 7.3 %collective-permute-start.48 = (f32[3,7,16]{1,0,2:T(4,128)S(1)}, f32[3,7,16]{1,0,2:T(4,128)S(1)}, u32[]{:S(2)}, u32[]{:S(2)}) collective-permute-start(f32[3,7,16]{1,0,2:T(4,128)S(1)} %get-tuple-element.142), channel_id=1, source_target_pairs={{1,0},{2,1},{3,2},{4,3},{5,4},{6,5},{7,6},{8,7},{9,8},{10,9},{11,1... | collective-permute-start | bytes 4040 | tf_op jit(solution)/shard_map/ppermute | solution.py:18
  173.9 4.3 collective-permute-start.54
  178.2 4.8 collective-permute-start.55
  212.2 5.8 %collective-permute-start.8 = (f32[3,7,16]{1,0,2:T(4,128)S(1)}, f32[3,7,16]{1,0,2:T(4,128)}, u32[]{:S(2)}, u32[]{:S(2)}) collective-permute-start(f32[3,7,16]{1,0,2:T(4,128)S(1)} %get-tuple-element.182), channel_id=1, source_target_pairs={{1,0},{2,1},{3,2},{4,3},{5,4},{6,5},{7,6},{8,7},{9,8},{10,9},{11,1... | collective-permute-start | bytes 4040 | tf_op jit(solution)/shard_map/ppermute | solution.py:18
  237.4 4.2 collective-permute-start.14
  243.0 4.6 collective-permute-start.15
  264.5 4.1 collective-permute-start.24
  287.4 4.3 collective-permute-start.30
  291.7 5.0 %collective-permute-start.31 = (f32[3,7,16]{1,0,2:T(4,128)S(1)}, f32[3,7,16]{1,0,2:T(4,128)S(1)}, u32[]{:S(2)}, u32[]{:S(2)}) collective-permute-start(f32[3,7,16]{1,0,2:T(4,128)S(1)} %get-tuple-element.159), channel_id=1, source_target_pairs={{0,4},{1,5},{2,6},{3,7},{4,8},{5,9},{6,10},{7,11},{8,12},{9,13},{1... | collective-permute-start | bytes 4040 | tf_op jit(solution)/shard_map/ppermute | solution.py:18
  298.1 4.5 collective-permute-done.31
  336.5 6.0 %collective-permute-start.47 = (f32[3,7,16]{1,0,2:T(4,128)S(1)}, f32[3,7,16]{1,0,2:T(4,128)S(1)}, u32[]{:S(2)}, u32[]{:S(2)}) collective-permute-start(f32[3,7,16]{1,0,2:T(4,128)S(1)} %get-tuple-element.143), channel_id=1, source_target_pairs={{0,4},{1,5},{2,6},{3,7},{4,8},{5,9},{6,10},{7,11},{8,12},{9,13},{1... | collective-permute-start | bytes 4040 | tf_op jit(solution)/shard_map/ppermute | solution.py:18
  343.5 4.1 collective-permute-done.47
  366.5 96.3 %psum.34 = f32[1]{0:T(128)} all-reduce(f32[1]{0:T(128)} %bitcast.225), channel_id=1, replica_groups=mesh['dom'=512] {'dom'}, use_global_device_ids=true, to_apply=%region_2.5 | all-reduce | flops 1 | bytes 8 | tf_op jit(solution)/shard_map/psum | solution.py:247
  462.8 4.3 collective-permute-start.57
  469.4 4.5 collective-permute-start.59
  (687 shorter events, 270.1 us)
Async XLA Ops:
  13.0 53.3 %collective-permute-start = (f32[3,7,16]{1,0,2:T(4,128)}, f32[3,7,16]{1,0,2:T(4,128)}, u32[]{:S(2)}, u32[]{:S(2)}) collective-permute-start(f32[3,7,16]{1,0,2:T(4,128)} %get-tuple-element.190), channel_id=1, source_target_pairs={{1,0},{2,1},{3,2},{4,3},{5,4},{6,5},{7,6},{8,7},{9,8},{10,9},{11,1... | collective-permute-start | bytes 4040 | tf_op jit(solution)/shard_map/ppermute | solution.py:18
  26.3 44.8 %collective-permute-start.1 = (f32[3,7,16]{1,0,2:T(4,128)}, f32[3,7,16]{1,0,2:T(4,128)}, u32[]{:S(2)}, u32[]{:S(2)}) collective-permute-start(f32[3,7,16]{1,0,2:T(4,128)} %get-tuple-element.189), channel_id=1, source_target_pairs={{2,0},{3,1},{4,2},{5,3},{6,4},{7,5},{8,6},{9,7},{10,8},{11,9},{12,... | collective-permute-start | bytes 4040 | tf_op jit(solution)/shard_map/ppermute | solution.py:18
  28.8 48.1 %collective-permute-start.2 = (f32[3,7,16]{1,0,2:T(4,128)}, f32[3,7,16]{1,0,2:T(4,128)}, u32[]{:S(2)}, u32[]{:S(2)}) collective-permute-start(f32[3,7,16]{1,0,2:T(4,128)} %get-tuple-element.188), channel_id=1, source_target_pairs={{3,0},{4,1},{5,2},{6,3},{7,4},{8,5},{9,6},{10,7},{11,8},{12,9},{13... | collective-permute-start | bytes 4040 | tf_op jit(solution)/shard_map/ppermute | solution.py:18
  31.1 51.7 %collective-permute-start.3 = (f32[3,7,16]{1,0,2:T(4,128)}, f32[3,7,16]{1,0,2:T(4,128)}, u32[]{:S(2)}, u32[]{:S(2)}) collective-permute-start(f32[3,7,16]{1,0,2:T(4,128)} %get-tuple-element.187), channel_id=1, source_target_pairs={{4,0},{5,1},{6,2},{7,3},{8,4},{9,5},{10,6},{11,7},{12,8},{13,9},{1... | collective-permute-start | bytes 4040 | tf_op jit(solution)/shard_map/ppermute | solution.py:18
  33.3 58.3 %collective-permute-start.4 = (f32[3,7,16]{1,0,2:T(4,128)}, f32[3,7,16]{1,0,2:T(4,128)}, u32[]{:S(2)}, u32[]{:S(2)}) collective-permute-start(f32[3,7,16]{1,0,2:T(4,128)} %get-tuple-element.186), channel_id=1, source_target_pairs={{0,1},{1,2},{2,3},{3,4},{4,5},{5,6},{6,7},{7,8},{8,9},{9,10},{10,1... | collective-permute-start | bytes 4040 | tf_op jit(solution)/shard_map/ppermute | solution.py:18
  66.4 29.1 %collective-permute-start.5 = (f32[3,7,16]{1,0,2:T(4,128)S(1)}, f32[3,7,16]{1,0,2:T(4,128)S(1)}, u32[]{:S(2)}, u32[]{:S(2)}) collective-permute-start(f32[3,7,16]{1,0,2:T(4,128)S(1)} %copy-done.104), channel_id=1, source_target_pairs={{0,2},{1,3},{2,4},{3,5},{4,6},{5,7},{6,8},{7,9},{8,10},{9,11},{10,... | collective-permute-start | bytes 4040 | tf_op jit(solution)/shard_map/ppermute | solution.py:18
  71.1 26.9 %collective-permute-start.6 = (f32[3,7,16]{1,0,2:T(4,128)S(1)}, f32[3,7,16]{1,0,2:T(4,128)S(1)}, u32[]{:S(2)}, u32[]{:S(2)}) collective-permute-start(f32[3,7,16]{1,0,2:T(4,128)S(1)} %copy-done.103), channel_id=1, source_target_pairs={{0,3},{1,4},{2,5},{3,6},{4,7},{5,8},{6,9},{7,10},{8,11},{9,12},{10... | collective-permute-start | bytes 4040 | tf_op jit(solution)/shard_map/ppermute | solution.py:18
  76.9 24.2 %collective-permute-start.7 = (f32[3,7,16]{1,0,2:T(4,128)S(1)}, f32[3,7,16]{1,0,2:T(4,128)S(1)}, u32[]{:S(2)}, u32[]{:S(2)}) collective-permute-start(f32[3,7,16]{1,0,2:T(4,128)S(1)} %copy-done.102), channel_id=1, source_target_pairs={{0,4},{1,5},{2,6},{3,7},{4,8},{5,9},{6,10},{7,11},{8,12},{9,13},{1... | collective-permute-start | bytes 4040 | tf_op jit(solution)/shard_map/ppermute | solution.py:18
  82.8 21.2 %collective-permute-start.32 = (f32[3,7,16]{1,0,2:T(4,128)S(1)}, f32[3,7,16]{1,0,2:T(4,128)S(1)}, u32[]{:S(2)}, u32[]{:S(2)}) collective-permute-start(f32[3,7,16]{1,0,2:T(4,128)S(1)} %copy-done.106), channel_id=1, source_target_pairs={{1,0},{2,1},{3,2},{4,3},{5,4},{6,5},{7,6},{8,7},{9,8},{10,9},{11,1... | collective-permute-start | bytes 4040 | tf_op jit(solution)/shard_map/ppermute | solution.py:18
  101.1 24.6 %collective-permute-start.36 = (f32[3,7,16]{1,0,2:T(4,128)S(1)}, f32[3,7,16]{1,0,2:T(4,128)S(1)}, u32[]{:S(2)}, u32[]{:S(2)}) collective-permute-start(f32[3,7,16]{1,0,2:T(4,128)S(1)} %get-tuple-element.154), channel_id=1, source_target_pairs={{0,1},{1,2},{2,3},{3,4},{4,5},{5,6},{6,7},{7,8},{8,9},{9,10},{10,1... | collective-permute-start | bytes 4040 | tf_op jit(solution)/shard_map/ppermute | solution.py:18
  104.0 24.8 %collective-permute-start.37 = (f32[3,7,16]{1,0,2:T(4,128)S(1)}, f32[3,7,16]{1,0,2:T(4,128)S(1)}, u32[]{:S(2)}, u32[]{:S(2)}) collective-permute-start(f32[3,7,16]{1,0,2:T(4,128)S(1)} %get-tuple-element.153), channel_id=1, source_target_pairs={{0,2},{1,3},{2,4},{3,5},{4,6},{5,7},{6,8},{7,9},{8,10},{9,11},{10,... | collective-permute-start | bytes 4040 | tf_op jit(solution)/shard_map/ppermute | solution.py:18
  107.7 23.6 %collective-permute-start.38 = (f32[3,7,16]{1,0,2:T(4,128)S(1)}, f32[3,7,16]{1,0,2:T(4,128)S(1)}, u32[]{:S(2)}, u32[]{:S(2)}) collective-permute-start(f32[3,7,16]{1,0,2:T(4,128)S(1)} %get-tuple-element.152), channel_id=1, source_target_pairs={{0,3},{1,4},{2,5},{3,6},{4,7},{5,8},{6,9},{7,10},{8,11},{9,12},{10... | collective-permute-start | bytes 4040 | tf_op jit(solution)/shard_map/ppermute | solution.py:18
  112.6 21.9 %collective-permute-start.39 = (f32[3,7,16]{1,0,2:T(4,128)S(1)}, f32[3,7,16]{1,0,2:T(4,128)S(1)}, u32[]{:S(2)}, u32[]{:S(2)}) collective-permute-start(f32[3,7,16]{1,0,2:T(4,128)S(1)} %get-tuple-element.151), channel_id=1, source_target_pairs={{0,4},{1,5},{2,6},{3,7},{4,8},{5,9},{6,10},{7,11},{8,12},{9,13},{1... | collective-permute-start | bytes 4040 | tf_op jit(solution)/shard_map/ppermute | solution.py:18
  134.5 24.6 %collective-permute-start.20 = (f32[3,7,16]{1,0,2:T(4,128)S(1)}, f32[3,7,16]{1,0,2:T(4,128)S(1)}, u32[]{:S(2)}, u32[]{:S(2)}) collective-permute-start(f32[3,7,16]{1,0,2:T(4,128)S(1)} %get-tuple-element.170), channel_id=1, source_target_pairs={{0,1},{1,2},{2,3},{3,4},{4,5},{5,6},{6,7},{7,8},{8,9},{9,10},{10,1... | collective-permute-start | bytes 4040 | tf_op jit(solution)/shard_map/ppermute | solution.py:18
  137.4 24.8 %collective-permute-start.21 = (f32[3,7,16]{1,0,2:T(4,128)S(1)}, f32[3,7,16]{1,0,2:T(4,128)S(1)}, u32[]{:S(2)}, u32[]{:S(2)}) collective-permute-start(f32[3,7,16]{1,0,2:T(4,128)S(1)} %get-tuple-element.169), channel_id=1, source_target_pairs={{0,2},{1,3},{2,4},{3,5},{4,6},{5,7},{6,8},{7,9},{8,10},{9,11},{10,... | collective-permute-start | bytes 4040 | tf_op jit(solution)/shard_map/ppermute | solution.py:18
  141.1 23.6 %collective-permute-start.22 = (f32[3,7,16]{1,0,2:T(4,128)S(1)}, f32[3,7,16]{1,0,2:T(4,128)S(1)}, u32[]{:S(2)}, u32[]{:S(2)}) collective-permute-start(f32[3,7,16]{1,0,2:T(4,128)S(1)} %get-tuple-element.168), channel_id=1, source_target_pairs={{0,3},{1,4},{2,5},{3,6},{4,7},{5,8},{6,9},{7,10},{8,11},{9,12},{10... | collective-permute-start | bytes 4040 | tf_op jit(solution)/shard_map/ppermute | solution.py:18
  146.0 21.9 %collective-permute-start.23 = (f32[3,7,16]{1,0,2:T(4,128)S(1)}, f32[3,7,16]{1,0,2:T(4,128)S(1)}, u32[]{:S(2)}, u32[]{:S(2)}) collective-permute-start(f32[3,7,16]{1,0,2:T(4,128)S(1)} %get-tuple-element.167), channel_id=1, source_target_pairs={{0,4},{1,5},{2,6},{3,7},{4,8},{5,9},{6,10},{7,11},{8,12},{9,13},{1... | collective-permute-start | bytes 4040 | tf_op jit(solution)/shard_map/ppermute | solution.py:18
  212.2 20.7 %collective-permute-start.8 = (f32[3,7,16]{1,0,2:T(4,128)S(1)}, f32[3,7,16]{1,0,2:T(4,128)}, u32[]{:S(2)}, u32[]{:S(2)}) collective-permute-start(f32[3,7,16]{1,0,2:T(4,128)S(1)} %get-tuple-element.182), channel_id=1, source_target_pairs={{1,0},{2,1},{3,2},{4,3},{5,4},{6,5},{7,6},{8,7},{9,8},{10,9},{11,1... | collective-permute-start | bytes 4040 | tf_op jit(solution)/shard_map/ppermute | solution.py:18
  220.5 22.5 %collective-permute-start.10 = (f32[3,7,16]{1,0,2:T(4,128)S(1)}, f32[3,7,16]{1,0,2:T(4,128)S(1)}, u32[]{:S(2)}, u32[]{:S(2)}) collective-permute-start(f32[3,7,16]{1,0,2:T(4,128)S(1)} %get-tuple-element.180), channel_id=1, source_target_pairs={{3,0},{4,1},{5,2},{6,3},{7,4},{8,5},{9,6},{10,7},{11,8},{12,9},{13... | collective-permute-start | bytes 4040 | tf_op jit(solution)/shard_map/ppermute | solution.py:18
  222.4 25.8 %collective-permute-start.11 = (f32[3,7,16]{1,0,2:T(4,128)S(1)}, f32[3,7,16]{1,0,2:T(4,128)S(1)}, u32[]{:S(2)}, u32[]{:S(2)}) collective-permute-start(f32[3,7,16]{1,0,2:T(4,128)S(1)} %get-tuple-element.179), channel_id=1, source_target_pairs={{4,0},{5,1},{6,2},{7,3},{8,4},{9,5},{10,6},{11,7},{12,8},{13,9},{1... | collective-permute-start | bytes 4040 | tf_op jit(solution)/shard_map/ppermute | solution.py:18
  225.0 23.9 %collective-permute-start.12 = (f32[3,7,16]{1,0,2:T(4,128)S(1)}, f32[3,7,16]{1,0,2:T(4,128)S(1)}, u32[]{:S(2)}, u32[]{:S(2)}) collective-permute-start(f32[3,7,16]{1,0,2:T(4,128)S(1)} %get-tuple-element.178), channel_id=1, source_target_pairs={{0,1},{1,2},{2,3},{3,4},{4,5},{5,6},{6,7},{7,8},{8,9},{9,10},{10,1... | collective-permute-start | bytes 4040 | tf_op jit(solution)/shard_map/ppermute | solution.py:18
  271.1 20.6 %collective-permute-start.26 = (f32[3,7,16]{1,0,2:T(4,128)S(1)}, f32[3,7,16]{1,0,2:T(4,128)S(1)}, u32[]{:S(2)}, u32[]{:S(2)}) collective-permute-start(f32[3,7,16]{1,0,2:T(4,128)S(1)} %get-tuple-element.164), channel_id=1, source_target_pairs={{3,0},{4,1},{5,2},{6,3},{7,4},{8,5},{9,6},{10,7},{11,8},{12,9},{13... | collective-permute-start | bytes 4040 | tf_op jit(solution)/shard_map/ppermute | solution.py:18
  315.7 20.9 %collective-permute-start.42 = (f32[3,7,16]{1,0,2:T(4,128)S(1)}, f32[3,7,16]{1,0,2:T(4,128)S(1)}, u32[]{:S(2)}, u32[]{:S(2)}) collective-permute-start(f32[3,7,16]{1,0,2:T(4,128)S(1)} %get-tuple-element.148), channel_id=1, source_target_pairs={{3,0},{4,1},{5,2},{6,3},{7,4},{8,5},{9,6},{10,7},{11,8},{12,9},{13... | collective-permute-start | bytes 4040 | tf_op jit(solution)/shard_map/ppermute | solution.py:18
  359.2 117.5 %collective-permute-start.56 = (f32[3,7,16]{1,0,2:T(4,128)S(1)}, f32[3,7,16]{1,0,2:T(4,128)S(1)}, u32[]{:S(2)}, u32[]{:S(2)}) collective-permute-start(f32[3,7,16]{1,0,2:T(4,128)S(1)} %get-tuple-element.134), channel_id=1, source_target_pairs={{1,0},{2,1},{3,2},{4,3},{5,4},{6,5},{7,6},{8,7},{9,8},{10,9},{11,1... | collective-permute-start | bytes 4040 | tf_op jit(solution)/shard_map/ppermute | solution.py:18
  (181 other events, 1021.7 us)
where the time goes:
time: 503 us; the launch traced here: 498 us
  starting transfers between devices  223 us (44%)
  local copies, waits for them, and re-layouts  104 us (21%)
  blocking collectives  96.3 us (19%)
  other arithmetic  30.3 us (6%)
  waiting for transfers between devices  23 us (5%)
  matrix products  12.8 us (3%)
  between operations  9.32 us (2%)
    ppermute x64, starting transfers between devices, passed_along(): return lax.ppermute(x, axis, pairs)  223 us
    psum x1, blocking collectives, drag_part(): return lax.psum(drag_term, 'dom')  96.3 us
    unnamed x354, local copies, waits for them, and re-layouts  47.9 us
    ppermute x64, waiting for transfers between devices, passed_along(): return lax.ppermute(x, axis, pairs)  23 us
    gather x4, local copies, waits for them, and re-layouts, one_section(): outer = jnp.take(jnp.concatenate([own, received], axis=-1), links, axis=-1)  12.5 us
  transfers between devices with their start and end apart: 64, of which 9 were waited for; matrix products, arithmetic and copies ran while one was open for 14% of the time, Pallas kernels for 0%

commit v1 on v0

v1 whole, which is shorter than its diff:
```python
import math

import jax
import jax.numpy as jnp
import ml_dtypes
import numpy as np
from jax import lax
from jax.experimental import pallas as pl
from jax.experimental.pallas import tpu as pltpu
from jax.sharding import PartitionSpec as P

GRAVITY = 1.0
PENALTY = 3.0
WIND_COEF = 5.0
TIME_STEP = 0.01
HALF = 0.5 * TIME_STEP
SIXTH = TIME_STEP / 6.0

GROUP = 32
ROW = 16
REACH = 4
DIRS = 8
SLOTS = 16
E = 128
F32 = jnp.float32
BF16 = jnp.bfloat16


def solve_dense(matrix, right):
    system = np.array(matrix) + 0.0
    result = np.array(right) + 0.0
    extent = system.shape[0]
    for column in range(extent):
        pivot_index = column + int(np.argmax(np.abs(system[column:, column])))
        system[[column, pivot_index]] = system[[pivot_index, column]]
        result[[column, pivot_index]] = result[[pivot_index, column]]
        for target in range(column + 1, extent):
            factor = system[target, column] / system[column, column]
            system[target] = system[target] - factor * system[column]
            result[target] = result[target] - factor * result[column]
    solution = np.zeros(result.shape)
    for column in range(extent - 1, -1, -1):
        solution[column] = (
            result[column] - system[column, column + 1 :] @ solution[column + 1 :]
        ) / system[column, column]
    return solution


def element_tables():
    degree = 6
    nodes = [
        (column, row_index)
        for row_index in range(degree + 1)
        for column in range(degree + 1 - row_index)
    ]
    node_total = len(nodes)
    coord_x = np.array([node[0] / degree for node in nodes])
    coord_y = np.array([node[1] / degree for node in nodes])
    vander = np.zeros((node_total, node_total))
    vander_r = np.zeros((node_total, node_total))
    vander_s = np.zeros((node_total, node_total))
    grams = np.zeros((node_total, node_total))
    for column_index, power in enumerate(nodes):
        first, second = power
        vander[:, column_index] = coord_x**first * coord_y**second
        if first > 0:
            vander_r[:, column_index] = 0.5 * first * coord_x ** (first - 1) * coord_y**second
        if second > 0:
            vander_s[:, column_index] = 0.5 * second * coord_x**first * coord_y ** (second - 1)
        for other_index, other_power in enumerate(nodes):
            sum_x = first + other_power[0]
            sum_y = second + other_power[1]
            grams[column_index, other_index] = (
                4.0
                * math.factorial(sum_x)
                * math.factorial(sum_y)
                / math.factorial(sum_x + sum_y + 2)
            )
    deriv_r = solve_dense(vander.T, vander_r.T).T
    deriv_s = solve_dense(vander.T, vander_s.T).T
    mass_inverse = vander @ solve_dense(grams, vander.T)
    points = np.arange(degree + 1) / degree
    line_vander = np.stack([points**power for power in range(degree + 1)], axis=1)
    line_grams = np.array(
        [
            [2.0 / (first + second + 1) for second in range(degree + 1)]
            for first in range(degree + 1)
        ]
    )
    line_inverse = solve_dense(line_vander, np.eye(degree + 1))
    line_mass = line_inverse.T @ line_grams @ line_inverse
    lookup = {node: number for number, node in enumerate(nodes)}
    face_nodes = [
        [lookup[step, 0] for step in range(degree + 1)],
        [lookup[degree - step, step] for step in range(degree + 1)],
        [lookup[0, degree - step] for step in range(degree + 1)],
    ]
    embed = np.zeros((node_total, 3 * (degree + 1)))
    extract = np.zeros((3 * (degree + 1), node_total))
    for face_index in range(3):
        for step in range(degree + 1):
            extract[face_index * (degree + 1) + step, face_nodes[face_index][step]] = 1.0
            for other_step in range(degree + 1):
                embed[
                    face_nodes[face_index][other_step], face_index * (degree + 1) + step
                ] += line_mass[other_step, step]
    lifting = mass_inverse @ embed
    return deriv_r, deriv_s, lifting, extract


def offset_of(direction):
    return direction + 1 if direction < REACH else REACH - direction - 1


def direction_of(offset):
    if 1 <= offset <= REACH:
        return offset - 1
    if -REACH <= offset <= -1:
        return REACH - 1 - offset
    return None


def place_a(d):
    return ROW + d


def place_b(d):
    return d if d < ROW else d + ROW * 2


def holder(place):
    if place < ROW:
        return place, 1
    if place < ROW + GROUP:
        return place - ROW, 0
    return place - 2 * ROW, 1


def routes():
    table = np.zeros((GROUP, 128), np.int32)
    for d in range(GROUP):
        for which, place in ((0, place_a(d)), (1, place_b(d))):
            for e in range(GROUP):
                found = direction_of(place_a(e) - place)
                if found is None:
                    found = direction_of(place_b(e) - place)
                table[d, 32 * which + e] = DIRS if found is None else found
            for j in range(DIRS):
                source = place + offset_of(j)
                if 0 <= source < 4 * ROW:
                    e, kind = holder(source)
                else:
                    e, kind = 0, 2
                table[d, 64 + 16 * which + j] = e
                table[d, 72 + 16 * which + j] = kind
    return table


def parts3(matrix, width):
    padded = np.zeros((matrix.shape[0], width))
    padded[:, : matrix.shape[1]] = matrix
    hi = padded.astype(np.float32).astype(ml_dtypes.bfloat16)
    lo = (padded - hi.astype(np.float64)).astype(ml_dtypes.bfloat16)
    return np.concatenate([hi, lo, hi], axis=1)


def constants():
    deriv_r, deriv_s, lifting, extract = element_tables()

    def pad_rows(matrix):
        return np.concatenate([matrix, np.zeros((4, matrix.shape[1]))])

    lift = np.zeros((24, 28))
    flip = np.zeros((24, 28))
    take = np.zeros((24, 28))
    give = np.zeros((24, 28))
    for face in range(3):
        for k in range(7):
            lift[8 * face + k] = lifting[:, 7 * face + k]
            flip[8 * face + k] = lifting[:, 7 * face + 6 - k]
            take[8 * face + k] = extract[7 * face + k]
            give[8 * face + k] = extract[7 * face + k]
        take[8 * face + 7] = extract[7 * face + 6]
    back = np.concatenate([pad_rows(deriv_r.T), pad_rows(deriv_s.T), lift, flip])
    back3 = parts3(back, 32)
    flip3 = parts3(flip, 32)
    grad3 = parts3(np.concatenate([pad_rows(deriv_r), pad_rows(deriv_s)]), 32)
    take2 = np.zeros((24, 64))
    take2[:, 0:28] = take
    take2[:, 32:60] = take
    spread = np.concatenate([pad_rows(give.T), flip @ give.T])
    spread3 = parts3(spread, 24)
    spread3 = np.concatenate([spread3, np.zeros((56, 8), ml_dtypes.bfloat16)], axis=1)
    as_bf16 = lambda m: jnp.asarray(np.asarray(m).astype(ml_dtypes.bfloat16))
    return as_bf16(back3), as_bf16(flip3), as_bf16(grad3), as_bf16(take2), as_bf16(spread3)


def dot(a, b):
    return jnp.dot(a, b, preferred_element_type=F32)


def dot_nt(a, b):
    return lax.dot_general(a, b, (((1,), (1,)), ((), ())), preferred_element_type=F32)


def halves(x):
    hi = x.astype(BF16).astype(F32)
    return hi, x - hi


def times3(matrix3, x):
    hi = x.astype(BF16)
    lo = (x - hi.astype(F32)).astype(BF16)
    return dot(matrix3, jnp.concatenate([hi, hi, lo], axis=0))


def spread_faces(spread3, faces):
    hi, lo = halves(faces)
    stack = jnp.concatenate([hi, hi, lo, jnp.zeros((8, faces.shape[1]), F32)], axis=0)
    return dot(spread3, stack.astype(BF16))


def geometry(misc):
    rx, ry, sx, sy = misc[0:1], misc[1:2], misc[2:3], misc[3:4]
    normals = []
    for nx, ny in ((-sx, -sy), (rx + sx, ry + sy), (-rx, -ry)):
        normals.append((nx, ny, jnp.sqrt(nx * nx + ny * ny)))
    return (rx, ry, sx, sy), normals


def jump_back(n, t, u, v, gh):
    nx, ny, size = n
    un = nx * u + ny * v
    mixed = u * t[1] + v * t[2]
    pull = 0.5 * PENALTY * size
    return (
        0.5 * (gh * (nx * t[1] + ny * t[2]) - un * mixed) - pull * t[0],
        0.5 * (nx * (t[0] + mixed) + un * t[1]) - pull * t[1],
        0.5 * (ny * (t[0] + mixed) + un * t[2]) - pull * t[2],
    )


def traces(flipped, normals):
    last = lax.broadcasted_iota(jnp.int32, (8, E), 0) == 7
    rows = []
    for c in range(3):
        rows.append(
            jnp.concatenate(
                [jnp.where(last, normals[f][c], flipped[c][f]) for f in range(3)], axis=1
            )
        )
    return jnp.concatenate(rows, axis=0)


def far_index(link, block):
    v = link - 3 * E
    j = lax.shift_right_arithmetic(v, 4)
    c = jnp.bitwise_and(v, 15)
    row = lax.shift_right_arithmetic(c, 3) * 128 + j * 8 + jnp.bitwise_and(c, 7) + 64 * block
    return jnp.where(v >= 0, row, -1)


def send(x_ref, scratch, route, sends, trace_list):
    zero = lambda r, n: jnp.zeros((r, n), F32)
    for b in range(2):
        v = trace_list[b]
        n = 3 * E
        rows = []
        if b:
            rows.append(zero(64, 2 * n))
        rows += [
            jnp.concatenate([v, zero(24, n)], axis=1),
            zero(8, 2 * n),
            jnp.concatenate([zero(24, n), v], axis=1),
            zero(8 if b else 72, 2 * n),
        ]
        hi, lo = halves(jnp.concatenate(rows, axis=0))
        out = dot_nt(sends[b], hi.astype(BF16)) + dot_nt(sends[b], lo.astype(BF16))
        scratch[b, 0:64, :] = out
        scratch[b, 64:72, :] = zero(8, 128)
    for e in range(GROUP):
        first = pl.multiple_of(route[e] * 8, 8)
        second = pl.multiple_of(route[32 + e] * 8, 8)
        x_ref[8 * e : 8 * e + 8, :] = (
            scratch[0, pl.ds(first, 8), :] + scratch[1, pl.ds(second, 8), :]
        )


def send_matrix(misc):
    faces = misc[16:24]
    lane = lax.broadcasted_iota(jnp.int32, (8, 128), 1)
    low = jnp.where(lane < 8, faces, 0.0)
    high = jnp.where((lane >= 8) & (lane < 16), faces, 0.0)
    both = low + pltpu.roll(high, 56, 1)
    row = lax.broadcasted_iota(jnp.int32, (8, 128), 0)
    lined = jnp.zeros((8, 128), F32)
    for j in range(DIRS):
        moved = both if j == 0 else pltpu.roll(both, 8 * j, 1)
        lined = lined + jnp.where(row == j, moved, 0.0)
    line = jnp.sum(lined, axis=0, keepdims=True)
    column = jnp.transpose(jnp.broadcast_to(line, (128, 128)))
    face = lax.broadcasted_iota(jnp.int32, (64, 128), 1).astype(F32)
    pieces = []
    for half in range(2):
        part = column[64 * half : 64 * half + 64]
        for f in range(3):
            pieces.append(jnp.where(part == face + float(128 * f), 1.0, 0.0))
    return jnp.concatenate(pieces, axis=1).astype(BF16)


def pack_kernel(q_ref, lam_ref, depth_ref, metric_ref, tag_ref, link_ref, face_ref, out_ref):
    ones, zeros = jnp.ones((4, E), F32), jnp.zeros((4, E), F32)
    for s in range(3):
        for c in range(3):
            out_ref[3 * s + c, 0:28, :] = q_ref[s + 1, c]
            out_ref[3 * s + c, 28:32, :] = ones
    for c in range(3):
        out_ref[9 + c, 0:28, :] = lam_ref[c]
        out_ref[9 + c, 28:32, :] = zeros
    out_ref[12, 0:28, :] = depth_ref[...]
    out_ref[12, 28:32, :] = ones
    out_ref[13] = jnp.zeros((32, E), F32)
    out_ref[13, 0:4, :] = metric_ref[...]
    out_ref[13, 4:7, :] = tag_ref[...].astype(F32)
    out_ref[13, 8:11, :] = link_ref[...].astype(F32)
    out_ref[13, 16:24, 0:16] = face_ref[...].astype(F32)


def first_kernel(route, lam_a, lam_b, misc_a, misc_b, flip3, x_ref, sends_ref, scratch):
    weights = jnp.concatenate(
        [HALF * ref[c] for ref in (lam_a, lam_b) for c in range(3)], axis=1
    )
    flipped = times3(flip3[...], weights)
    trace_list, sends = [], []
    for b, misc_ref in enumerate((misc_a, misc_b)):
        misc = misc_ref[0]
        normals = geometry(misc)[1]
        pick = lambda c, f: flipped[8 * f : 8 * f + 8, 384 * b + 128 * c : 384 * b + 128 * c + 128]
        trace_list.append(traces([[pick(c, f) for f in range(3)] for c in range(3)], normals))
        sends.append(send_matrix(misc))
        sends_ref[b] = sends[b]
    send(x_ref, scratch, route, sends, trace_list)


def near_kernel(section, blocks, *refs):
    refs = list(refs)
    drag = refs.pop(0)
    back3, flip3, grad3, take2, spread3 = [refs.pop(0)[...] for _ in range(5)]
    lams = [refs.pop(0) for _ in range(blocks)]
    states = [refs.pop(0) for _ in range(blocks)]
    depths = [refs.pop(0) for _ in range(blocks)]
    miscs = [refs.pop(0) for _ in range(blocks)]
    old_ref = refs.pop(0) if section < 3 else None
    if section == 0:
        lam3_ref, speed_ref, angle_ref = refs.pop(0), refs.pop(0), refs.pop(0)
    base_ref = refs.pop(0)
    if section > 0:
        ahead_ref = refs.pop(0)
    motion_ref = refs.pop(0)
    if section > 0:
        sum_ref = refs.pop(0)
    else:
        depth_out, speed_out, angle_out = refs.pop(0), refs.pop(0), refs.pop(0)
    scale = SIXTH if section == 2 else HALF
    later = SIXTH if section == 3 else HALF
    drag_rate = drag[0]
    pad = jnp.ones((4, E), F32)

    lam = [[lams[b][c] for c in range(3)] for b in range(blocks)]
    w = [[scale * x for x in lam[b]] for b in range(blocks)]
    if section == 0:
        q = [[jnp.concatenate([states[0][0, c], pad], axis=0) for c in range(3)]]
    else:
        q = [[states[b][c] for c in range(3)] for b in range(blocks)]
    z = [depths[b][0] for b in range(blocks)]
    pulled = times3(back3, jnp.concatenate([x for b in range(blocks) for x in w[b]], axis=1))
    slopes = times3(grad3, jnp.concatenate(z, axis=1))
    fields = jnp.concatenate([x for b in range(blocks) for x in q[b] + [z[b]]], axis=1)
    hi, lo = halves(fields)
    at_faces = dot(take2, jnp.concatenate([hi, lo], axis=0).astype(BF16))

    face_sums, volumes, opens = [], [], []
    for b in range(blocks):
        misc = miscs[b][0]
        (rx, ry, sx, sy), normals = geometry(misc)
        part = lambda r0, r1, c: pulled[r0:r1, 384 * b + 128 * c : 384 * b + 128 * c + 128]
        h = q[b][0]
        inv = 1.0 / h
        u, v = q[b][1] * inv, q[b][2] * inv
        gh = GRAVITY * h
        along = [part(0, 32, c) for c in range(3)]
        across = [part(32, 64, c) for c in range(3)]
        fx = [-(rx * along[c] + sx * across[c]) for c in range(3)]
        fy = [-(ry * along[c] + sy * across[c]) for c in range(3)]
        cross = fx[2] + fy[1]
        slope_r = slopes[0:32, 128 * b : 128 * b + 128]
        slope_s = slopes[32:64, 128 * b : 128 * b + 128]
        slope_x = rx * slope_r + sx * slope_s
        slope_y = ry * slope_r + sy * slope_s
        flow = u * w[b][1] + v * w[b][2]
        drag_inv = drag_rate * inv
        volumes.append(
            (
                gh * (fx[1] + fy[2])
                - u * (u * fx[1] + v * cross)
                - v * v * fy[2]
                + GRAVITY * (slope_x * w[b][1] + slope_y * w[b][2])
                + drag_inv * flow,
                fx[0] + 2.0 * u * fx[1] + v * cross - drag_inv * w[b][1],
                fy[0] + u * cross + 2.0 * v * fy[2] - drag_inv * w[b][2],
            )
        )
        own = [[part(64 + 8 * f, 72 + 8 * f, c) for f in range(3)] for c in range(3)]
        flipped = [[part(88 + 8 * f, 96 + 8 * f, c) for f in range(3)] for c in range(3)]
        hi, lo = halves(traces(flipped, normals))
        pool = jnp.concatenate([hi, lo], axis=0).astype(BF16)
        links = misc[8:11].astype(jnp.int32)
        rows = lax.broadcasted_iota(jnp.int32, (3 * E, E), 0)
        opened = []
        sums = [[], [], []]
        for f in range(3):
            match = jnp.where(rows == links[f : f + 1], 1.0, 0.0).astype(BF16)
            got = dot(pool, match)
            got = got[0:24] + got[24:48]
            value = lambda i: at_faces[
                8 * f : 8 * f + 8, 512 * b + 128 * i : 512 * b + 128 * i + 128
            ]
            fh, fm, fn, fz = value(0), value(1), value(2), value(3)
            finv = 1.0 / fh
            fu, fv, fgh = fm * finv, fn * finv, GRAVITY * fh
            motion_ref[b, 0, 8 * f : 8 * f + 8, :] = fu
            motion_ref[b, 1, 8 * f : 8 * f + 8, :] = fv
            motion_ref[b, 2, 8 * f : 8 * f + 8, :] = fgh
            tag = misc[4 + f : 5 + f]
            linked, wall, free = tag == 0.0, tag == 1.0, tag == 2.0
            nx, ny, size = normals[f]
            t = [own[c][f] for c in range(3)]
            mine = jump_back(normals[f], t, fu, fv, fgh)
            inv_size = 1.0 / size
            ux, uy = nx * inv_size, ny * inv_size
            twice = 2.0 * (ux * t[1] + uy * t[2])
            mirrored = (t[0], t[1] - twice * ux, t[2] - twice * uy)
            near = (got[0:8], got[8:16], got[16:24])
            other_n = tuple(
                jnp.where(linked, near[c][7:8], jnp.where(wall, m, 0.0))
                for c, m in enumerate((-nx, -ny, size))
            )
            other_t = [
                jnp.where(linked, near[c], jnp.where(wall, mirrored[c], 0.0)) for c in range(3)
            ]
            theirs = jump_back(other_n, other_t, fu, fv, fgh)
            zinv = 1.0 / fz
            out = jump_back(normals[f], t, fm * zinv, fn * zinv, GRAVITY * fz)
            opened.append(jnp.where(free, -out[0], 0.0))
            sums[0].append(mine[0] - theirs[0])
            sums[1].append(mine[1] - theirs[1] - jnp.where(free, out[1], 0.0))
            sums[2].append(mine[2] - theirs[2] - jnp.where(free, out[2], 0.0))
        face_sums.append([jnp.concatenate(sums[c], axis=0) for c in range(3)])
        if b == 0:
            opens = jnp.concatenate(opened, axis=0)
            height, moved = h, flow
    to_nodes = [x for b in range(blocks) for x in face_sums[b]]
    if section == 0:
        old = [old_ref[i] for i in range(5)]
        opens = opens + old[4][0:24]
        to_nodes.append(opens)
    nodes = spread_faces(spread3, jnp.concatenate(to_nodes, axis=1))
    for b in range(blocks):
        bases = []
        for c in range(3):
            first = lam[b][c]
            if section == 2:
                first = first * (1.0 / 3.0)
            if section == 0:
                first = first + (2.0 / 3.0) * lam3_ref[c]
            where = 384 * b + 128 * c
            bases.append(first + volumes[b][c] + nodes[0:32, where : where + 128])
            base_ref[b, c] = bases[c]
        if section > 0:
            ahead = times3(flip3, later * jnp.concatenate(bases, axis=1))
            for c in range(3):
                ahead_ref[b, c] = ahead[:, 128 * c : 128 * c + 128]
    w1, w2 = w[0][1], w[0][2]
    g1, g2 = height * w1, height * w2
    if section == 3:
        fold = moved[0:8] + moved[8:16] + moved[16:24] + moved[24:32]
        news = [w1, w2, g1, g2]
    else:
        if section > 0:
            old = [old_ref[i] for i in range(5)]
            opens = opens + old[4][0:24]
            fold = old[4][24:32] + (moved[0:8] + moved[8:16] + moved[16:24] + moved[24:32])
        news = [x + y for x, y in zip(old[0:4], (w1, w2, g1, g2))]
    if section > 0:
        for i in range(4):
            sum_ref[i] = news[i]
        sum_ref[4, 0:24, :] = opens
        sum_ref[4, 24:32, :] = fold
    else:
        rx, ry, sx, sy = geometry(miscs[0][0])[0]
        w1, w2, g1, g2 = news
        pair = GRAVITY * jnp.concatenate([rx * g1 + ry * g2, sx * g1 + sy * g2], axis=1)
        pulled = times3(back3, pair)
        depth = pulled[0:32, 0:128] + pulled[32:64, 128:256] + nodes[0:32, 384:512]
        depth_out[...] = depth[0:28]
        speed, angle = speed_ref[...], angle_ref[...]
        cosine, sine = jnp.cos(angle), jnp.sin(angle)
        w1, w2 = w1[0:28], w2[0:28]
        speed_out[...] = (2.0 * WIND_COEF) * speed * (cosine * w1 + sine * w2)
        angle_out[...] = WIND_COEF * speed * speed * (cosine * w2 - sine * w1)


def far_kernel(section, blocks, *refs):
    refs = list(refs)
    route, y_ref, spread3_ref, base_ref, motion_ref = [refs.pop(0) for _ in range(5)]
    miscs = [refs.pop(0) for _ in range(blocks)]
    if section > 0:
        ahead_ref, sends_ref = refs.pop(0), refs.pop(0)
    if section == 1:
        q0_ref, sum_ref = refs.pop(0), refs.pop(0)
    lam_refs = [refs.pop(0) for _ in range(blocks)]
    if section > 0:
        x_ref, scratch = refs.pop(0), refs.pop(0)
    later = SIXTH if section == 3 else HALF

    boxes = []
    for b in range(2):
        for j in range(DIRS):
            if b < blocks:
                place = pl.multiple_of(route[64 + 16 * b + j] * 8, 8)
                kind = route[72 + 16 * b + j]
                box = y_ref[pl.ds(place, 8), :]
                box = jnp.where(kind == 1, pltpu.roll(box, 64, 1), box)
                boxes.append(jnp.where(kind == 2, 0.0, box))
            else:
                boxes.append(jnp.zeros((8, 128), F32))
    turned = jnp.transpose(jnp.concatenate(boxes, axis=0))
    hi, lo = halves(jnp.concatenate([turned[0:24], turned[32:56]], axis=1))
    pool = jnp.concatenate([hi, lo], axis=0).astype(BF16)
    rows = lax.broadcasted_iota(jnp.int32, (256, E), 0)
    face_sums = []
    for b in range(blocks):
        links = miscs[b][0][8:11].astype(jnp.int32)
        sums = [[], [], []]
        for f in range(3):
            match = jnp.where(rows == far_index(links[f : f + 1], b), 1.0, 0.0).astype(BF16)
            got = dot(pool, match)
            got = got[0:24] + got[24:48]
            far = (got[0:8], got[8:16], got[16:24])
            motion = [motion_ref[b, i, 8 * f : 8 * f + 8, :] for i in range(3)]
            theirs = jump_back(tuple(x[7:8] for x in far), far, *motion)
            for c in range(3):
                sums[c].append(-theirs[c])
        face_sums += [jnp.concatenate(sums[c], axis=0) for c in range(3)]
    spread = spread_faces(spread3_ref[...], jnp.concatenate(face_sums, axis=1))
    trace_list = []
    for b in range(blocks):
        lam = []
        for c in range(3):
            where = 384 * b + 128 * c
            lam.append(base_ref[b, c] + spread[0:32, where : where + 128])
        if section > 0:
            for c in range(3):
                lam_refs[b][c] = lam[c]
            flipped = [
                ahead_ref[b, c]
                + later * spread[32:56, 384 * b + 128 * c : 384 * b + 128 * c + 128]
                for c in range(3)
            ]
            split = [[flipped[c][8 * f : 8 * f + 8] for f in range(3)] for c in range(3)]
            trace_list.append(traces(split, geometry(miscs[b][0])[1]))
        else:
            for c in range(3):
                lam_refs[b][c] = lam[c][0:28]
        if section == 1 and b == 0:
            first = lam
    if section > 0:
        send(x_ref, scratch, route, [sends_ref[0], sends_ref[1]], trace_list)
    if section == 1:
        q0 = [q0_ref[0, c] for c in range(3)]
        flow = (q0[1] * first[1][0:28] + q0[2] * first[2][0:28]) * (HALF / q0[0])
        total = jnp.sum(sum_ref[4, 24:32, :]) + jnp.sum(flow)
        lane = lax.broadcasted_iota(jnp.int32, (8, 128), 1)
        for e in range(GROUP):
            part = x_ref[8 * e : 8 * e + 8, :]
            x_ref[8 * e : 8 * e + 8, :] = jnp.where(lane == 127, -total, part)


def whole(shape):
    return pl.BlockSpec(shape, lambda i: (0,) * len(shape))


def block(shape, first):
    return pl.BlockSpec(shape, lambda i: (first,) + (0,) * (len(shape) - 1))


SCALARS = pl.BlockSpec(memory_space=pltpu.SMEM)


def call(kernel, in_specs, outs, args, scratch=()):
    return pl.pallas_call(
        kernel,
        grid=(1,),
        in_specs=in_specs,
        out_specs=[whole(shape) for shape, _ in outs],
        out_shape=[jax.ShapeDtypeStruct(shape, dtype) for shape, dtype in outs],
        scratch_shapes=list(scratch),
        compiler_params=pltpu.CompilerParams(vmem_limit_bytes=32 * 1024 * 1024),
    )(*args)


def local(
    saved_states,
    adjoint_final,
    bathymetry,
    wind_speed,
    wind_angle,
    drag_rate,
    metrics,
    face_link,
    face_tag,
    send_faces,
):
    devices = lax.axis_size("dom")
    groups = [list(range(g, g + GROUP)) for g in range(0, devices, GROUP)]
    strides = [list(range(d, devices, GROUP)) for d in range(GROUP)]
    back3, flip3, grad3, take2, spread3 = constants()
    tables = [back3, flip3, grad3, take2, spread3]
    table_specs = [whole(t.shape) for t in tables]
    me = lax.rem(lax.axis_index("dom"), GROUP)
    route = lax.dynamic_slice(jnp.asarray(routes()), (me, 0), (1, 128)).reshape(128)

    nodes, mixed = (32, E), (3, 32, E)
    mine = call(
        pack_kernel,
        [whole(x.shape) for x in (saved_states, adjoint_final, bathymetry, metrics)]
        + [whole(x.shape) for x in (face_tag, face_link, send_faces)],
        [((14, 32, E), F32)],
        (saved_states, adjoint_final, bathymetry, metrics, face_tag, face_link, send_faces),
    )[0]
    pairs = [(i, i) for i in range(ROW)] + [(i, i) for i in range(devices - ROW, devices)]
    for row in range(1, devices // ROW - 1, 2):
        for i in range(row * ROW, row * ROW + ROW):
            pairs += [(i, i + ROW), (i + ROW, i)]
    halo = lax.ppermute(mine, "dom", pairs)
    both = (mine, halo)

    scratch = [pltpu.VMEM((2, 72, 128), F32)]
    x_out = ((GROUP * 8, 128), F32)
    x, sends = call(
        first_kernel,
        [SCALARS]
        + [block((3, 32, E), 3)] * 2
        + [block((1, 32, E), 13)] * 2
        + [whole(flip3.shape)],
        [x_out, ((2, 64, 768), BF16)],
        (route, mine, halo, mine, halo, flip3),
        scratch,
    )
    lams = both
    lam3 = sums = None
    for section in (3, 2, 1, 0):
        y = lax.all_to_all(x, "dom", 0, 0, tiled=True, axis_index_groups=groups)
        blocks = 2 if section > 0 else 1
        args = [drag_rate] + tables + list(lams[:blocks])
        specs = [SCALARS] + table_specs
        specs += [block(mixed, 3)] * blocks if section == 3 else [whole(mixed)] * blocks
        if section > 0:
            args += list(both)
            specs += [block(mixed, section - 1)] * blocks
        else:
            args += [saved_states]
            specs += [pl.BlockSpec((1, 3, 28, E), lambda i: (0, 0, 0, 0))]
        args += list(both[:blocks]) * 2
        specs += [block((1, 32, E), 12)] * blocks + [block((1, 32, E), 13)] * blocks
        if section < 3:
            args.append(sums)
            specs.append(whole((5, 32, E)))
        outs = [((blocks, 3, 32, E), F32)]
        if section > 0:
            outs.append(((blocks, 3, 24, E), F32))
        outs.append(((blocks, 3, 24, E), F32))
        if section > 0:
            outs.append(((5, 32, E), F32))
        else:
            args += [lam3, wind_speed, wind_angle]
            specs += [whole(mixed), whole((28, E)), whole((28, E))]
            outs += [((28, E), F32)] * 3
        got = call(
            lambda *refs, s=section, n=blocks: near_kernel(s, n, *refs), specs, outs, args
        )
        if section > 0:
            base, ahead, motion, sums = got
        else:
            base, motion, depth_gradient, speed_gradient, angle_gradient = got

        args = [route, y, spread3, base, motion] + list(both[:blocks])
        specs = [SCALARS] + [whole(v.shape) for v in (y, spread3, base, motion)]
        specs += [block((1, 32, E), 13)] * blocks
        if section > 0:
            args += [ahead, sends]
            specs += [whole(ahead.shape), whole(sends.shape)]
        if section == 1:
            args += [saved_states, sums]
            specs += [pl.BlockSpec((1, 3, 28, E), lambda i: (0, 0, 0, 0)), whole((5, 32, E))]
        if section > 0:
            outs = [(mixed, F32)] * 2 + [x_out]
        else:
            outs = [((3, 28, E), F32)]
        got = call(
            lambda *refs, s=section, n=blocks: far_kernel(s, n, *refs),
            specs,
            outs,
            args,
            scratch if section > 0 else (),
        )
        if section > 0:
            lams, x = got[0:2], got[2]
            if section == 3:
                lam3 = lams[0]
        else:
            initial = got[0]
    within = jnp.sum(y.reshape(GROUP, 8, 128)[:, 0, 127])
    spread = lax.all_to_all(
        jnp.broadcast_to(within, (devices // GROUP, 128)),
        "dom",
        0,
        0,
        tiled=True,
        axis_index_groups=strides,
    )
    drag_gradient = jnp.sum(spread[:, 0]).reshape(1)
    return (initial, depth_gradient, speed_gradient, angle_gradient, drag_gradient)


def solution(mesh):
    return jax.shard_map(
        local,
        mesh=mesh,
        in_specs=(
            P(None, None, None, "dom"),
            P(None, None, "dom"),
            P(None, "dom"),
            P(None, "dom"),
            P(None, "dom"),
            P(),
            P(None, "dom"),
            P(None, "dom"),
            P(None, "dom"),
            P(None, "dom"),
        ),
        out_specs=(P(None, None, "dom"), P(None, "dom"), P(None, "dom"), P(None, "dom"), P()),
        check_vma=False,
    )
```

time: 503 us -> 101 us (0.20)
  the two profiles are of different devices: /device:TPU:2 before, /device:TPU:1 now
where the time goes in v1:
time: 101 us; the launch traced here: 99.8 us
  starting transfers between devices  39.9 us (40%)
  waiting for transfers between devices  28.2 us (28%)
  blocking collectives  13.2 us (13%)
  Pallas kernels  12.7 us (13%)
  local copies, waits for them, and re-layouts  2.98 us (3%)
  between operations  1.51 us (1%)
  other arithmetic  1.3 us (1%)
    all_to_all x3, starting transfers between devices, local(): y = lax.all_to_all(x, 'dom', 0, 0, tiled=True, axis_index_groups=groups)  29.7 us
    all_to_all x3, waiting for transfers between devices, local(): y = lax.all_to_all(x, 'dom', 0, 0, tiled=True, axis_index_groups=groups)  22.4 us
    all_to_all x1, blocking collectives, local(): y = lax.all_to_all(x, 'dom', 0, 0, tiled=True, axis_index_groups=groups)  13.2 us
    pallas_call x10, Pallas kernels, call(): pl.pallas_call(kernel, grid=(1,), in_specs=in_specs, out_specs=[whole(sha...  12.7 us
    all_to_all x1, starting transfers between devices, local(): lax.all_to_all(jnp.broadcast_to(within, (devices // GROUP, 128)), 'dom',...  9.59 us
    all_to_all x1, waiting for transfers between devices, local(): lax.all_to_all(jnp.broadcast_to(within, (devices // GROUP, 128)), 'dom',...  5.83 us
  transfers between devices with their start and end apart: 5, of which 4 were waited for; matrix products, arithmetic and copies ran while one was open for 1% of the time, Pallas kernels for 5%

profile of v1, /device:TPU:1, one launch (start us, length us, event | category | flops | bytes accessed | tf_op | source)
XLA Modules:
  0.0 99.8 jit_solution(12832104189091784215)
XLA Ops:
  0.7 1.0 copy.27.q_ref.refs_9_.refs_7_
  1.8 0.7 collective-permute-start
  2.5 0.7 dynamic-slice_bitcast_fusion.route.refs_0_
  3.2 1.8 %shard_map.192 = (f32[256,128]{1,0:T(8,128)}, bf16[2,64,768]{2,1,0:T(8,128)(2,1)S(1)}) custom-call(s32[128]{0:T(128)S(1)} %dynamic-slice_bitcast_fusion.route.refs_0_, f32[14,32,128]{2,1,0:T(8,128)S(1)} %shard_map.191.lam_a.misc_a.refs_6_.refs_8_.refs_10_.refs_12_.refs_5_.refs_9_, ...), custom_call_target="tpu_custom_call" | custom-call | tf_op jit(solution)/shard_map/pallas_call | solution.py:601
  5.0 21.0 %all-to-all-start = ((f32[32,8,128]{2,1,0:T(8,128)}), f32[32,8,128]{2,1,0:T(8,128)S(1)}, u32[]{:S(2)}, u32[]{:S(2)}) async-start(f32[32,8,128]{2,1,0:T(8,128)} %bitcast.1), calls=%async_computation | async-start | bytes 262144 | tf_op jit(solution)/shard_map/all_to_all | solution.py:663
  26.6 0.8 shard_map.193
  27.4 7.4 %all-to-all-done = f32[32,8,128]{2,1,0:T(8,128)S(1)} async-done(((f32[32,8,128]{2,1,0:T(8,128)}), f32[32,8,128]{2,1,0:T(8,128)S(1)}, u32[]{:S(2)}, u32[]{:S(2)}) %all-to-all-start) | async-done | bytes 131104 | tf_op jit(solution)/shard_map/all_to_all | solution.py:663
  34.8 2.0 %shard_map.194 = (f32[3,32,128]{2,1,0:T(8,128)S(1)}, f32[3,32,128]{2,1,0:T(8,128)S(1)}, f32[256,128]{1,0:T(8,128)}) custom-call(s32[128]{0:T(128)S(1)} %dynamic-slice_bitcast_fusion.route.refs_0_, f32[256,128]{1,0:T(8,128)S(1)} %bitcast.15, bf16[56,80]{1,0:T(8,128)(2,1)S(1)} %copy-done, f32[2,3,32,128]{3,2,1,0:T(8,128)S(1)} %get-tuple-element.33.refs_3_, ...), custom_call_target="tpu_custom_call" | custom-call | tf_op jit(solution)/shard_map/pallas_call | solution.py:601
  36.9 4.0 %all-to-all-start.1 = ((f32[32,8,128]{2,1,0:T(8,128)}), f32[32,8,128]{2,1,0:T(8,128)S(1)}, u32[]{:S(2)}, u32[]{:S(2)}) async-start(f32[32,8,128]{2,1,0:T(8,128)} %bitcast.3), calls=%async_computation.1 | async-start | bytes 262144 | tf_op jit(solution)/shard_map/all_to_all | solution.py:663
  40.9 0.8 shard_map.195
  41.6 7.5 %all-to-all-done.1 = f32[32,8,128]{2,1,0:T(8,128)S(1)} async-done(((f32[32,8,128]{2,1,0:T(8,128)}), f32[32,8,128]{2,1,0:T(8,128)S(1)}, u32[]{:S(2)}, u32[]{:S(2)}) %all-to-all-start.1) | async-done | bytes 131104 | tf_op jit(solution)/shard_map/all_to_all | solution.py:663
  49.1 2.0 %shard_map.196 = (f32[3,32,128]{2,1,0:T(8,128)S(1)}, f32[3,32,128]{2,1,0:T(8,128)S(1)}, f32[256,128]{1,0:T(8,128)}) custom-call(s32[128]{0:T(128)S(1)} %dynamic-slice_bitcast_fusion.route.refs_0_, f32[256,128]{1,0:T(8,128)S(1)} %bitcast.14, bf16[56,80]{1,0:T(8,128)(2,1)S(1)} %copy-done, f32[2,3,32,128]{3,2,1,0:T(8,128)S(1)} %get-tuple-element.41.refs_3_, ...), custom_call_target="tpu_custom_call" | custom-call | tf_op jit(solution)/shard_map/pallas_call | solution.py:601
  51.2 4.7 %all-to-all-start.2 = ((f32[32,8,128]{2,1,0:T(8,128)}), f32[32,8,128]{2,1,0:T(8,128)S(1)}, u32[]{:S(2)}, u32[]{:S(2)}) async-start(f32[32,8,128]{2,1,0:T(8,128)} %bitcast.5), calls=%async_computation.2 | async-start | bytes 262144 | tf_op jit(solution)/shard_map/all_to_all | solution.py:663
  55.9 0.8 shard_map.197
  56.7 7.5 %all-to-all-done.2 = f32[32,8,128]{2,1,0:T(8,128)S(1)} async-done(((f32[32,8,128]{2,1,0:T(8,128)}), f32[32,8,128]{2,1,0:T(8,128)S(1)}, u32[]{:S(2)}, u32[]{:S(2)}) %all-to-all-start.2) | async-done | bytes 131104 | tf_op jit(solution)/shard_map/all_to_all | solution.py:663
  64.2 1.6 %shard_map.198 = (f32[3,32,128]{2,1,0:T(8,128)S(1)}, f32[3,32,128]{2,1,0:T(8,128)}, f32[256,128]{1,0:T(8,128)S(1)}) custom-call(s32[128]{0:T(128)S(1)} %dynamic-slice_bitcast_fusion.route.refs_0_, f32[256,128]{1,0:T(8,128)S(1)} %bitcast.13, bf16[56,80]{1,0:T(8,128)(2,1)S(1)} %copy-done, f32[2,3,32,128]{3,2,1,0:T(8,128)S(1)} %get-tuple-element.48.refs_3_, ...), custom_call_target="tpu_custom_call" | custom-call | tf_op jit(solution)/shard_map/pallas_call | solution.py:601
  65.8 13.2 %all_to_all.53 = f32[32,8,128]{2,1,0:T(8,128)S(1)} all-to-all(f32[32,8,128]{2,1,0:T(8,128)S(1)} %bitcast.16), channel_id=1, replica_groups={{0,1,2,3,4,5,6,7,8,9,10,11,12,13,14,15,16,17,18,19,20,21,22,23,24,25,26..., dimensions={0} | all-to-all | bytes 262144 | tf_op jit(solution)/shard_map/all_to_all | solution.py:663
  79.0 0.7 slice_reduce_fusion
  79.7 1.3 %broadcast_in_dim.3 = f32[16,1,128]{2,1,0:T(1,128)} broadcast(f32[]{:T(128)} %slice_reduce_fusion), dimensions={} | broadcast | bytes 8196 | tf_op jit(solution)/shard_map/broadcast_in_dim | solution.py:725
  81.0 9.6 %all-to-all-start.4 = ((f32[16,1,128]{2,1,0:T(1,128)}), f32[16,1,128]{2,1,0:T(1,128)S(1)}, u32[]{:S(2)}, u32[]{:S(2)}) async-start(f32[16,1,128]{2,1,0:T(1,128)} %broadcast_in_dim.3), calls=%async_computation.4 | async-start | bytes 16384 | tf_op jit(solution)/shard_map/all_to_all | solution.py:724
  90.6 1.2 %shard_map.199 = (f32[1,3,32,128]{3,2,1,0:T(8,128)S(1)}, f32[1,3,24,128]{3,2,1,0:T(8,128)S(1)}, f32[28,128]{1,0:T(8,128)}, f32[28,128]{1,0:T(8,128)}, f32[28,128]{1,0:T(8,128)}) custom-call(f32[1]{0:T(128)S(6)} %copy.32.refs_0_, bf16[112,96]{1,0:T(8,128)(2,1)S(1)} %copy-done.1, bf16[24,96]{1,0:T(8,128)(2,1)S(1)} %copy-done.3, bf16[64,96]{1,0:T(8,128)(2,1)S(1)} %copy-done.2, ...), custom_call_target="tpu_custom_call" | custom-call | tf_op jit(solution)/shard_map/pallas_call | solution.py:601
  91.8 1.6 %shard_map.200 = f32[3,28,128]{2,1,0:T(8,128)} custom-call(s32[128]{0:T(128)S(1)} %dynamic-slice_bitcast_fusion.route.refs_0_, f32[256,128]{1,0:T(8,128)S(1)} %bitcast.12, bf16[56,80]{1,0:T(8,128)(2,1)S(1)} %copy-done, f32[1,3,32,128]{3,2,1,0:T(8,128)S(1)} %get-tuple-element.54.refs_3_, f32[1,3,24,128]{3,2,1,0:T(8,128)S(1)} %get-tuple-element.55.refs_4_, ...), custom_call_target="tpu_custom_call" | custom-call | tf_op jit(solution)/shard_map/pallas_call | solution.py:601
  93.4 5.8 %all-to-all-done.4 = f32[16,1,128]{2,1,0:T(1,128)S(1)} async-done(((f32[16,1,128]{2,1,0:T(1,128)}), f32[16,1,128]{2,1,0:T(1,128)S(1)}, u32[]{:S(2)}, u32[]{:S(2)}) %all-to-all-start.4) | async-done | bytes 8224 | tf_op jit(solution)/shard_map/all_to_all | solution.py:724
  99.2 0.6 slice_reduce_fusion.1
  (28 shorter events, 0.1 us)
Async XLA Ops:
  0.6 1.0 %copy-start.9 = (s32[8,16]{1,0:T(8,128)S(1)}, s32[8,16]{1,0:T(8,128)}, u32[]{:S(2)}) copy-start(s32[8,16]{1,0:T(8,128)} %face_ref.1) | copy-start | bytes 1540
  0.6 1.0 %copy-start.11 = (s32[3,128]{1,0:T(4,128)S(1)}, s32[3,128]{1,0:T(4,128)}, u32[]{:S(2)}) copy-start(s32[3,128]{1,0:T(4,128)} %tag_ref.1) | copy-start | bytes 4612
  0.7 1.0 %copy-start.12 = (s32[3,128]{1,0:T(4,128)S(1)}, s32[3,128]{1,0:T(4,128)}, u32[]{:S(2)}) copy-start(s32[3,128]{1,0:T(4,128)} %link_ref.1) | copy-start | bytes 4612
  0.7 1.0 %copy-start.10 = (f32[4,128]{1,0:T(4,128)S(1)}, f32[4,128]{1,0:T(4,128)}, u32[]{:S(2)}) copy-start(f32[4,128]{1,0:T(4,128)} %metric_ref.1) | copy-start | bytes 6148
  0.7 1.0 %copy-start.8 = (f32[28,128]{1,0:T(8,128)S(1)}, f32[28,128]{1,0:T(8,128)}, u32[]{:S(2)}) copy-start(f32[28,128]{1,0:T(8,128)} %depth_ref.1) | copy-start | bytes 43012
  0.7 1.0 %copy-start.5 = (f32[3,28,128]{2,1,0:T(8,128)S(1)}, f32[3,28,128]{2,1,0:T(8,128)}, u32[]{:S(2)}) copy-start(f32[3,28,128]{2,1,0:T(8,128)} %lam_ref.1) | copy-start | bytes 129028
  1.8 1.4 %collective-permute-start = (f32[14,32,128]{2,1,0:T(8,128)S(1)}, f32[14,32,128]{2,1,0:T(8,128)S(1)}, u32[]{:S(2)}, u32[]{:S(2)}) collective-permute-start(f32[14,32,128]{2,1,0:T(8,128)S(1)} %shard_map.191.lam_a.misc_a.refs_6_.refs_8_.refs_10_.refs_12_.refs_5_.refs_9_), channel_id=1, source_target_pairs={{0,0},{1,1},{2,2},{3,3},{4,4},{5,5},{6,6},{7,7},{8,8},{9,9},{10,10... | collective-permute-start | bytes 688136 | tf_op jit(solution)/shard_map/ppermute | solution.py:645
  2.5 0.7 copy-start.3
  5.0 21.6 %copy-start = (bf16[56,80]{1,0:T(8,128)(2,1)S(1)}, bf16[56,80]{1,0:T(8,128)(2,1)}, u32[]{:S(2)}) copy-start(bf16[56,80]{1,0:T(8,128)(2,1)} %constant.29.clone.refs_5_.refs_2_) | copy-start | bytes 26884
  5.0 21.6 %copy-start.1 = (bf16[112,96]{1,0:T(8,128)(2,1)S(1)}, bf16[112,96]{1,0:T(8,128)(2,1)}, u32[]{:S(2)}) copy-start(bf16[112,96]{1,0:T(8,128)(2,1)} %constant.25.clone.refs_1_) | copy-start | bytes 64516
  5.0 21.6 %copy-start.2 = (bf16[64,96]{1,0:T(8,128)(2,1)S(1)}, bf16[64,96]{1,0:T(8,128)(2,1)}, u32[]{:S(2)}) copy-start(bf16[64,96]{1,0:T(8,128)(2,1)} %constant.27.clone.refs_3_) | copy-start | bytes 36868
  5.0 21.6 %copy-start.4 = (bf16[24,64]{1,0:T(8,128)(2,1)S(1)}, bf16[24,64]{1,0:T(8,128)(2,1)}, u32[]{:S(2)}) copy-start(bf16[24,64]{1,0:T(8,128)(2,1)} %constant.28.clone.refs_4_) | copy-start | bytes 9220
  5.0 29.9 %all-to-all-start = ((f32[32,8,128]{2,1,0:T(8,128)}), f32[32,8,128]{2,1,0:T(8,128)S(1)}, u32[]{:S(2)}, u32[]{:S(2)}) async-start(f32[32,8,128]{2,1,0:T(8,128)} %bitcast.1), calls=%async_computation | async-start | bytes 262144 | tf_op jit(solution)/shard_map/all_to_all | solution.py:663
  36.9 12.3 %all-to-all-start.1 = ((f32[32,8,128]{2,1,0:T(8,128)}), f32[32,8,128]{2,1,0:T(8,128)S(1)}, u32[]{:S(2)}, u32[]{:S(2)}) async-start(f32[32,8,128]{2,1,0:T(8,128)} %bitcast.3), calls=%async_computation.1 | async-start | bytes 262144 | tf_op jit(solution)/shard_map/all_to_all | solution.py:663
  51.2 13.0 %all-to-all-start.2 = ((f32[32,8,128]{2,1,0:T(8,128)}), f32[32,8,128]{2,1,0:T(8,128)S(1)}, u32[]{:S(2)}, u32[]{:S(2)}) async-start(f32[32,8,128]{2,1,0:T(8,128)} %bitcast.5), calls=%async_computation.2 | async-start | bytes 262144 | tf_op jit(solution)/shard_map/all_to_all | solution.py:663
  79.0 11.6 %copy-start.7 = (f32[28,128]{1,0:T(8,128)S(1)}, f32[28,128]{1,0:T(8,128)}, u32[]{:S(2)}) copy-start(f32[28,128]{1,0:T(8,128)} %refs_13_.1) | copy-start | bytes 43012
  79.7 10.9 %copy-start.6 = (f32[28,128]{1,0:T(8,128)S(1)}, f32[28,128]{1,0:T(8,128)}, u32[]{:S(2)}) copy-start(f32[28,128]{1,0:T(8,128)} %refs_12_.1) | copy-start | bytes 43012
  81.0 18.3 %all-to-all-start.4 = ((f32[16,1,128]{2,1,0:T(1,128)}), f32[16,1,128]{2,1,0:T(1,128)S(1)}, u32[]{:S(2)}, u32[]{:S(2)}) async-start(f32[16,1,128]{2,1,0:T(1,128)} %broadcast_in_dim.3), calls=%async_computation.4 | async-start | bytes 16384 | tf_op jit(solution)/shard_map/all_to_all | solution.py:724

commit v2 on v1

--- a/solution.py
+++ b/solution.py
@@ -22,6 +22,7 @@
 DIRS = 8
 SLOTS = 16
 E = 128
+DEPTH, MISC = 12, 13
 F32 = jnp.float32
 BF16 = jnp.bfloat16
 
@@ -112,48 +113,17 @@
     return direction + 1 if direction < REACH else REACH - direction - 1
 
 
-def direction_of(offset):
-    if 1 <= offset <= REACH:
-        return offset - 1
-    if -REACH <= offset <= -1:
-        return REACH - 1 - offset
-    return None
-
-
-def place_a(d):
-    return ROW + d
-
-
-def place_b(d):
-    return d if d < ROW else d + ROW * 2
-
-
-def holder(place):
-    if place < ROW:
-        return place, 1
-    if place < ROW + GROUP:
-        return place - ROW, 0
-    return place - 2 * ROW, 1
-
-
-def routes():
-    table = np.zeros((GROUP, 128), np.int32)
-    for d in range(GROUP):
-        for which, place in ((0, place_a(d)), (1, place_b(d))):
-            for e in range(GROUP):
-                found = direction_of(place_a(e) - place)
-                if found is None:
-                    found = direction_of(place_b(e) - place)
-                table[d, 32 * which + e] = DIRS if found is None else found
-            for j in range(DIRS):
-                source = place + offset_of(j)
-                if 0 <= source < 4 * ROW:
-                    e, kind = holder(source)
-                else:
-                    e, kind = 0, 2
-                table[d, 64 + 16 * which + j] = e
-                table[d, 72 + 16 * which + j] = kind
-    return table
+def neighbours():
+    me = jnp.bitwise_and(lax.axis_index("dom"), GROUP - 1)
+    found = []
+    for own in (me + ROW, jnp.where(me < ROW, me, me + 2 * ROW)):
+        for j in range(DIRS):
+            place = own + offset_of(j)
+            inner = (place >= ROW) & (place < ROW + GROUP)
+            exists = (place >= 0) & (place < 4 * ROW)
+            device = jnp.where(inner, place - ROW, jnp.where(place < ROW, place, place - 2 * ROW))
+            found.append((jnp.where(exists, device, 0), jnp.where(inner, 0, 1), exists))
+    return found
 
 
 def parts3(matrix, width):
@@ -252,38 +222,35 @@
     return jnp.concatenate(rows, axis=0)
 
 
-def far_index(link, block):
+def far_index(link):
     v = link - 3 * E
     j = lax.shift_right_arithmetic(v, 4)
     c = jnp.bitwise_and(v, 15)
-    row = lax.shift_right_arithmetic(c, 3) * 128 + j * 8 + jnp.bitwise_and(c, 7) + 64 * block
+    row = lax.shift_right_arithmetic(c, 3) * 64 + j * 8 + jnp.bitwise_and(c, 7)
     return jnp.where(v >= 0, row, -1)
 
 
-def send(x_ref, scratch, route, sends, trace_list):
-    zero = lambda r, n: jnp.zeros((r, n), F32)
+def slot_rows(sends, v, block):
+    first = 64 * block
+    n = v.shape[1]
+    hi, lo = halves(v)
+    rows = [jnp.zeros((first, n), F32)] if block else []
+    rest = [jnp.zeros((32 - v.shape[0], n), F32)] if v.shape[0] < 32 else []
+    rows += [hi] + rest + [lo] + rest + [jnp.zeros((64 - first, n), F32)] * (1 - block)
+    out = dot_nt(sends, jnp.concatenate(rows, axis=0).astype(BF16))
+    lane = lax.broadcasted_iota(jnp.int32, (128, 128), 1)
+    out = jnp.where((lane >= first) & (lane < first + 32), out + pltpu.roll(out, 96, 1), 0.0)
+    return out[0:64] + pltpu.roll(out[64:128], 32, 1)
+
+
+def send(x_ref, near_by, boxes):
+    x_ref[...] = jnp.zeros(x_ref.shape, F32)
     for b in range(2):
-        v = trace_list[b]
-        n = 3 * E
-        rows = []
-        if b:
-            rows.append(zero(64, 2 * n))
-        rows += [
-            jnp.concatenate([v, zero(24, n)], axis=1),
-            zero(8, 2 * n),
-            jnp.concatenate([zero(24, n), v], axis=1),
-            zero(8 if b else 72, 2 * n),
-        ]
-        hi, lo = halves(jnp.concatenate(rows, axis=0))
-        out = dot_nt(sends[b], hi.astype(BF16)) + dot_nt(sends[b], lo.astype(BF16))
-        scratch[b, 0:64, :] = out
-        scratch[b, 64:72, :] = zero(8, 128)
-    for e in range(GROUP):
-        first = pl.multiple_of(route[e] * 8, 8)
-        second = pl.multiple_of(route[32 + e] * 8, 8)
-        x_ref[8 * e : 8 * e + 8, :] = (
-            scratch[0, pl.ds(first, 8), :] + scratch[1, pl.ds(second, 8), :]
-        )
+        for j in range(DIRS):
+            device, _, exists = near_by[DIRS * b + j]
+            rows = pl.ds(pl.multiple_of(device * 8, 8), 8)
+            box = jnp.where(exists, boxes[b][8 * j : 8 * j + 8], 0.0)
+            x_ref[rows, :] = x_ref[rows, :] + box
 
 
 def send_matrix(misc):
@@ -299,47 +266,54 @@
         lined = lined + jnp.where(row == j, moved, 0.0)
     line = jnp.sum(lined, axis=0, keepdims=True)
     column = jnp.transpose(jnp.broadcast_to(line, (128, 128)))
-    face = lax.broadcasted_iota(jnp.int32, (64, 128), 1).astype(F32)
-    pieces = []
-    for half in range(2):
-        part = column[64 * half : 64 * half + 64]
-        for f in range(3):
-            pieces.append(jnp.where(part == face + float(128 * f), 1.0, 0.0))
+    face = lax.broadcasted_iota(jnp.int32, (128, 128), 1).astype(F32)
+    pieces = [jnp.where(column == face + float(128 * f), 1.0, 0.0) for f in range(3)]
     return jnp.concatenate(pieces, axis=1).astype(BF16)
 
 
 def pack_kernel(q_ref, lam_ref, depth_ref, metric_ref, tag_ref, link_ref, face_ref, out_ref):
-    ones, zeros = jnp.ones((4, E), F32), jnp.zeros((4, E), F32)
+    ones = jnp.ones((4, E), F32)
+    for c in range(3):
+        out_ref[c, 0:28, :] = lam_ref[c]
+        out_ref[c, 28:32, :] = jnp.zeros((4, E), F32)
     for s in range(3):
         for c in range(3):
-            out_ref[3 * s + c, 0:28, :] = q_ref[s + 1, c]
-            out_ref[3 * s + c, 28:32, :] = ones
-    for c in range(3):
-        out_ref[9 + c, 0:28, :] = lam_ref[c]
-        out_ref[9 + c, 28:32, :] = zeros
-    out_ref[12, 0:28, :] = depth_ref[...]
-    out_ref[12, 28:32, :] = ones
-    out_ref[13] = jnp.zeros((32, E), F32)
-    out_ref[13, 0:4, :] = metric_ref[...]
-    out_ref[13, 4:7, :] = tag_ref[...].astype(F32)
-    out_ref[13, 8:11, :] = link_ref[...].astype(F32)
-    out_ref[13, 16:24, 0:16] = face_ref[...].astype(F32)
-
-
-def first_kernel(route, lam_a, lam_b, misc_a, misc_b, flip3, x_ref, sends_ref, scratch):
-    weights = jnp.concatenate(
-        [HALF * ref[c] for ref in (lam_a, lam_b) for c in range(3)], axis=1
-    )
+            out_ref[3 * (3 - s) + c, 0:28, :] = q_ref[s + 1, c]
+            out_ref[3 * (3 - s) + c, 28:32, :] = ones
+    out_ref[DEPTH, 0:28, :] = depth_ref[...]
+    out_ref[DEPTH, 28:32, :] = ones
+    out_ref[MISC] = jnp.zeros((32, E), F32)
+    out_ref[MISC, 0:4, :] = metric_ref[...]
+    out_ref[MISC, 4:7, :] = tag_ref[...].astype(F32)
+    out_ref[MISC, 8:11, :] = link_ref[...].astype(F32)
+    out_ref[MISC, 16:24, 0:16] = face_ref[...].astype(F32)
+
+
+def first_boxes(part_ref, flip3, block):
+    misc = part_ref[MISC]
+    weights = jnp.concatenate([HALF * part_ref[c] for c in range(3)], axis=1)
     flipped = times3(flip3[...], weights)
-    trace_list, sends = [], []
-    for b, misc_ref in enumerate((misc_a, misc_b)):
-        misc = misc_ref[0]
-        normals = geometry(misc)[1]
-        pick = lambda c, f: flipped[8 * f : 8 * f + 8, 384 * b + 128 * c : 384 * b + 128 * c + 128]
-        trace_list.append(traces([[pick(c, f) for f in range(3)] for c in range(3)], normals))
-        sends.append(send_matrix(misc))
-        sends_ref[b] = sends[b]
-    send(x_ref, scratch, route, sends, trace_list)
+    split = [
+        [flipped[8 * f : 8 * f + 8, 128 * c : 128 * c + 128] for f in range(3)] for c in range(3)
+    ]
+    sends = send_matrix(misc)
+    return sends, slot_rows(sends, traces(split, geometry(misc)[1]), block)
+
+
+def own_first_kernel(part_ref, flip3, sends_ref, boxes_ref):
+    sends_ref[...], boxes_ref[...] = first_boxes(part_ref, flip3, 0)
+
+
+def halo_first_kernel(part_ref, flip3, boxes_ref, x_ref, sends_ref):
+    sends_ref[...], boxes = first_boxes(part_ref, flip3, 1)
+    send(x_ref, neighbours(), [boxes_ref[...], boxes])
+
+
+def fold_kernel(y_ref, out_ref):
+    total = y_ref[0:8, :]
+    for e in range(1, GROUP):
+        total = total + y_ref[8 * e : 8 * e + 8, :]
+    out_ref[...] = jnp.broadcast_to(total[0:1, 127:128], out_ref.shape)
 
 
 def near_kernel(section, blocks, *refs):
@@ -347,12 +321,11 @@
     drag = refs.pop(0)
     back3, flip3, grad3, take2, spread3 = [refs.pop(0)[...] for _ in range(5)]
     lams = [refs.pop(0) for _ in range(blocks)]
-    states = [refs.pop(0) for _ in range(blocks)]
-    depths = [refs.pop(0) for _ in range(blocks)]
-    miscs = [refs.pop(0) for _ in range(blocks)]
+    parts = [refs.pop(0) for _ in range(blocks)]
     old_ref = refs.pop(0) if section < 3 else None
     if section == 0:
-        lam3_ref, speed_ref, angle_ref = refs.pop(0), refs.pop(0), refs.pop(0)
+        state_ref, lam3_ref = refs.pop(0), refs.pop(0)
+        speed_ref, angle_ref = refs.pop(0), refs.pop(0)
     base_ref = refs.pop(0)
     if section > 0:
         ahead_ref = refs.pop(0)
@@ -369,10 +342,10 @@
     lam = [[lams[b][c] for c in range(3)] for b in range(blocks)]
     w = [[scale * x for x in lam[b]] for b in range(blocks)]
     if section == 0:
-        q = [[jnp.concatenate([states[0][0, c], pad], axis=0) for c in range(3)]]
+        q = [[jnp.concatenate([state_ref[0, c], pad], axis=0) for c in range(3)]]
     else:
-        q = [[states[b][c] for c in range(3)] for b in range(blocks)]
-    z = [depths[b][0] for b in range(blocks)]
+        q = [[parts[b][3 * (4 - section) + c] for c in range(3)] for b in range(blocks)]
+    z = [parts[b][DEPTH] for b in range(blocks)]
     pulled = times3(back3, jnp.concatenate([x for b in range(blocks) for x in w[b]], axis=1))
     slopes = times3(grad3, jnp.concatenate(z, axis=1))
     fields = jnp.concatenate([x for b in range(blocks) for x in q[b] + [z[b]]], axis=1)
@@ -381,7 +354,7 @@
 
     face_sums, volumes, opens = [], [], []
     for b in range(blocks):
-        misc = miscs[b][0]
+        misc = parts[b][MISC]
         (rx, ry, sx, sy), normals = geometry(misc)
         part = lambda r0, r1, c: pulled[r0:r1, 384 * b + 128 * c : 384 * b + 128 * c + 128]
         h = q[b][0]
@@ -497,7 +470,7 @@
         sum_ref[4, 0:24, :] = opens
         sum_ref[4, 24:32, :] = fold
     else:
-        rx, ry, sx, sy = geometry(miscs[0][0])[0]
+        rx, ry, sx, sy = geometry(parts[0][MISC])[0]
         w1, w2, g1, g2 = news
         pair = GRAVITY * jnp.concatenate([rx * g1 + ry * g2, sx * g1 + sy * g2], axis=1)
         pulled = times3(back3, pair)
@@ -512,41 +485,49 @@
 
 def far_kernel(section, blocks, *refs):
     refs = list(refs)
-    route, y_ref, spread3_ref, base_ref, motion_ref = [refs.pop(0) for _ in range(5)]
-    miscs = [refs.pop(0) for _ in range(blocks)]
+    y_ref, spread3_ref, base_ref, motion_ref = [refs.pop(0) for _ in range(4)]
+    parts = [refs.pop(0) for _ in range(blocks)]
     if section > 0:
-        ahead_ref, sends_ref = refs.pop(0), refs.pop(0)
+        ahead_ref = refs.pop(0)
+        sends_refs = [refs.pop(0), refs.pop(0)]
     if section == 1:
         q0_ref, sum_ref = refs.pop(0), refs.pop(0)
     lam_refs = [refs.pop(0) for _ in range(blocks)]
     if section > 0:
-        x_ref, scratch = refs.pop(0), refs.pop(0)
+        x_ref = refs.pop(0)
     later = SIXTH if section == 3 else HALF
 
+    near_by = neighbours()
     boxes = []
     for b in range(2):
         for j in range(DIRS):
             if b < blocks:
-                place = pl.multiple_of(route[64 + 16 * b + j] * 8, 8)
-                kind = route[72 + 16 * b + j]
-                box = y_ref[pl.ds(place, 8), :]
-                box = jnp.where(kind == 1, pltpu.roll(box, 64, 1), box)
-                boxes.append(jnp.where(kind == 2, 0.0, box))
+                device, second, exists = near_by[DIRS * b + j]
+                box = y_ref[pl.ds(pl.multiple_of(device * 8, 8), 8), :]
+                box = jnp.where(second == 1, pltpu.roll(box, 64, 1), box)
+                boxes.append(jnp.where(exists, box, 0.0))
             else:
                 boxes.append(jnp.zeros((8, 128), F32))
     turned = jnp.transpose(jnp.concatenate(boxes, axis=0))
-    hi, lo = halves(jnp.concatenate([turned[0:24], turned[32:56]], axis=1))
-    pool = jnp.concatenate([hi, lo], axis=0).astype(BF16)
-    rows = lax.broadcasted_iota(jnp.int32, (256, E), 0)
+    low, high = turned[0:24], turned[32:56]
+    left = lax.broadcasted_iota(jnp.int32, (24, 128), 1) < 64
+    rows = lax.broadcasted_iota(jnp.int32, (128, E), 0)
     face_sums = []
     for b in range(blocks):
-        links = miscs[b][0][8:11].astype(jnp.int32)
+        if b == 0:
+            pool = jnp.where(left, low, pltpu.roll(high, 64, 1))
+        else:
+            pool = jnp.where(left, pltpu.roll(low, 64, 1), high)
+        pool = jnp.concatenate(halves(pool), axis=0).astype(BF16)
+        links = parts[b][MISC, 8:11].astype(jnp.int32)
+        match = [
+            jnp.where(rows == far_index(links[f : f + 1]), 1.0, 0.0).astype(BF16) for f in range(3)
+        ]
+        got = dot(pool, jnp.concatenate(match, axis=1))
+        got = got[0:24] + got[24:48]
         sums = [[], [], []]
         for f in range(3):
-            match = jnp.where(rows == far_index(links[f : f + 1], b), 1.0, 0.0).astype(BF16)
-            got = dot(pool, match)
-            got = got[0:24] + got[24:48]
-            far = (got[0:8], got[8:16], got[16:24])
+            far = [got[8 * c : 8 * c + 8, 128 * f : 128 * f + 128] for c in range(3)]
             motion = [motion_ref[b, i, 8 * f : 8 * f + 8, :] for i in range(3)]
             theirs = jump_back(tuple(x[7:8] for x in far), far, *motion)
             for c in range(3):
@@ -568,14 +549,15 @@
                 for c in range(3)
             ]
             split = [[flipped[c][8 * f : 8 * f + 8] for f in range(3)] for c in range(3)]
-            trace_list.append(traces(split, geometry(miscs[b][0])[1]))
+            trace_list.append(traces(split, geometry(parts[b][MISC])[1]))
         else:
             for c in range(3):
                 lam_refs[b][c] = lam[c][0:28]
         if section == 1 and b == 0:
             first = lam
     if section > 0:
-        send(x_ref, scratch, route, [sends_ref[0], sends_ref[1]], trace_list)
+        boxes = [slot_rows(sends_refs[b][...], trace_list[b], b) for b in range(2)]
+        send(x_ref, near_by, boxes)
     if section == 1:
         q0 = [q0_ref[0, c] for c in range(3)]
         flow = (q0[1] * first[1][0:28] + q0[2] * first[2][0:28]) * (HALF / q0[0])
@@ -586,25 +568,13 @@
             x_ref[8 * e : 8 * e + 8, :] = jnp.where(lane == 127, -total, part)
 
 
-def whole(shape):
-    return pl.BlockSpec(shape, lambda i: (0,) * len(shape))
-
-
-def block(shape, first):
-    return pl.BlockSpec(shape, lambda i: (first,) + (0,) * (len(shape) - 1))
-
-
-SCALARS = pl.BlockSpec(memory_space=pltpu.SMEM)
-
-
-def call(kernel, in_specs, outs, args, scratch=()):
+def call(kernel, outs, args, scalars=0):
+    vmem, smem = pl.BlockSpec(memory_space=pltpu.VMEM), pl.BlockSpec(memory_space=pltpu.SMEM)
     return pl.pallas_call(
         kernel,
-        grid=(1,),
-        in_specs=in_specs,
-        out_specs=[whole(shape) for shape, _ in outs],
+        in_specs=[smem] * scalars + [vmem] * (len(args) - scalars),
+        out_specs=[vmem] * len(outs),
         out_shape=[jax.ShapeDtypeStruct(shape, dtype) for shape, dtype in outs],
-        scratch_shapes=list(scratch),
         compiler_params=pltpu.CompilerParams(vmem_limit_bytes=32 * 1024 * 1024),
     )(*args)
 
@@ -626,109 +596,58 @@
     strides = [list(range(d, devices, GROUP)) for d in range(GROUP)]
     back3, flip3, grad3, take2, spread3 = constants()
     tables = [back3, flip3, grad3, take2, spread3]
-    table_specs = [whole(t.shape) for t in tables]
-    me = lax.rem(lax.axis_index("dom"), GROUP)
-    route = lax.dynamic_slice(jnp.asarray(routes()), (me, 0), (1, 128)).reshape(128)
-
-    nodes, mixed = (32, E), (3, 32, E)
-    mine = call(
-        pack_kernel,
-        [whole(x.shape) for x in (saved_states, adjoint_final, bathymetry, metrics)]
-        + [whole(x.shape) for x in (face_tag, face_link, send_faces)],
-        [((14, 32, E), F32)],
-        (saved_states, adjoint_final, bathymetry, metrics, face_tag, face_link, send_faces),
-    )[0]
+
+    mixed, x_out = ((3, 32, E), F32), ((GROUP * 8, 128), F32)
+    sends_out, sums_out = ((128, 384), BF16), ((5, 32, E), F32)
     pairs = [(i, i) for i in range(ROW)] + [(i, i) for i in range(devices - ROW, devices)]
     for row in range(1, devices // ROW - 1, 2):
         for i in range(row * ROW, row * ROW + ROW):
             pairs += [(i, i + ROW), (i + ROW, i)]
+    pack_args = (saved_states, adjoint_final, bathymetry)
+    pack_args += (metrics, face_tag, face_link, send_faces)
+    mine = call(pack_kernel, [((14, 32, E), F32)], pack_args)[0]
     halo = lax.ppermute(mine, "dom", pairs)
-    both = (mine, halo)
-
-    scratch = [pltpu.VMEM((2, 72, 128), F32)]
-    x_out = ((GROUP * 8, 128), F32)
-    x, sends = call(
-        first_kernel,
-        [SCALARS]
-        + [block((3, 32, E), 3)] * 2
-        + [block((1, 32, E), 13)] * 2
-        + [whole(flip3.shape)],
-        [x_out, ((2, 64, 768), BF16)],
-        (route, mine, halo, mine, halo, flip3),
-        scratch,
-    )
+    both = [mine, halo]
+
+    my_sends, boxes = call(own_first_kernel, [sends_out, ((64, 128), F32)], (mine, flip3))
+    x, halo_sends = call(halo_first_kernel, [x_out, sends_out], (halo, flip3, boxes))
     lams = both
-    lam3 = sums = None
+    sums = []
     for section in (3, 2, 1, 0):
         y = lax.all_to_all(x, "dom", 0, 0, tiled=True, axis_index_groups=groups)
         blocks = 2 if section > 0 else 1
-        args = [drag_rate] + tables + list(lams[:blocks])
-        specs = [SCALARS] + table_specs
-        specs += [block(mixed, 3)] * blocks if section == 3 else [whole(mixed)] * blocks
+        bases, faces = ((blocks, 3, 32, E), F32), ((blocks, 3, 24, E), F32)
+        args = [drag_rate] + tables + list(lams[:blocks]) + both[:blocks] + sums
         if section > 0:
-            args += list(both)
-            specs += [block(mixed, section - 1)] * blocks
+            outs = [bases, faces, faces, sums_out]
         else:
-            args += [saved_states]
-            specs += [pl.BlockSpec((1, 3, 28, E), lambda i: (0, 0, 0, 0))]
-        args += list(both[:blocks]) * 2
-        specs += [block((1, 32, E), 12)] * blocks + [block((1, 32, E), 13)] * blocks
-        if section < 3:
-            args.append(sums)
-            specs.append(whole((5, 32, E)))
-        outs = [((blocks, 3, 32, E), F32)]
+            args += [saved_states, lam3, wind_speed, wind_angle]
+            outs = [bases, faces] + [((28, E), F32)] * 3
+        got = call(lambda *refs, s=section, n=blocks: near_kernel(s, n, *refs), outs, args, 1)
         if section > 0:
-            outs.append(((blocks, 3, 24, E), F32))
-        outs.append(((blocks, 3, 24, E), F32))
-        if section > 0:
-            outs.append(((5, 32, E), F32))
-        else:
-            args += [lam3, wind_speed, wind_angle]
-            specs += [whole(mixed), whole((28, E)), whole((28, E))]
-            outs += [((28, E), F32)] * 3
-        got = call(
-            lambda *refs, s=section, n=blocks: near_kernel(s, n, *refs), specs, outs, args
-        )
-        if section > 0:
-            base, ahead, motion, sums = got
+            base, ahead, motion = got[:3]
+            sums = list(got[3:])
         else:
             base, motion, depth_gradient, speed_gradient, angle_gradient = got
 
-        args = [route, y, spread3, base, motion] + list(both[:blocks])
-        specs = [SCALARS] + [whole(v.shape) for v in (y, spread3, base, motion)]
-        specs += [block((1, 32, E), 13)] * blocks
+        args = [y, spread3, base, motion] + both[:blocks]
         if section > 0:
-            args += [ahead, sends]
-            specs += [whole(ahead.shape), whole(sends.shape)]
-        if section == 1:
-            args += [saved_states, sums]
-            specs += [pl.BlockSpec((1, 3, 28, E), lambda i: (0, 0, 0, 0)), whole((5, 32, E))]
-        if section > 0:
-            outs = [(mixed, F32)] * 2 + [x_out]
+            args += [ahead, my_sends, halo_sends]
+            outs = [mixed] * 2 + [x_out]
         else:
             outs = [((3, 28, E), F32)]
-        got = call(
-            lambda *refs, s=section, n=blocks: far_kernel(s, n, *refs),
-            specs,
-            outs,
-            args,
-            scratch if section > 0 else (),
-        )
+        if section == 1:
+            args += [saved_states] + sums
+        got = call(lambda *refs, s=section, n=blocks: far_kernel(s, n, *refs), outs, args)
         if section > 0:
             lams, x = got[0:2], got[2]
             if section == 3:
                 lam3 = lams[0]
         else:
             initial = got[0]
-    within = jnp.sum(y.reshape(GROUP, 8, 128)[:, 0, 127])
-    spread = lax.all_to_all(
-        jnp.broadcast_to(within, (devices // GROUP, 128)),
-        "dom",
-        0,
-        0,
-        tiled=True,
-        axis_index_groups=strides,
-    )
+    y, initial = lax.optimization_barrier((y, initial))
+    within = call(fold_kernel, [((devices // GROUP, 128), F32)], (y,))[0]
+    spread = lax.all_to_all(within, "dom", 0, 0, tiled=True, axis_index_groups=strides)
     drag_gradient = jnp.sum(spread[:, 0]).reshape(1)
     return (initial, depth_gradient, speed_gradient, angle_gradient, drag_gradient)
 

time: 101 us -> 99.1 us (0.981)
  blocking collectives: 13.2 us -> 18.2 us
  starting transfers between devices: 39.9 us -> 35.4 us
  local copies, waits for them, and re-layouts: 2.98 us -> 1.03 us
  Pallas kernels: 12.7 us -> 11.5 us
  waiting for transfers between devices: 28.2 us -> 29.4 us
    all_to_all x1 -> x0, starting transfers between devices: 9.59 us -> none  [local(): lax.all_to_all(jnp.broadcast_to(within, (devices // GROUP, 128)), 'dom',...]
    all_to_all x3 -> x4, waiting for transfers between devices: 22.4 us -> 29.4 us  [local(): y = lax.all_to_all(x, 'dom', 0, 0, tiled=True, axis_index_groups=groups)]
    all_to_all x1 -> x0, waiting for transfers between devices: 5.83 us -> none  [local(): lax.all_to_all(jnp.broadcast_to(within, (devices // GROUP, 128)), 'dom',...]
    all_to_all x3 -> x4, starting transfers between devices: 29.7 us -> 34.7 us  [local(): y = lax.all_to_all(x, 'dom', 0, 0, tiled=True, axis_index_groups=groups)]
    all_to_all x1, blocking collectives: 13.2 us -> 18.2 us  [local(): lax.all_to_all(within, 'dom', 0, 0, tiled=True, axis_index_groups=strides)]
    broadcast_in_dim x1 -> x0, local copies, waits for them, and re-layouts: 1.25 us -> none  [local(): jnp.broadcast_to(within, (devices // GROUP, 128))]
    pallas_call x10 -> x12, Pallas kernels: 12.7 us -> 11.5 us  [call(): pl.pallas_call(kernel, in_specs=[smem] * scalars + [vmem] * (len(args) -...]
  transfers between devices with their start and end apart: 5 -> 5, of which waited for: 4 -> 4; matrix products, arithmetic and copies ran while one was open for 1% -> 0% of each run, Pallas kernels for 5% -> 4%
where the time goes in v2:
time: 99.1 us; the launch traced here: 97.6 us
  starting transfers between devices  35.4 us (36%)
  waiting for transfers between devices  29.4 us (30%)
  blocking collectives  18.2 us (18%)
  Pallas kernels  11.5 us (12%)
  between operations  1.53 us (2%)
  local copies, waits for them, and re-layouts  1.03 us (1%)
    all_to_all x4, starting transfers between devices, local(): y = lax.all_to_all(x, 'dom', 0, 0, tiled=True, axis_index_groups=groups)  34.7 us
    all_to_all x4, waiting for transfers between devices, local(): y = lax.all_to_all(x, 'dom', 0, 0, tiled=True, axis_index_groups=groups)  29.4 us
    all_to_all x1, blocking collectives, local(): lax.all_to_all(within, 'dom', 0, 0, tiled=True, axis_index_groups=strides)  18.2 us
    pallas_call x12, Pallas kernels, call(): pl.pallas_call(kernel, in_specs=[smem] * scalars + [vmem] * (len(args) -...  11.5 us
  transfers between devices with their start and end apart: 5, of which 4 were waited for; matrix products, arithmetic and copies ran while one was open for 0% of the time, Pallas kernels for 4%

profile of v2, /device:TPU:1, one launch (start us, length us, event | category | flops | bytes accessed | tf_op | source)
XLA Modules:
  0.0 97.6 jit_solution(14251610334477139737)
XLA Ops:
  0.7 1.0 %copy.23.q_ref.refs_9_ = f32[4,3,28,128]{3,2,1,0:T(8,128)S(1)} copy(f32[4,3,28,128]{3,0,2,1:T(4,128)} %param.15) | data formatting | bytes 344064 | tf_op args[0]
  1.7 0.0 copy-start.3
  1.8 0.7 collective-permute-start
  2.5 0.5 shard_map.183
  3.0 1.2 %shard_map.184 = (f32[256,128]{1,0:T(8,128)}, bf16[128,384]{1,0:T(8,128)(2,1)S(1)}) custom-call(f32[14,32,128]{2,1,0:T(8,128)S(1)} %collective-permute-done.part_ref.refs_7_.refs_9_.refs_5_, bf16[24,96]{1,0:T(8,128)(2,1)S(1)} %copy-done.3, f32[64,128]{1,0:T(8,128)S(1)} %get-tuple-element.36.boxes_ref), custom_call_target="tpu_custom_call" | custom-call | tf_op jit(solution)/shard_map/pallas_call | solution.py:573
  4.3 21.1 %all-to-all-start = ((f32[32,8,128]{2,1,0:T(8,128)}), f32[32,8,128]{2,1,0:T(8,128)S(1)}, u32[]{:S(2)}, u32[]{:S(2)}) async-start(f32[32,8,128]{2,1,0:T(8,128)} %bitcast), calls=%async_computation | async-start | bytes 262144 | tf_op jit(solution)/shard_map/all_to_all | solution.py:617
  26.1 0.8 shard_map.185
  26.9 7.4 %all-to-all-done = f32[32,8,128]{2,1,0:T(8,128)S(1)} async-done(((f32[32,8,128]{2,1,0:T(8,128)}), f32[32,8,128]{2,1,0:T(8,128)S(1)}, u32[]{:S(2)}, u32[]{:S(2)}) %all-to-all-start) | async-done | bytes 131104 | tf_op jit(solution)/shard_map/all_to_all | solution.py:617
  34.3 1.6 %shard_map.186 = (f32[3,32,128]{2,1,0:T(8,128)S(1)}, f32[3,32,128]{2,1,0:T(8,128)S(1)}, f32[256,128]{1,0:T(8,128)}) custom-call(f32[256,128]{1,0:T(8,128)S(1)} %bitcast.17, bf16[56,80]{1,0:T(8,128)(2,1)S(1)} %copy-done, f32[2,3,32,128]{3,2,1,0:T(8,128)S(1)} %get-tuple-element.38.refs_2_, f32[2,3,24,128]{3,2,1,0:T(8,128)S(1)} %get-tuple-element.39.refs_3_, ...), custom_call_target="tpu_custom_call" | custom-call | tf_op jit(solution)/shard_map/pallas_call | solution.py:573
  35.9 4.0 %all-to-all-start.1 = ((f32[32,8,128]{2,1,0:T(8,128)}), f32[32,8,128]{2,1,0:T(8,128)S(1)}, u32[]{:S(2)}, u32[]{:S(2)}) async-start(f32[32,8,128]{2,1,0:T(8,128)} %bitcast.2), calls=%async_computation.1 | async-start | bytes 262144 | tf_op jit(solution)/shard_map/all_to_all | solution.py:617
  39.9 0.8 shard_map.187
  40.7 7.5 %all-to-all-done.1 = f32[32,8,128]{2,1,0:T(8,128)S(1)} async-done(((f32[32,8,128]{2,1,0:T(8,128)}), f32[32,8,128]{2,1,0:T(8,128)S(1)}, u32[]{:S(2)}, u32[]{:S(2)}) %all-to-all-start.1) | async-done | bytes 131104 | tf_op jit(solution)/shard_map/all_to_all | solution.py:617
  48.2 1.6 %shard_map.188 = (f32[3,32,128]{2,1,0:T(8,128)S(1)}, f32[3,32,128]{2,1,0:T(8,128)S(1)}, f32[256,128]{1,0:T(8,128)}) custom-call(f32[256,128]{1,0:T(8,128)S(1)} %bitcast.16, bf16[56,80]{1,0:T(8,128)(2,1)S(1)} %copy-done, f32[2,3,32,128]{3,2,1,0:T(8,128)S(1)} %get-tuple-element.47.refs_2_, f32[2,3,24,128]{3,2,1,0:T(8,128)S(1)} %get-tuple-element.48.refs_3_, ...), custom_call_target="tpu_custom_call" | custom-call | tf_op jit(solution)/shard_map/pallas_call | solution.py:573
  49.8 4.7 %all-to-all-start.2 = ((f32[32,8,128]{2,1,0:T(8,128)}), f32[32,8,128]{2,1,0:T(8,128)S(1)}, u32[]{:S(2)}, u32[]{:S(2)}) async-start(f32[32,8,128]{2,1,0:T(8,128)} %bitcast.4), calls=%async_computation.2 | async-start | bytes 262144 | tf_op jit(solution)/shard_map/all_to_all | solution.py:617
  54.5 0.8 shard_map.189
  55.3 7.5 %all-to-all-done.2 = f32[32,8,128]{2,1,0:T(8,128)S(1)} async-done(((f32[32,8,128]{2,1,0:T(8,128)}), f32[32,8,128]{2,1,0:T(8,128)S(1)}, u32[]{:S(2)}, u32[]{:S(2)}) %all-to-all-start.2) | async-done | bytes 131104 | tf_op jit(solution)/shard_map/all_to_all | solution.py:617
  62.8 1.6 %shard_map.190 = (f32[3,32,128]{2,1,0:T(8,128)S(1)}, f32[3,32,128]{2,1,0:T(8,128)}, f32[256,128]{1,0:T(8,128)}) custom-call(f32[256,128]{1,0:T(8,128)S(1)} %bitcast.15, bf16[56,80]{1,0:T(8,128)(2,1)S(1)} %copy-done, f32[2,3,32,128]{3,2,1,0:T(8,128)S(1)} %get-tuple-element.54.refs_2_, f32[2,3,24,128]{3,2,1,0:T(8,128)S(1)} %get-tuple-element.55.refs_3_, ...), custom_call_target="tpu_custom_call" | custom-call | tf_op jit(solution)/shard_map/pallas_call | solution.py:573
  64.4 4.9 %all-to-all-start.3 = ((f32[32,8,128]{2,1,0:T(8,128)}), f32[32,8,128]{2,1,0:T(8,128)S(1)}, u32[]{:S(2)}, u32[]{:S(2)}) async-start(f32[32,8,128]{2,1,0:T(8,128)} %bitcast.6), calls=%async_computation.3 | async-start | bytes 262144 | tf_op jit(solution)/shard_map/all_to_all | solution.py:617
  69.3 1.2 %shard_map.191 = (f32[1,3,32,128]{3,2,1,0:T(8,128)S(1)}, f32[1,3,24,128]{3,2,1,0:T(8,128)S(1)}, f32[28,128]{1,0:T(8,128)}, f32[28,128]{1,0:T(8,128)}, f32[28,128]{1,0:T(8,128)}) custom-call(f32[1]{0:T(128)S(6)} %copy.27.refs_0_, bf16[112,96]{1,0:T(8,128)(2,1)S(1)} %copy-done.1, bf16[24,96]{1,0:T(8,128)(2,1)S(1)} %copy-done.3, bf16[64,96]{1,0:T(8,128)(2,1)S(1)} %copy-done.2, ...), custom_call_target="tpu_custom_call" | custom-call | tf_op jit(solution)/shard_map/pallas_call | solution.py:573
  70.5 7.0 %all-to-all-done.3 = f32[32,8,128]{2,1,0:T(8,128)S(1)} async-done(((f32[32,8,128]{2,1,0:T(8,128)}), f32[32,8,128]{2,1,0:T(8,128)S(1)}, u32[]{:S(2)}, u32[]{:S(2)}) %all-to-all-start.3) | async-done | bytes 131104 | tf_op jit(solution)/shard_map/all_to_all | solution.py:617
  77.6 1.1 %shard_map.192 = f32[3,28,128]{2,1,0:T(8,128)} custom-call(f32[256,128]{1,0:T(8,128)S(1)} %bitcast.13, bf16[56,80]{1,0:T(8,128)(2,1)S(1)} %copy-done, f32[1,3,32,128]{3,2,1,0:T(8,128)S(1)} %get-tuple-element.60.refs_2_, f32[1,3,24,128]{3,2,1,0:T(8,128)S(1)} %get-tuple-element.61.refs_3_, f32[14,32,128]{2,1,0:T(8,128)S(1)} %shard_map.182.part_ref.refs_6_.refs_8_.refs_4_.refs_7_), custom_call_target="tpu_custom_call" | custom-call | tf_op jit(solution)/shard_map/pallas_call | solution.py:573
  78.7 0.1 shard_map.193
  78.8 18.2 %all_to_all.56 = f32[16,1,128]{2,1,0:T(1,128)S(1)} all-to-all(f32[16,1,128]{2,1,0:T(1,128)S(1)} %bitcast.18), channel_id=1, replica_groups={{0,32,64,96,128,160,192,224,256,288,320,352,384,416,448,480},{1,33,65,9..., dimensions={0} | all-to-all | bytes 16384 | tf_op jit(solution)/shard_map/all_to_all | solution.py:650
  97.0 0.6 slice_reduce_fusion
  (27 shorter events, 0.1 us)
Async XLA Ops:
  0.6 1.0 %copy-start.9 = (s32[8,16]{1,0:T(8,128)S(1)}, s32[8,16]{1,0:T(8,128)}, u32[]{:S(2)}) copy-start(s32[8,16]{1,0:T(8,128)} %face_ref.1) | copy-start | bytes 1540
  0.6 1.0 %copy-start.11 = (s32[3,128]{1,0:T(4,128)S(1)}, s32[3,128]{1,0:T(4,128)}, u32[]{:S(2)}) copy-start(s32[3,128]{1,0:T(4,128)} %tag_ref.1) | copy-start | bytes 4612
  0.7 1.0 %copy-start.12 = (s32[3,128]{1,0:T(4,128)S(1)}, s32[3,128]{1,0:T(4,128)}, u32[]{:S(2)}) copy-start(s32[3,128]{1,0:T(4,128)} %link_ref.1) | copy-start | bytes 4612
  0.7 1.0 %copy-start.10 = (f32[4,128]{1,0:T(4,128)S(1)}, f32[4,128]{1,0:T(4,128)}, u32[]{:S(2)}) copy-start(f32[4,128]{1,0:T(4,128)} %metric_ref.1) | copy-start | bytes 6148
  0.7 1.0 %copy-start.6 = (f32[28,128]{1,0:T(8,128)S(1)}, f32[28,128]{1,0:T(8,128)}, u32[]{:S(2)}) copy-start(f32[28,128]{1,0:T(8,128)} %depth_ref.1) | copy-start | bytes 43012
  0.7 1.0 %copy-start.5 = (f32[3,28,128]{2,1,0:T(8,128)S(1)}, f32[3,28,128]{2,1,0:T(8,128)}, u32[]{:S(2)}) copy-start(f32[3,28,128]{2,1,0:T(8,128)} %lam_ref.1) | copy-start | bytes 129028
  1.7 0.7 copy-start.3
  1.8 1.2 %collective-permute-start = (f32[14,32,128]{2,1,0:T(8,128)S(1)}, f32[14,32,128]{2,1,0:T(8,128)S(1)}, u32[]{:S(2)}, u32[]{:S(2)}) collective-permute-start(f32[14,32,128]{2,1,0:T(8,128)S(1)} %shard_map.182.part_ref.refs_6_.refs_8_.refs_4_.refs_7_), channel_id=1, source_target_pairs={{0,0},{1,1},{2,2},{3,3},{4,4},{5,5},{6,6},{7,7},{8,8},{9,9},{10,10... | collective-permute-start | bytes 688136 | tf_op jit(solution)/shard_map/ppermute | solution.py:609
  4.3 21.8 %copy-start = (bf16[56,80]{1,0:T(8,128)(2,1)S(1)}, bf16[56,80]{1,0:T(8,128)(2,1)}, u32[]{:S(2)}) copy-start(bf16[56,80]{1,0:T(8,128)(2,1)} %constant.16.clone.refs_5_.refs_1_) | copy-start | bytes 26884
  4.3 21.8 %copy-start.1 = (bf16[112,96]{1,0:T(8,128)(2,1)S(1)}, bf16[112,96]{1,0:T(8,128)(2,1)}, u32[]{:S(2)}) copy-start(bf16[112,96]{1,0:T(8,128)(2,1)} %constant.12.clone.refs_1_) | copy-start | bytes 64516
  4.3 21.8 %copy-start.2 = (bf16[64,96]{1,0:T(8,128)(2,1)S(1)}, bf16[64,96]{1,0:T(8,128)(2,1)}, u32[]{:S(2)}) copy-start(bf16[64,96]{1,0:T(8,128)(2,1)} %constant.14.clone.refs_3_) | copy-start | bytes 36868
  4.3 21.8 %copy-start.4 = (bf16[24,64]{1,0:T(8,128)(2,1)S(1)}, bf16[24,64]{1,0:T(8,128)(2,1)}, u32[]{:S(2)}) copy-start(bf16[24,64]{1,0:T(8,128)(2,1)} %constant.15.clone.refs_4_) | copy-start | bytes 9220
  4.3 30.0 %all-to-all-start = ((f32[32,8,128]{2,1,0:T(8,128)}), f32[32,8,128]{2,1,0:T(8,128)S(1)}, u32[]{:S(2)}, u32[]{:S(2)}) async-start(f32[32,8,128]{2,1,0:T(8,128)} %bitcast), calls=%async_computation | async-start | bytes 262144 | tf_op jit(solution)/shard_map/all_to_all | solution.py:617
  35.9 12.3 %all-to-all-start.1 = ((f32[32,8,128]{2,1,0:T(8,128)}), f32[32,8,128]{2,1,0:T(8,128)S(1)}, u32[]{:S(2)}, u32[]{:S(2)}) async-start(f32[32,8,128]{2,1,0:T(8,128)} %bitcast.2), calls=%async_computation.1 | async-start | bytes 262144 | tf_op jit(solution)/shard_map/all_to_all | solution.py:617
  49.8 13.0 %all-to-all-start.2 = ((f32[32,8,128]{2,1,0:T(8,128)}), f32[32,8,128]{2,1,0:T(8,128)S(1)}, u32[]{:S(2)}, u32[]{:S(2)}) async-start(f32[32,8,128]{2,1,0:T(8,128)} %bitcast.4), calls=%async_computation.2 | async-start | bytes 262144 | tf_op jit(solution)/shard_map/all_to_all | solution.py:617
  64.4 4.9 %copy-start.7 = (f32[28,128]{1,0:T(8,128)S(1)}, f32[28,128]{1,0:T(8,128)}, u32[]{:S(2)}) copy-start(f32[28,128]{1,0:T(8,128)} %refs_11_.1) | copy-start | bytes 43012
  64.4 4.9 %copy-start.8 = (f32[28,128]{1,0:T(8,128)S(1)}, f32[28,128]{1,0:T(8,128)}, u32[]{:S(2)}) copy-start(f32[28,128]{1,0:T(8,128)} %refs_12_.1) | copy-start | bytes 43012
  64.4 13.1 %all-to-all-start.3 = ((f32[32,8,128]{2,1,0:T(8,128)}), f32[32,8,128]{2,1,0:T(8,128)S(1)}, u32[]{:S(2)}, u32[]{:S(2)}) async-start(f32[32,8,128]{2,1,0:T(8,128)} %bitcast.6), calls=%async_computation.3 | async-start | bytes 262144 | tf_op jit(solution)/shard_map/all_to_all | solution.py:617

commit v3 on v2

--- a/solution.py
+++ b/solution.py
@@ -17,6 +17,7 @@
 SIXTH = TIME_STEP / 6.0
 
 GROUP = 32
+STRIDE = 16
 ROW = 16
 REACH = 4
 DIRS = 8
@@ -126,6 +127,20 @@
     return found
 
 
+def spread_steps():
+    return [(q // 4, q % 4, 1 if q % 4 in (1, 2) else 0) for q in range(STRIDE)]
+
+
+def spread_pairs(devices):
+    pairs = []
+    for group in range(devices // GROUP):
+        for q, (dx, dy, row) in enumerate(spread_steps()):
+            other = (group // 4 + dx) % 4 * 4 + (group % 4 + dy) % 4
+            other_row = 0 if dy == 0 else 1 - row
+            pairs.append((other * GROUP + other_row * ROW + q, group * GROUP + row * ROW + q))
+    return pairs
+
+
 def parts3(matrix, width):
     padded = np.zeros((matrix.shape[0], width))
     padded[:, : matrix.shape[1]] = matrix
@@ -300,7 +315,9 @@
     return sends, slot_rows(sends, traces(split, geometry(misc)[1]), block)
 
 
-def own_first_kernel(part_ref, flip3, sends_ref, boxes_ref):
+def own_first_kernel(part_ref, flip3, drag_ref, *refs):
+    sends_ref, boxes_ref, rate_ref = refs[-3:]
+    rate_ref[...] = jnp.full((8, E), drag_ref[0], F32)
     sends_ref[...], boxes_ref[...] = first_boxes(part_ref, flip3, 0)
 
 
@@ -309,20 +326,15 @@
     send(x_ref, neighbours(), [boxes_ref[...], boxes])
 
 
-def fold_kernel(y_ref, out_ref):
-    total = y_ref[0:8, :]
-    for e in range(1, GROUP):
-        total = total + y_ref[8 * e : 8 * e + 8, :]
-    out_ref[...] = jnp.broadcast_to(total[0:1, 127:128], out_ref.shape)
-
-
 def near_kernel(section, blocks, *refs):
     refs = list(refs)
-    drag = refs.pop(0)
     back3, flip3, grad3, take2, spread3 = [refs.pop(0)[...] for _ in range(5)]
+    rate_ref = refs.pop(0)
     lams = [refs.pop(0) for _ in range(blocks)]
     parts = [refs.pop(0) for _ in range(blocks)]
     old_ref = refs.pop(0) if section < 3 else None
+    if section == 3:
+        state_ref = refs.pop(0)
     if section == 0:
         state_ref, lam3_ref = refs.pop(0), refs.pop(0)
         speed_ref, angle_ref = refs.pop(0), refs.pop(0)
@@ -330,13 +342,15 @@
     if section > 0:
         ahead_ref = refs.pop(0)
     motion_ref = refs.pop(0)
+    if section == 3:
+        past_ref = refs.pop(0)
     if section > 0:
         sum_ref = refs.pop(0)
     else:
         depth_out, speed_out, angle_out = refs.pop(0), refs.pop(0), refs.pop(0)
     scale = SIXTH if section == 2 else HALF
     later = SIXTH if section == 3 else HALF
-    drag_rate = drag[0]
+    drag_rate = rate_ref[...][0:1]
     pad = jnp.ones((4, E), F32)
 
     lam = [[lams[b][c] for c in range(3)] for b in range(blocks)]
@@ -351,6 +365,16 @@
     fields = jnp.concatenate([x for b in range(blocks) for x in q[b] + [z[b]]], axis=1)
     hi, lo = halves(fields)
     at_faces = dot(take2, jnp.concatenate([hi, lo], axis=0).astype(BF16))
+
+    if section == 3:
+        fields = [jnp.concatenate([state_ref[0, c], pad], axis=0) for c in range(3)]
+        fields += [parts[0][9 + c] for c in range(3)]
+        hi, lo = halves(jnp.concatenate(fields, axis=1))
+        past = dot(take2, jnp.concatenate([hi, lo], axis=0).astype(BF16))
+        for i in range(2):
+            finv = 1.0 / past[:, 384 * i : 384 * i + 128]
+            past_ref[2 * i] = past[:, 384 * i + 128 : 384 * i + 256] * finv
+            past_ref[2 * i + 1] = past[:, 384 * i + 256 : 384 * i + 384] * finv
 
     face_sums, volumes, opens = [], [], []
     for b in range(blocks):
@@ -487,54 +511,96 @@
     refs = list(refs)
     y_ref, spread3_ref, base_ref, motion_ref = [refs.pop(0) for _ in range(4)]
     parts = [refs.pop(0) for _ in range(blocks)]
+    if section < 3:
+        normal_ref = refs.pop(0)
     if section > 0:
         ahead_ref = refs.pop(0)
         sends_refs = [refs.pop(0), refs.pop(0)]
-    if section == 1:
-        q0_ref, sum_ref = refs.pop(0), refs.pop(0)
+    if section == 3:
+        past_ref = refs.pop(0)
     lam_refs = [refs.pop(0) for _ in range(blocks)]
     if section > 0:
         x_ref = refs.pop(0)
+    if section == 3:
+        normal_ref = refs.pop(0)
+    if section == 0:
+        drag_ref = refs.pop(0)
     later = SIXTH if section == 3 else HALF
 
+    lane = lax.broadcasted_iota(jnp.int32, (8, 128), 1)
+    place_in = jnp.bitwise_and(lane, 31)
+    spare = (place_in >= 24) | (place_in == 7) | (place_in == 15) | (place_in == 23)
     near_by = neighbours()
-    boxes = []
+    boxes, extras = [], []
     for b in range(2):
         for j in range(DIRS):
             if b < blocks:
                 device, second, exists = near_by[DIRS * b + j]
-                box = y_ref[pl.ds(pl.multiple_of(device * 8, 8), 8), :]
-                box = jnp.where(second == 1, pltpu.roll(box, 64, 1), box)
+                raw = y_ref[pl.ds(pl.multiple_of(device * 8, 8), 8), :]
+                turned = pltpu.roll(raw, 64, 1)
+                if section == 2:
+                    box = jnp.where(second == 1, jnp.where(spare, 0.0, turned), raw)
+                    extras.append(jnp.where(exists & (second == 0), turned, 0.0))
+                else:
+                    box = jnp.where(second == 1, turned, raw)
                 boxes.append(jnp.where(exists, box, 0.0))
             else:
                 boxes.append(jnp.zeros((8, 128), F32))
-    turned = jnp.transpose(jnp.concatenate(boxes, axis=0))
-    low, high = turned[0:24], turned[32:56]
-    left = lax.broadcasted_iota(jnp.int32, (24, 128), 1) < 64
+    stacks = [jnp.transpose(jnp.concatenate(boxes, axis=0))]
+    if section == 2:
+        stacks.append(jnp.transpose(jnp.concatenate(extras, axis=0)))
+    left = lax.broadcasted_iota(jnp.int32, (32, 128), 1) < 64
     rows = lax.broadcasted_iota(jnp.int32, (128, E), 0)
-    face_sums = []
+    row = lax.broadcasted_iota(jnp.int32, (8, E), 0)
+    face_sums, factors = [], []
     for b in range(blocks):
-        if b == 0:
-            pool = jnp.where(left, low, pltpu.roll(high, 64, 1))
-        else:
-            pool = jnp.where(left, pltpu.roll(low, 64, 1), high)
+        pools = []
+        for turned in stacks:
+            low, high = turned[0:32], turned[32:64]
+            if b == 0:
+                pools.append(jnp.where(left, low, pltpu.roll(high, 64, 1)))
+            else:
+                pools.append(jnp.where(left, pltpu.roll(low, 64, 1), high))
+        pool = jnp.concatenate(pools, axis=0)
+        tall = pool.shape[0]
         pool = jnp.concatenate(halves(pool), axis=0).astype(BF16)
         links = parts[b][MISC, 8:11].astype(jnp.int32)
         match = [
             jnp.where(rows == far_index(links[f : f + 1]), 1.0, 0.0).astype(BF16) for f in range(3)
         ]
         got = dot(pool, jnp.concatenate(match, axis=1))
-        got = got[0:24] + got[24:48]
-        sums = [[], [], []]
+        got = got[0:tall] + got[tall:]
+        sums, scales = [[], [], []], [[], [], []]
         for f in range(3):
-            far = [got[8 * c : 8 * c + 8, 128 * f : 128 * f + 128] for c in range(3)]
+            piece = lambda r: got[r : r + 8, 128 * f : 128 * f + 128]
+            far = [piece(8 * c) for c in range(3)]
+            if section == 3:
+                normal = tuple(x[7:8] for x in far)
+                for i in range(3):
+                    normal_ref[b, f, i : i + 1, :] = normal[i]
+            else:
+                normal = tuple(normal_ref[b, f, i : i + 1, :] for i in range(3))
             motion = [motion_ref[b, i, 8 * f : 8 * f + 8, :] for i in range(3)]
-            theirs = jump_back(tuple(x[7:8] for x in far), far, *motion)
+            theirs = jump_back(normal, far, *motion)
             for c in range(3):
                 sums[c].append(-theirs[c])
+            if section == 3 and b == 0:
+                u0, v0, u1, v1 = [past_ref[i, 8 * f : 8 * f + 8, :] for i in range(4)]
+                nx, ny, size = normal
+                mean = 0.5 * (nx * u0 + ny * v0)
+                rate = 0.5 * (nx * u1 + ny * v1) - 0.5 * PENALTY * size
+                factors.append((mean, mean * u1 + u0 * rate, mean * v1 + v0 * rate))
+            if section == 2:
+                singles = (piece(24)[7:8], piece(56)[7:8], far[0][7:8], far[1][7:8], far[2][7:8])
+                singles += (piece(32)[7:8], piece(40)[7:8])
+                third = jnp.zeros((8, E), F32)
+                for k in range(7):
+                    third = jnp.where(row == k, singles[k], third)
+                factors.append((piece(24), piece(56), third))
         face_sums += [jnp.concatenate(sums[c], axis=0) for c in range(3)]
     spread = spread_faces(spread3_ref[...], jnp.concatenate(face_sums, axis=1))
-    trace_list = []
+    slots = []
+    partial = jnp.zeros((8, E), F32)
     for b in range(blocks):
         lam = []
         for c in range(3):
@@ -549,32 +615,111 @@
                 for c in range(3)
             ]
             split = [[flipped[c][8 * f : 8 * f + 8] for f in range(3)] for c in range(3)]
-            trace_list.append(traces(split, geometry(parts[b][MISC])[1]))
+            none = jnp.zeros((1, E), F32)
+            lasts = [(none,) * 3] * 3
+            if section == 3 and b == 0:
+                lasts = [tuple(factors[f][2][k : k + 1] for k in (2, 3, 4)) for f in range(3)]
+            trace = traces(split, lasts)
+            if section == 3 and b == 0:
+                last = row == 7
+                third = lambda f, k: factors[f][2][k : k + 1]
+                one = [jnp.where(last, third(f, 0), factors[f][0]) for f in range(3)]
+                two = [jnp.where(last, third(f, 1), factors[f][1]) for f in range(3)]
+                five = [jnp.where(last, third(f, 5), 0.0) for f in range(3)]
+                six = [jnp.where(last, third(f, 6), 0.0) for f in range(3)]
+                line = lambda parts: jnp.concatenate(parts, axis=1)
+                trace = jnp.concatenate([trace, line(one)], axis=0)
+                extra = [line(five), line(six), jnp.zeros((8, 3 * E), F32), line(two)]
+                slots.append(
+                    slot_rows(sends_refs[0][...], trace, 0)
+                    + slot_rows(sends_refs[0][...], jnp.concatenate(extra, axis=0), 1)
+                )
+            else:
+                slots.append(slot_rows(sends_refs[b][...], trace, b))
+            if section == 2:
+                for f in range(3):
+                    for c in range(3):
+                        partial = partial + split[c][f] * factors[3 * b + f][c]
         else:
             for c in range(3):
                 lam_refs[b][c] = lam[c][0:28]
-        if section == 1 and b == 0:
-            first = lam
     if section > 0:
-        boxes = [slot_rows(sends_refs[b][...], trace_list[b], b) for b in range(2)]
-        send(x_ref, near_by, boxes)
-    if section == 1:
-        q0 = [q0_ref[0, c] for c in range(3)]
-        flow = (q0[1] * first[1][0:28] + q0[2] * first[2][0:28]) * (HALF / q0[0])
-        total = jnp.sum(sum_ref[4, 24:32, :]) + jnp.sum(flow)
-        lane = lax.broadcasted_iota(jnp.int32, (8, 128), 1)
-        for e in range(GROUP):
-            part = x_ref[8 * e : 8 * e + 8, :]
-            x_ref[8 * e : 8 * e + 8, :] = jnp.where(lane == 127, -total, part)
-
-
-def call(kernel, outs, args, scalars=0):
-    vmem, smem = pl.BlockSpec(memory_space=pltpu.VMEM), pl.BlockSpec(memory_space=pltpu.SMEM)
+        send(x_ref, near_by, slots)
+    else:
+        group = lax.shift_right_logical(lax.axis_index("dom"), 5)
+        total = jnp.zeros((8, 128), F32)
+        for g in range(STRIDE):
+            dx = jnp.bitwise_and(g // 4 - lax.shift_right_logical(group, 2), 3)
+            dy = jnp.bitwise_and(g % 4 - jnp.bitwise_and(group, 3), 3)
+            device = 4 * dx + dy + jnp.where((dy == 1) | (dy == 2), ROW, 0)
+            total = total + y_ref[pl.ds(pl.multiple_of(device * 8, 8), 8), :]
+        first = (lax.broadcasted_iota(jnp.int32, (8, 128), 0) == 0) & (lane == 127)
+        drag_ref[0] = jnp.sum(jnp.where(first, total, 0.0))
+    return partial
+
+
+def round3_kernel(*refs):
+    tables, parts, (state_ref, y_ref) = refs[0:6], refs[6:8], refs[8:10]
+    sends, (lam, halo_lam, x_ref, normal_ref, sum_ref) = refs[10:12], refs[12:17]
+    base, ahead, motion, past = refs[17:]
+    near_kernel(
+        3, 2, *tables, *parts, *parts, state_ref, base, ahead, motion, past, sum_ref
+    )
+    far_kernel(
+        3, 2, y_ref, tables[4], base, motion, *parts, ahead, *sends, past,
+        lam, halo_lam, x_ref, normal_ref,
+    )
+
+
+def round2_kernel(*refs):
+    tables, lams, parts, (old_ref, state_ref, y_ref) = refs[0:6], refs[6:8], refs[8:10], refs[10:13]
+    normal_ref, sends, (x_ref, base_ref, ahead_ref, motion_ref, sum_ref) = (
+        refs[13], refs[14:16], refs[16:21],
+    )
+    base, ahead, motion, lam, halo_lam, sums = refs[21:]
+    near_kernel(2, 2, *tables, *lams, *parts, old_ref, base, ahead, motion, sums)
+    partial = far_kernel(
+        2, 2, y_ref, tables[4], base, motion, *parts, normal_ref, ahead, *sends,
+        lam, halo_lam, x_ref,
+    )
+    near_kernel(
+        1, 2, *tables, lam, halo_lam, *parts, sums, base_ref, ahead_ref, motion_ref, sum_ref
+    )
+    flow = state_ref[0, 1] * base_ref[0, 1, 0:28, :] + state_ref[0, 2] * base_ref[0, 2, 0:28, :]
+    total = jnp.sum(sum_ref[4, 24:32, :] - HALF * partial)
+    total = total + jnp.sum(flow * (HALF / state_ref[0, 0]))
+    put_value(x_ref, -total)
+
+
+def put_value(x_ref, value):
+    lane = lax.broadcasted_iota(jnp.int32, (8, 128), 1)
+    for e in range(GROUP):
+        part = x_ref[8 * e : 8 * e + 8, :]
+        x_ref[8 * e : 8 * e + 8, :] = jnp.where(lane == 127, value, part)
+
+
+def fold_kernel(y_ref, out_ref):
+    total = y_ref[0:8, :]
+    for e in range(1, GROUP):
+        total = total + y_ref[8 * e : 8 * e + 8, :]
+    out_ref[...] = jnp.broadcast_to(total[:, 127:128], (8, 128))
+
+
+def insert_kernel(x_ref, value_ref, out_ref):
+    lane = lax.broadcasted_iota(jnp.int32, (8, 128), 1)
+    for e in range(GROUP):
+        part = x_ref[8 * e : 8 * e + 8, :]
+        out_ref[8 * e : 8 * e + 8, :] = jnp.where(lane == 127, value_ref[...], part)
+
+
+def call(kernel, outs, args, values=0, scratch=(), smem=()):
+    vmem, scalar = pl.BlockSpec(memory_space=pltpu.VMEM), pl.BlockSpec(memory_space=pltpu.SMEM)
     return pl.pallas_call(
         kernel,
-        in_specs=[smem] * scalars + [vmem] * (len(args) - scalars),
-        out_specs=[vmem] * len(outs),
+        in_specs=[scalar if i in smem else vmem for i in range(len(args))],
+        out_specs=[vmem] * (len(outs) - values) + [scalar] * values,
         out_shape=[jax.ShapeDtypeStruct(shape, dtype) for shape, dtype in outs],
+        scratch_shapes=[pltpu.VMEM(shape, dtype) for shape, dtype in scratch],
         compiler_params=pltpu.CompilerParams(vmem_limit_bytes=32 * 1024 * 1024),
     )(*args)
 
@@ -593,7 +738,6 @@
 ):
     devices = lax.axis_size("dom")
     groups = [list(range(g, g + GROUP)) for g in range(0, devices, GROUP)]
-    strides = [list(range(d, devices, GROUP)) for d in range(GROUP)]
     back3, flip3, grad3, take2, spread3 = constants()
     tables = [back3, flip3, grad3, take2, spread3]
 
@@ -609,46 +753,57 @@
     halo = lax.ppermute(mine, "dom", pairs)
     both = [mine, halo]
 
-    my_sends, boxes = call(own_first_kernel, [sends_out, ((64, 128), F32)], (mine, flip3))
+    my_sends, boxes, rate = call(
+        own_first_kernel,
+        [sends_out, ((64, 128), F32), ((8, E), F32)],
+        [mine, flip3, drag_rate] + tables,
+        smem=(2,),
+    )
+    tables.append(rate)
     x, halo_sends = call(halo_first_kernel, [x_out, sends_out], (halo, flip3, boxes))
-    lams = both
-    sums = []
-    for section in (3, 2, 1, 0):
-        y = lax.all_to_all(x, "dom", 0, 0, tiled=True, axis_index_groups=groups)
-        blocks = 2 if section > 0 else 1
-        bases, faces = ((blocks, 3, 32, E), F32), ((blocks, 3, 24, E), F32)
-        args = [drag_rate] + tables + list(lams[:blocks]) + both[:blocks] + sums
-        if section > 0:
-            outs = [bases, faces, faces, sums_out]
-        else:
-            args += [saved_states, lam3, wind_speed, wind_angle]
-            outs = [bases, faces] + [((28, E), F32)] * 3
-        got = call(lambda *refs, s=section, n=blocks: near_kernel(s, n, *refs), outs, args, 1)
-        if section > 0:
-            base, ahead, motion = got[:3]
-            sums = list(got[3:])
-        else:
-            base, motion, depth_gradient, speed_gradient, angle_gradient = got
-
-        args = [y, spread3, base, motion] + both[:blocks]
-        if section > 0:
-            args += [ahead, my_sends, halo_sends]
-            outs = [mixed] * 2 + [x_out]
-        else:
-            outs = [((3, 28, E), F32)]
-        if section == 1:
-            args += [saved_states] + sums
-        got = call(lambda *refs, s=section, n=blocks: far_kernel(s, n, *refs), outs, args)
-        if section > 0:
-            lams, x = got[0:2], got[2]
-            if section == 3:
-                lam3 = lams[0]
-        else:
-            initial = got[0]
-    y, initial = lax.optimization_barrier((y, initial))
-    within = call(fold_kernel, [((devices // GROUP, 128), F32)], (y,))[0]
-    spread = lax.all_to_all(within, "dom", 0, 0, tiled=True, axis_index_groups=strides)
-    drag_gradient = jnp.sum(spread[:, 0]).reshape(1)
+    def exchange(x):
+        return lax.all_to_all(x, "dom", 0, 0, tiled=True, axis_index_groups=groups)
+
+    bases, faces = ((2, 3, 32, E), F32), ((2, 3, 24, E), F32)
+    far_outs, near_outs = [mixed, mixed, x_out], [bases, faces, faces, sums_out]
+    sends = [my_sends, halo_sends]
+
+    y = exchange(x)
+    lam3, _, x, normals, sums = got = call(
+        round3_kernel,
+        far_outs + [((2, 3, 8, E), F32), sums_out],
+        tables + both + [saved_states, y] + sends,
+        scratch=[bases, faces, faces, ((4, 24, E), F32)],
+    )
+    y = exchange(x)
+    x, base, ahead, motion, sums = call(
+        round2_kernel,
+        [x_out] + near_outs,
+        tables + list(got[0:2]) + both + [sums, saved_states, y, normals] + sends,
+        scratch=[bases, faces, faces, mixed, mixed, sums_out],
+    )
+    y = exchange(x)
+    within = call(fold_kernel, [((8, 128), F32)], (y,))[0]
+    within = lax.ppermute(within, "dom", spread_pairs(devices))
+    lam1, _, x = call(
+        lambda *refs: (far_kernel(1, 2, *refs), None)[1],
+        far_outs,
+        [y, spread3, base, motion] + both + [normals, ahead] + sends,
+    )
+    args = tables + [lam1, mine, sums, saved_states, lam3, wind_speed, wind_angle]
+    base, motion, depth_gradient, speed_gradient, angle_gradient = call(
+        lambda *refs: near_kernel(0, 1, *refs),
+        [((1, 3, 32, E), F32), ((1, 3, 24, E), F32)] + [((28, E), F32)] * 3,
+        args,
+    )
+    x, base = lax.optimization_barrier((x, base))
+    y = exchange(call(insert_kernel, [x_out], (x, within))[0])
+    initial, drag_gradient = call(
+        lambda *refs: (far_kernel(0, 1, *refs), None)[1],
+        [((3, 28, E), F32), ((1,), F32)],
+        [y, spread3, base, motion, mine, normals],
+        values=1,
+    )
     return (initial, depth_gradient, speed_gradient, angle_gradient, drag_gradient)
 
 

time: 99.1 us -> 87.9 us (0.89)
  blocking collectives: 18.2 us -> 69 us
  waiting for transfers between devices: 29.4 us -> 0.01 us
  starting transfers between devices: 35.4 us -> 7.73 us
  Pallas kernels: 11.5 us -> 8.12 us
    all_to_all x1 -> x4, blocking collectives: 18.2 us -> 69 us  [exchange(): return lax.all_to_all(x, 'dom', 0, 0, tiled=True, axis_index_groups=groups)]
    all_to_all x4 -> x0, starting transfers between devices: 34.7 us -> none  [local(): y = lax.all_to_all(x, 'dom', 0, 0, tiled=True, axis_index_groups=groups)]
    all_to_all x4 -> x0, waiting for transfers between devices: 29.4 us -> none  [local(): y = lax.all_to_all(x, 'dom', 0, 0, tiled=True, axis_index_groups=groups)]
    ppermute x0 -> x1, starting transfers between devices: none -> 7.05 us  [local(): within = lax.ppermute(within, 'dom', spread_pairs(devices))]
    pallas_call x12 -> x10, Pallas kernels: 11.5 us -> 8.12 us  [call(): pl.pallas_call(kernel, in_specs=[scalar if i in smem else vmem for i in r...]
  transfers between devices with their start and end apart: 5 -> 2, of which waited for: 4 -> 0; matrix products, arithmetic and copies ran while one was open for 0% -> 0% of each run, Pallas kernels for 4% -> 3%
where the time goes in v3:
time: 87.9 us; the launch traced here: 87.4 us
  blocking collectives  69 us (78%)
  Pallas kernels  8.12 us (9%)
  starting transfers between devices  7.73 us (9%)
  between operations  1.53 us (2%)
  local copies, waits for them, and re-layouts  1.05 us (1%)
    all_to_all x4, blocking collectives, exchange(): return lax.all_to_all(x, 'dom', 0, 0, tiled=True, axis_index_groups=groups)  69 us
    pallas_call x10, Pallas kernels, call(): pl.pallas_call(kernel, in_specs=[scalar if i in smem else vmem for i in r...  8.12 us
    ppermute x1, starting transfers between devices, local(): within = lax.ppermute(within, 'dom', spread_pairs(devices))  7.05 us
  transfers between devices with their start and end apart: 2, of which 0 were waited for; matrix products, arithmetic and copies ran while one was open for 0% of the time, Pallas kernels for 3%

profile of v3, /device:TPU:1, one launch (start us, length us, event | category | flops | bytes accessed | tf_op | source)
XLA Modules:
  0.0 87.4 jit_solution(18177801340555756442)
XLA Ops:
  0.7 1.0 %copy.20.q_ref.refs_8_.refs_11_.refs_9_ = f32[4,3,28,128]{3,2,1,0:T(8,128)S(1)} copy(f32[4,3,28,128]{3,0,2,1:T(4,128)} %param.15) | data formatting | bytes 344064 | tf_op args[0]
  1.7 0.0 copy-start
  1.7 0.0 copy-start.1
  1.8 0.0 copy-start.2
  1.8 0.0 copy-start.3
  1.8 0.0 copy-start.4
  1.8 0.7 collective-permute-start
  3.2 0.5 shard_map.183
  3.7 0.0 collective-permute-done.part_ref.refs_7_.refs_9_.refs_5_
  3.7 0.6 shard_map.184
  4.3 29.0 %all_to_all.44 = f32[32,8,128]{2,1,0:T(8,128)S(1)} all-to-all(f32[32,8,128]{2,1,0:T(8,128)S(1)} %bitcast.16), channel_id=1, replica_groups={{0,1,2,3,4,5,6,7,8,9,10,11,12,13,14,15,16,17,18,19,20,21,22,23,24,25,26..., dimensions={0} | all-to-all | bytes 262144 | tf_op jit(solution)/shard_map/all_to_all | solution.py:765
  33.3 1.5 %shard_map.185 = (f32[3,32,128]{2,1,0:T(8,128)S(1)}, f32[3,32,128]{2,1,0:T(8,128)S(1)}, f32[256,128]{1,0:T(8,128)S(1)}, f32[2,3,8,128]{3,2,1,0:T(8,128)S(1)}, f32[5,32,128]{2,1,0:T(8,128)S(1)}) custom-call(bf16[112,96]{1,0:T(8,128)(2,1)S(1)} %copy-done.1, bf16[24,96]{1,0:T(8,128)(2,1)S(1)} %copy-done.3, bf16[64,96]{1,0:T(8,128)(2,1)S(1)} %copy-done.2, ...), custom_call_target="tpu_custom_call" | custom-call | tf_op jit(solution)/shard_map/pallas_call | solution.py:717
  34.8 12.5 %all_to_all.45 = f32[32,8,128]{2,1,0:T(8,128)S(1)} all-to-all(f32[32,8,128]{2,1,0:T(8,128)S(1)} %bitcast.15), channel_id=1, replica_groups={{0,1,2,3,4,5,6,7,8,9,10,11,12,13,14,15,16,17,18,19,20,21,22,23,24,25,26..., dimensions={0} | all-to-all | bytes 262144 | tf_op jit(solution)/shard_map/all_to_all | solution.py:765
  47.3 1.9 %shard_map.186 = (f32[256,128]{1,0:T(8,128)S(1)}, f32[2,3,32,128]{3,2,1,0:T(8,128)S(1)}, f32[2,3,24,128]{3,2,1,0:T(8,128)S(1)}, f32[2,3,24,128]{3,2,1,0:T(8,128)S(1)}, f32[5,32,128]{2,1,0:T(8,128)S(1)}) custom-call(bf16[112,96]{1,0:T(8,128)(2,1)S(1)} %copy-done.1, bf16[24,96]{1,0:T(8,128)(2,1)S(1)} %copy-done.3, bf16[64,96]{1,0:T(8,128)(2,1)S(1)} %copy-done.2, ...), custom_call_target="tpu_custom_call" | custom-call | tf_op jit(solution)/shard_map/pallas_call | solution.py:717
  49.2 12.5 %all_to_all.46 = f32[32,8,128]{2,1,0:T(8,128)S(1)} all-to-all(f32[32,8,128]{2,1,0:T(8,128)S(1)} %bitcast.14), channel_id=1, replica_groups={{0,1,2,3,4,5,6,7,8,9,10,11,12,13,14,15,16,17,18,19,20,21,22,23,24,25,26..., dimensions={0} | all-to-all | bytes 262144 | tf_op jit(solution)/shard_map/all_to_all | solution.py:765
  61.8 0.1 shard_map.189
  61.9 7.1 %collective-permute-start.1 = (f32[8,128]{1,0:T(8,128)S(1)}, f32[8,128]{1,0:T(8,128)S(1)}, u32[]{:S(2)}, u32[]{:S(2)}) collective-permute-start(f32[8,128]{1,0:T(8,128)S(1)} %shard_map.189), channel_id=1, source_target_pairs={{0,0},{33,17},{66,18},{115,3},{132,4},{165,21},{198,22},{247,7},{2... | collective-permute-start | bytes 12296 | tf_op jit(solution)/shard_map/ppermute | solution.py:787
  68.9 0.0 copy-start.7
  68.9 0.0 copy-start.8
  69.0 1.2 %shard_map.187 = (f32[3,32,128]{2,1,0:T(8,128)S(1)}, f32[3,32,128]{2,1,0:T(8,128)}, f32[256,128]{1,0:T(8,128)S(1)}) custom-call(f32[256,128]{1,0:T(8,128)S(1)} %bitcast.9, bf16[56,80]{1,0:T(8,128)(2,1)S(1)} %copy-done, f32[2,3,32,128]{3,2,1,0:T(8,128)S(1)} %get-tuple-element.42.refs_2_, f32[2,3,24,128]{3,2,1,0:T(8,128)S(1)} %get-tuple-element.43.refs_3_, ...), custom_call_target="tpu_custom_call" | custom-call | tf_op jit(solution)/shard_map/pallas_call | solution.py:717
  70.1 1.2 %shard_map.188 = (f32[1,3,32,128]{3,2,1,0:T(8,128)S(1)}, f32[1,3,24,128]{3,2,1,0:T(8,128)S(1)}, f32[28,128]{1,0:T(8,128)}, f32[28,128]{1,0:T(8,128)}, f32[28,128]{1,0:T(8,128)}) custom-call(bf16[112,96]{1,0:T(8,128)(2,1)S(1)} %copy-done.1, bf16[24,96]{1,0:T(8,128)(2,1)S(1)} %copy-done.3, bf16[64,96]{1,0:T(8,128)(2,1)S(1)} %copy-done.2, ...), custom_call_target="tpu_custom_call" | custom-call | tf_op jit(solution)/shard_map/pallas_call | solution.py:717
  71.4 0.0 collective-permute-done.1.value_ref
  71.4 14.9 %all_to_all.47 = f32[32,8,128]{2,1,0:T(8,128)S(1)} all-to-all(f32[32,8,128]{2,1,0:T(8,128)S(1)} %bitcast.11), channel_id=1, replica_groups={{0,1,2,3,4,5,6,7,8,9,10,11,12,13,14,15,16,17,18,19,20,21,22,23,24,25,26..., dimensions={0} | all-to-all | bytes 262144 | tf_op jit(solution)/shard_map/all_to_all | solution.py:765
  86.3 1.1 %shard_map.191 = (f32[3,28,128]{2,1,0:T(8,128)}, f32[1]{0:T(128)}) custom-call(f32[256,128]{1,0:T(8,128)S(1)} %bitcast.12, bf16[56,80]{1,0:T(8,128)(2,1)S(1)} %copy-done, f32[1,3,32,128]{3,2,1,0:T(8,128)S(1)} %get-tuple-element.50.refs_2_, f32[1,3,24,128]{3,2,1,0:T(8,128)S(1)} %get-tuple-element.51.refs_3_, ...), custom_call_target="tpu_custom_call" | custom-call | tf_op jit(solution)/shard_map/pallas_call | solution.py:717
  (21 shorter events, 0.1 us)
Async XLA Ops:
  0.6 1.0 %copy-start.9 = (s32[8,16]{1,0:T(8,128)S(1)}, s32[8,16]{1,0:T(8,128)}, u32[]{:S(2)}) copy-start(s32[8,16]{1,0:T(8,128)} %face_ref.1) | copy-start | bytes 1540
  0.6 1.0 %copy-start.11 = (s32[3,128]{1,0:T(4,128)S(1)}, s32[3,128]{1,0:T(4,128)}, u32[]{:S(2)}) copy-start(s32[3,128]{1,0:T(4,128)} %tag_ref.1) | copy-start | bytes 4612
  0.7 1.0 %copy-start.12 = (s32[3,128]{1,0:T(4,128)S(1)}, s32[3,128]{1,0:T(4,128)}, u32[]{:S(2)}) copy-start(s32[3,128]{1,0:T(4,128)} %link_ref.1) | copy-start | bytes 4612
  0.7 1.0 %copy-start.10 = (f32[4,128]{1,0:T(4,128)S(1)}, f32[4,128]{1,0:T(4,128)}, u32[]{:S(2)}) copy-start(f32[4,128]{1,0:T(4,128)} %metric_ref.1) | copy-start | bytes 6148
  0.7 1.0 %copy-start.6 = (f32[28,128]{1,0:T(8,128)S(1)}, f32[28,128]{1,0:T(8,128)}, u32[]{:S(2)}) copy-start(f32[28,128]{1,0:T(8,128)} %depth_ref.1) | copy-start | bytes 43012
  0.7 1.0 %copy-start.5 = (f32[3,28,128]{2,1,0:T(8,128)S(1)}, f32[3,28,128]{2,1,0:T(8,128)}, u32[]{:S(2)}) copy-start(f32[3,28,128]{2,1,0:T(8,128)} %lam_ref.1) | copy-start | bytes 129028
  1.7 1.4 %copy-start = (bf16[56,80]{1,0:T(8,128)(2,1)S(1)}, bf16[56,80]{1,0:T(8,128)(2,1)}, u32[]{:S(2)}) copy-start(bf16[56,80]{1,0:T(8,128)(2,1)} %constant.14.clone.refs_4_.refs_1_) | copy-start | bytes 26884
  1.7 1.4 %copy-start.1 = (bf16[112,96]{1,0:T(8,128)(2,1)S(1)}, bf16[112,96]{1,0:T(8,128)(2,1)}, u32[]{:S(2)}) copy-start(bf16[112,96]{1,0:T(8,128)(2,1)} %constant.10.clone.refs_0_) | copy-start | bytes 64516
  1.8 1.4 %copy-start.2 = (bf16[64,96]{1,0:T(8,128)(2,1)S(1)}, bf16[64,96]{1,0:T(8,128)(2,1)}, u32[]{:S(2)}) copy-start(bf16[64,96]{1,0:T(8,128)(2,1)} %constant.12.clone.refs_2_) | copy-start | bytes 36868
  1.8 1.4 %copy-start.3 = (bf16[24,96]{1,0:T(8,128)(2,1)S(1)}, bf16[24,96]{1,0:T(8,128)(2,1)}, u32[]{:S(2)}) copy-start(bf16[24,96]{1,0:T(8,128)(2,1)} %constant.11.clone.flip3.refs_1_) | copy-start | bytes 13828
  1.8 1.4 %copy-start.4 = (bf16[24,64]{1,0:T(8,128)(2,1)S(1)}, bf16[24,64]{1,0:T(8,128)(2,1)}, u32[]{:S(2)}) copy-start(bf16[24,64]{1,0:T(8,128)(2,1)} %constant.13.clone.refs_3_) | copy-start | bytes 9220
  1.8 1.9 %collective-permute-start = (f32[14,32,128]{2,1,0:T(8,128)S(1)}, f32[14,32,128]{2,1,0:T(8,128)S(1)}, u32[]{:S(2)}, u32[]{:S(2)}) collective-permute-start(f32[14,32,128]{2,1,0:T(8,128)S(1)} %shard_map.182.part_ref.refs_6_.refs_8_.refs_4_.refs_7_), channel_id=1, source_target_pairs={{0,0},{1,1},{2,2},{3,3},{4,4},{5,5},{6,6},{7,7},{8,8},{9,9},{10,10... | collective-permute-start | bytes 688136 | tf_op jit(solution)/shard_map/ppermute | solution.py:753
  61.9 9.5 %collective-permute-start.1 = (f32[8,128]{1,0:T(8,128)S(1)}, f32[8,128]{1,0:T(8,128)S(1)}, u32[]{:S(2)}, u32[]{:S(2)}) collective-permute-start(f32[8,128]{1,0:T(8,128)S(1)} %shard_map.189), channel_id=1, source_target_pairs={{0,0},{33,17},{66,18},{115,3},{132,4},{165,21},{198,22},{247,7},{2... | collective-permute-start | bytes 12296 | tf_op jit(solution)/shard_map/ppermute | solution.py:787
  68.9 1.2 %copy-start.7 = (f32[28,128]{1,0:T(8,128)S(1)}, f32[28,128]{1,0:T(8,128)}, u32[]{:S(2)}) copy-start(f32[28,128]{1,0:T(8,128)} %refs_11_.2) | copy-start | bytes 43012
  68.9 1.2 %copy-start.8 = (f32[28,128]{1,0:T(8,128)S(1)}, f32[28,128]{1,0:T(8,128)}, u32[]{:S(2)}) copy-start(f32[28,128]{1,0:T(8,128)} %refs_12_.1) | copy-start | bytes 43012

commit v4 on v3

--- a/solution.py
+++ b/solution.py
@@ -23,7 +23,8 @@
 DIRS = 8
 SLOTS = 16
 E = 128
-DEPTH, MISC = 12, 13
+DEPTH, MISC = 12, 24
+PACKED = MISC + 28 * 13 + 4
 F32 = jnp.float32
 BF16 = jnp.bfloat16
 
@@ -127,17 +128,24 @@
     return found
 
 
-def spread_steps():
-    return [(q // 4, q % 4, 1 if q % 4 in (1, 2) else 0) for q in range(STRIDE)]
+def spread_place(dx, dy):
+    half, odd = dx // 2, dx % 2
+    if dy == 0:
+        return 6 + half + ROW * odd
+    if dy == 2:
+        return 4 + half + ROW * (1 - odd)
+    return dx + (ROW if dy == 1 else 0)
 
 
 def spread_pairs(devices):
     pairs = []
     for group in range(devices // GROUP):
-        for q, (dx, dy, row) in enumerate(spread_steps()):
-            other = (group // 4 + dx) % 4 * 4 + (group % 4 + dy) % 4
-            other_row = 0 if dy == 0 else 1 - row
-            pairs.append((other * GROUP + other_row * ROW + q, group * GROUP + row * ROW + q))
+        for dx in range(4):
+            for dy in range(4):
+                other = (group // 4 + dx) % 4 * 4 + (group % 4 + dy) % 4
+                place = spread_place(dx, dy)
+                source = place if dy == 0 else (place + ROW) % GROUP
+                pairs.append((other * GROUP + source, group * GROUP + place))
     return pairs
 
 
@@ -287,26 +295,30 @@
 
 
 def pack_kernel(q_ref, lam_ref, depth_ref, metric_ref, tag_ref, link_ref, face_ref, out_ref):
-    ones = jnp.ones((4, E), F32)
+    out_ref[0:MISC, :] = jnp.zeros((MISC, E), F32)
+    out_ref[0:4, :] = metric_ref[...]
+    out_ref[4:7, :] = tag_ref[...].astype(F32)
+    out_ref[8:11, :] = link_ref[...].astype(F32)
+    out_ref[16:24, 0:16] = face_ref[...].astype(F32)
     for c in range(3):
-        out_ref[c, 0:28, :] = lam_ref[c]
-        out_ref[c, 28:32, :] = jnp.zeros((4, E), F32)
+        out_ref[MISC + 28 * c : MISC + 28 * c + 28, :] = lam_ref[c]
     for s in range(3):
         for c in range(3):
-            out_ref[3 * (3 - s) + c, 0:28, :] = q_ref[s + 1, c]
-            out_ref[3 * (3 - s) + c, 28:32, :] = ones
-    out_ref[DEPTH, 0:28, :] = depth_ref[...]
-    out_ref[DEPTH, 28:32, :] = ones
-    out_ref[MISC] = jnp.zeros((32, E), F32)
-    out_ref[MISC, 0:4, :] = metric_ref[...]
-    out_ref[MISC, 4:7, :] = tag_ref[...].astype(F32)
-    out_ref[MISC, 8:11, :] = link_ref[...].astype(F32)
-    out_ref[MISC, 16:24, 0:16] = face_ref[...].astype(F32)
+            first = MISC + 28 * (3 * (3 - s) + c)
+            out_ref[first : first + 28, :] = q_ref[s + 1, c]
+    out_ref[MISC + 28 * DEPTH : MISC + 28 * DEPTH + 28, :] = depth_ref[...]
+    out_ref[PACKED - 4 : PACKED, :] = jnp.zeros((4, E), F32)
+
+
+def field(part_ref, i, fill):
+    first = MISC + 28 * i
+    row = lax.broadcasted_iota(jnp.int32, (32, E), 0)
+    return jnp.where(row < 28, part_ref[first : first + 32, :], fill)
 
 
 def first_boxes(part_ref, flip3, block):
-    misc = part_ref[MISC]
-    weights = jnp.concatenate([HALF * part_ref[c] for c in range(3)], axis=1)
+    misc = part_ref[0:MISC, :]
+    weights = jnp.concatenate([HALF * field(part_ref, c, 0.0) for c in range(3)], axis=1)
     flipped = times3(flip3[...], weights)
     split = [
         [flipped[8 * f : 8 * f + 8, 128 * c : 128 * c + 128] for f in range(3)] for c in range(3)
@@ -353,13 +365,16 @@
     drag_rate = rate_ref[...][0:1]
     pad = jnp.ones((4, E), F32)
 
-    lam = [[lams[b][c] for c in range(3)] for b in range(blocks)]
+    if section == 3:
+        lam = [[field(lams[b], c, 0.0) for c in range(3)] for b in range(blocks)]
+    else:
+        lam = [[lams[b][c] for c in range(3)] for b in range(blocks)]
     w = [[scale * x for x in lam[b]] for b in range(blocks)]
     if section == 0:
         q = [[jnp.concatenate([state_ref[0, c], pad], axis=0) for c in range(3)]]
     else:
-        q = [[parts[b][3 * (4 - section) + c] for c in range(3)] for b in range(blocks)]
-    z = [parts[b][DEPTH] for b in range(blocks)]
+        q = [[field(parts[b], 3 * (4 - section) + c, 1.0) for c in range(3)] for b in range(blocks)]
+    z = [field(parts[b], DEPTH, 1.0) for b in range(blocks)]
     pulled = times3(back3, jnp.concatenate([x for b in range(blocks) for x in w[b]], axis=1))
     slopes = times3(grad3, jnp.concatenate(z, axis=1))
     fields = jnp.concatenate([x for b in range(blocks) for x in q[b] + [z[b]]], axis=1)
@@ -368,7 +383,7 @@
 
     if section == 3:
         fields = [jnp.concatenate([state_ref[0, c], pad], axis=0) for c in range(3)]
-        fields += [parts[0][9 + c] for c in range(3)]
+        fields += [field(parts[0], 9 + c, 1.0) for c in range(3)]
         hi, lo = halves(jnp.concatenate(fields, axis=1))
         past = dot(take2, jnp.concatenate([hi, lo], axis=0).astype(BF16))
         for i in range(2):
@@ -378,7 +393,7 @@
 
     face_sums, volumes, opens = [], [], []
     for b in range(blocks):
-        misc = parts[b][MISC]
+        misc = parts[b][0:MISC, :]
         (rx, ry, sx, sy), normals = geometry(misc)
         part = lambda r0, r1, c: pulled[r0:r1, 384 * b + 128 * c : 384 * b + 128 * c + 128]
         h = q[b][0]
@@ -494,7 +509,7 @@
         sum_ref[4, 0:24, :] = opens
         sum_ref[4, 24:32, :] = fold
     else:
-        rx, ry, sx, sy = geometry(parts[0][MISC])[0]
+        rx, ry, sx, sy = geometry(parts[0][0:4, :])[0]
         w1, w2, g1, g2 = news
         pair = GRAVITY * jnp.concatenate([rx * g1 + ry * g2, sx * g1 + sy * g2], axis=1)
         pulled = times3(back3, pair)
@@ -564,7 +579,7 @@
         pool = jnp.concatenate(pools, axis=0)
         tall = pool.shape[0]
         pool = jnp.concatenate(halves(pool), axis=0).astype(BF16)
-        links = parts[b][MISC, 8:11].astype(jnp.int32)
+        links = parts[b][8:11, :].astype(jnp.int32)
         match = [
             jnp.where(rows == far_index(links[f : f + 1]), 1.0, 0.0).astype(BF16) for f in range(3)
         ]
@@ -651,10 +666,12 @@
         for g in range(STRIDE):
             dx = jnp.bitwise_and(g // 4 - lax.shift_right_logical(group, 2), 3)
             dy = jnp.bitwise_and(g % 4 - jnp.bitwise_and(group, 3), 3)
-            device = 4 * dx + dy + jnp.where((dy == 1) | (dy == 2), ROW, 0)
+            device = jnp.int32(0)
+            for x in range(4):
+                for y in range(4):
+                    device = jnp.where((dx == x) & (dy == y), spread_place(x, y), device)
             total = total + y_ref[pl.ds(pl.multiple_of(device * 8, 8), 8), :]
-        first = (lax.broadcasted_iota(jnp.int32, (8, 128), 0) == 0) & (lane == 127)
-        drag_ref[0] = jnp.sum(jnp.where(first, total, 0.0))
+        drag_ref[0] = jnp.sum(jnp.where(lane == 127, total, 0.0))
     return partial
 
 
@@ -686,9 +703,10 @@
         1, 2, *tables, lam, halo_lam, *parts, sums, base_ref, ahead_ref, motion_ref, sum_ref
     )
     flow = state_ref[0, 1] * base_ref[0, 1, 0:28, :] + state_ref[0, 2] * base_ref[0, 2, 0:28, :]
-    total = jnp.sum(sum_ref[4, 24:32, :] - HALF * partial)
-    total = total + jnp.sum(flow * (HALF / state_ref[0, 0]))
-    put_value(x_ref, -total)
+    flow = jnp.concatenate([flow * (HALF / state_ref[0, 0]), jnp.zeros((4, E), F32)], axis=0)
+    flow = flow[0:8] + flow[8:16] + flow[16:24] + flow[24:32]
+    total = sum_ref[4, 24:32, :] - HALF * partial + flow
+    put_value(x_ref, -jnp.sum(total, axis=1, keepdims=True))
 
 
 def put_value(x_ref, value):
@@ -749,7 +767,7 @@
             pairs += [(i, i + ROW), (i + ROW, i)]
     pack_args = (saved_states, adjoint_final, bathymetry)
     pack_args += (metrics, face_tag, face_link, send_faces)
-    mine = call(pack_kernel, [((14, 32, E), F32)], pack_args)[0]
+    mine = call(pack_kernel, [((PACKED, E), F32)], pack_args)[0]
     halo = lax.ppermute(mine, "dom", pairs)
     both = [mine, halo]
 

time: 87.9 us -> 86.9 us (0.989)
  blocking collectives: 69 us -> 68.1 us
where the time goes in v4:
time: 86.9 us; the launch traced here: 86.5 us
  blocking collectives  68.1 us (78%)
  Pallas kernels  8.09 us (9%)
  starting transfers between devices  7.71 us (9%)
  between operations  1.52 us (2%)
  local copies, waits for them, and re-layouts  1.05 us (1%)
    all_to_all x4, blocking collectives, exchange(): return lax.all_to_all(x, 'dom', 0, 0, tiled=True, axis_index_groups=groups)  68.1 us
    pallas_call x10, Pallas kernels, call(): pl.pallas_call(kernel, in_specs=[scalar if i in smem else vmem for i in r...  8.09 us
    ppermute x1, starting transfers between devices, local(): within = lax.ppermute(within, 'dom', spread_pairs(devices))  7.04 us
  transfers between devices with their start and end apart: 2, of which 0 were waited for; matrix products, arithmetic and copies ran while one was open for 0% of the time, Pallas kernels for 3%

profile of v4, /device:TPU:1, one launch (start us, length us, event | category | flops | bytes accessed | tf_op | source)
XLA Modules:
  0.0 86.5 jit_solution(12189687978929305503)
XLA Ops:
  0.7 1.0 %copy.20.q_ref.refs_8_.refs_11_.refs_9_ = f32[4,3,28,128]{3,2,1,0:T(8,128)S(1)} copy(f32[4,3,28,128]{3,0,2,1:T(4,128)} %param.15) | data formatting | bytes 344064 | tf_op args[0]
  1.7 0.0 copy-start
  1.7 0.0 copy-start.1
  1.8 0.0 copy-start.2
  1.8 0.0 copy-start.3
  1.8 0.0 copy-start.4
  1.8 0.7 collective-permute-start
  3.2 0.5 shard_map.183
  3.7 0.0 collective-permute-done.part_ref.refs_7_.refs_9_.refs_5_
  3.7 0.6 shard_map.184
  4.3 28.4 %all_to_all.44 = f32[32,8,128]{2,1,0:T(8,128)S(1)} all-to-all(f32[32,8,128]{2,1,0:T(8,128)S(1)} %bitcast.16), channel_id=1, replica_groups={{0,1,2,3,4,5,6,7,8,9,10,11,12,13,14,15,16,17,18,19,20,21,22,23,24,25,26..., dimensions={0} | all-to-all | bytes 262144 | tf_op jit(solution)/shard_map/all_to_all | solution.py:783
  32.7 1.5 %shard_map.185 = (f32[3,32,128]{2,1,0:T(8,128)S(1)}, f32[3,32,128]{2,1,0:T(8,128)S(1)}, f32[256,128]{1,0:T(8,128)S(1)}, f32[2,3,8,128]{3,2,1,0:T(8,128)S(1)}, f32[5,32,128]{2,1,0:T(8,128)S(1)}) custom-call(bf16[112,96]{1,0:T(8,128)(2,1)S(1)} %copy-done.1, bf16[24,96]{1,0:T(8,128)(2,1)S(1)} %copy-done.3, bf16[64,96]{1,0:T(8,128)(2,1)S(1)} %copy-done.2, ...), custom_call_target="tpu_custom_call" | custom-call | tf_op jit(solution)/shard_map/pallas_call | solution.py:735
  34.2 12.5 %all_to_all.45 = f32[32,8,128]{2,1,0:T(8,128)S(1)} all-to-all(f32[32,8,128]{2,1,0:T(8,128)S(1)} %bitcast.15), channel_id=1, replica_groups={{0,1,2,3,4,5,6,7,8,9,10,11,12,13,14,15,16,17,18,19,20,21,22,23,24,25,26..., dimensions={0} | all-to-all | bytes 262144 | tf_op jit(solution)/shard_map/all_to_all | solution.py:783
  46.7 1.9 %shard_map.186 = (f32[256,128]{1,0:T(8,128)S(1)}, f32[2,3,32,128]{3,2,1,0:T(8,128)S(1)}, f32[2,3,24,128]{3,2,1,0:T(8,128)S(1)}, f32[2,3,24,128]{3,2,1,0:T(8,128)S(1)}, f32[5,32,128]{2,1,0:T(8,128)S(1)}) custom-call(bf16[112,96]{1,0:T(8,128)(2,1)S(1)} %copy-done.1, bf16[24,96]{1,0:T(8,128)(2,1)S(1)} %copy-done.3, bf16[64,96]{1,0:T(8,128)(2,1)S(1)} %copy-done.2, ...), custom_call_target="tpu_custom_call" | custom-call | tf_op jit(solution)/shard_map/pallas_call | solution.py:735
  48.6 12.5 %all_to_all.46 = f32[32,8,128]{2,1,0:T(8,128)S(1)} all-to-all(f32[32,8,128]{2,1,0:T(8,128)S(1)} %bitcast.14), channel_id=1, replica_groups={{0,1,2,3,4,5,6,7,8,9,10,11,12,13,14,15,16,17,18,19,20,21,22,23,24,25,26..., dimensions={0} | all-to-all | bytes 262144 | tf_op jit(solution)/shard_map/all_to_all | solution.py:783
  61.1 0.1 shard_map.189
  61.2 7.0 %collective-permute-start.1 = (f32[8,128]{1,0:T(8,128)S(1)}, f32[8,128]{1,0:T(8,128)S(1)}, u32[]{:S(2)}, u32[]{:S(2)}) collective-permute-start(f32[8,128]{1,0:T(8,128)S(1)} %shard_map.189), channel_id=1, source_target_pairs={{6,6},{32,16},{68,20},{112,0},{150,22},{161,17},{212,4},{241,1},{2... | collective-permute-start | bytes 12296 | tf_op jit(solution)/shard_map/ppermute | solution.py:805
  68.3 0.0 copy-start.6
  68.3 0.0 copy-start.7
  68.3 1.2 %shard_map.187 = (f32[3,32,128]{2,1,0:T(8,128)S(1)}, f32[3,32,128]{2,1,0:T(8,128)}, f32[256,128]{1,0:T(8,128)S(1)}) custom-call(f32[256,128]{1,0:T(8,128)S(1)} %bitcast.9, bf16[56,80]{1,0:T(8,128)(2,1)S(1)} %copy-done, f32[2,3,32,128]{3,2,1,0:T(8,128)S(1)} %get-tuple-element.42.refs_2_, f32[2,3,24,128]{3,2,1,0:T(8,128)S(1)} %get-tuple-element.43.refs_3_, ...), custom_call_target="tpu_custom_call" | custom-call | tf_op jit(solution)/shard_map/pallas_call | solution.py:735
  69.5 1.2 %shard_map.188 = (f32[1,3,32,128]{3,2,1,0:T(8,128)S(1)}, f32[1,3,24,128]{3,2,1,0:T(8,128)S(1)}, f32[28,128]{1,0:T(8,128)}, f32[28,128]{1,0:T(8,128)}, f32[28,128]{1,0:T(8,128)}) custom-call(bf16[112,96]{1,0:T(8,128)(2,1)S(1)} %copy-done.1, bf16[24,96]{1,0:T(8,128)(2,1)S(1)} %copy-done.3, bf16[64,96]{1,0:T(8,128)(2,1)S(1)} %copy-done.2, ...), custom_call_target="tpu_custom_call" | custom-call | tf_op jit(solution)/shard_map/pallas_call | solution.py:735
  70.7 0.0 collective-permute-done.1.value_ref
  70.7 14.7 %all_to_all.47 = f32[32,8,128]{2,1,0:T(8,128)S(1)} all-to-all(f32[32,8,128]{2,1,0:T(8,128)S(1)} %bitcast.13), channel_id=1, replica_groups={{0,1,2,3,4,5,6,7,8,9,10,11,12,13,14,15,16,17,18,19,20,21,22,23,24,25,26..., dimensions={0} | all-to-all | bytes 262144 | tf_op jit(solution)/shard_map/all_to_all | solution.py:783
  85.4 1.1 %shard_map.191 = (f32[3,28,128]{2,1,0:T(8,128)}, f32[1]{0:T(128)}) custom-call(f32[256,128]{1,0:T(8,128)S(1)} %bitcast.12, bf16[56,80]{1,0:T(8,128)(2,1)S(1)} %copy-done, f32[1,3,32,128]{3,2,1,0:T(8,128)S(1)} %get-tuple-element.50.refs_2_, f32[1,3,24,128]{3,2,1,0:T(8,128)S(1)} %get-tuple-element.51.refs_3_, ...), custom_call_target="tpu_custom_call" | custom-call | tf_op jit(solution)/shard_map/pallas_call | solution.py:735
  (21 shorter events, 0.1 us)
Async XLA Ops:
  0.6 1.0 %copy-start.9 = (s32[8,16]{1,0:T(8,128)S(1)}, s32[8,16]{1,0:T(8,128)}, u32[]{:S(2)}) copy-start(s32[8,16]{1,0:T(8,128)} %face_ref.1) | copy-start | bytes 1540
  0.6 1.0 %copy-start.11 = (s32[3,128]{1,0:T(4,128)S(1)}, s32[3,128]{1,0:T(4,128)}, u32[]{:S(2)}) copy-start(s32[3,128]{1,0:T(4,128)} %tag_ref.1) | copy-start | bytes 4612
  0.7 1.0 %copy-start.12 = (s32[3,128]{1,0:T(4,128)S(1)}, s32[3,128]{1,0:T(4,128)}, u32[]{:S(2)}) copy-start(s32[3,128]{1,0:T(4,128)} %link_ref.1) | copy-start | bytes 4612
  0.7 1.0 %copy-start.10 = (f32[4,128]{1,0:T(4,128)S(1)}, f32[4,128]{1,0:T(4,128)}, u32[]{:S(2)}) copy-start(f32[4,128]{1,0:T(4,128)} %metric_ref.1) | copy-start | bytes 6148
  0.7 1.0 %copy-start.8 = (f32[28,128]{1,0:T(8,128)S(1)}, f32[28,128]{1,0:T(8,128)}, u32[]{:S(2)}) copy-start(f32[28,128]{1,0:T(8,128)} %depth_ref.1) | copy-start | bytes 43012
  0.7 1.0 %copy-start.5 = (f32[3,28,128]{2,1,0:T(8,128)S(1)}, f32[3,28,128]{2,1,0:T(8,128)}, u32[]{:S(2)}) copy-start(f32[3,28,128]{2,1,0:T(8,128)} %lam_ref.1) | copy-start | bytes 129028
  1.7 1.4 %copy-start = (bf16[56,80]{1,0:T(8,128)(2,1)S(1)}, bf16[56,80]{1,0:T(8,128)(2,1)}, u32[]{:S(2)}) copy-start(bf16[56,80]{1,0:T(8,128)(2,1)} %constant.14.clone.refs_4_.refs_1_) | copy-start | bytes 26884
  1.7 1.4 %copy-start.1 = (bf16[112,96]{1,0:T(8,128)(2,1)S(1)}, bf16[112,96]{1,0:T(8,128)(2,1)}, u32[]{:S(2)}) copy-start(bf16[112,96]{1,0:T(8,128)(2,1)} %constant.10.clone.refs_0_) | copy-start | bytes 64516
  1.8 1.4 %copy-start.2 = (bf16[64,96]{1,0:T(8,128)(2,1)S(1)}, bf16[64,96]{1,0:T(8,128)(2,1)}, u32[]{:S(2)}) copy-start(bf16[64,96]{1,0:T(8,128)(2,1)} %constant.12.clone.refs_2_) | copy-start | bytes 36868
  1.8 1.4 %copy-start.3 = (bf16[24,96]{1,0:T(8,128)(2,1)S(1)}, bf16[24,96]{1,0:T(8,128)(2,1)}, u32[]{:S(2)}) copy-start(bf16[24,96]{1,0:T(8,128)(2,1)} %constant.11.clone.flip3.refs_1_) | copy-start | bytes 13828
  1.8 1.4 %copy-start.4 = (bf16[24,64]{1,0:T(8,128)(2,1)S(1)}, bf16[24,64]{1,0:T(8,128)(2,1)}, u32[]{:S(2)}) copy-start(bf16[24,64]{1,0:T(8,128)(2,1)} %constant.13.clone.refs_3_) | copy-start | bytes 9220
  1.8 1.9 %collective-permute-start = (f32[392,128]{1,0:T(8,128)S(1)}, f32[392,128]{1,0:T(8,128)S(1)}, u32[]{:S(2)}, u32[]{:S(2)}) collective-permute-start(f32[392,128]{1,0:T(8,128)S(1)} %shard_map.182.part_ref.refs_6_.refs_8_.refs_4_.refs_7_), channel_id=1, source_target_pairs={{0,0},{1,1},{2,2},{3,3},{4,4},{5,5},{6,6},{7,7},{8,8},{9,9},{10,10... | collective-permute-start | bytes 602120 | tf_op jit(solution)/shard_map/ppermute | solution.py:771
  61.2 9.5 %collective-permute-start.1 = (f32[8,128]{1,0:T(8,128)S(1)}, f32[8,128]{1,0:T(8,128)S(1)}, u32[]{:S(2)}, u32[]{:S(2)}) collective-permute-start(f32[8,128]{1,0:T(8,128)S(1)} %shard_map.189), channel_id=1, source_target_pairs={{6,6},{32,16},{68,20},{112,0},{150,22},{161,17},{212,4},{241,1},{2... | collective-permute-start | bytes 12296 | tf_op jit(solution)/shard_map/ppermute | solution.py:805
  68.3 1.2 %copy-start.6 = (f32[28,128]{1,0:T(8,128)S(1)}, f32[28,128]{1,0:T(8,128)}, u32[]{:S(2)}) copy-start(f32[28,128]{1,0:T(8,128)} %refs_11_.2) | copy-start | bytes 43012
  68.3 1.2 %copy-start.7 = (f32[28,128]{1,0:T(8,128)S(1)}, f32[28,128]{1,0:T(8,128)}, u32[]{:S(2)}) copy-start(f32[28,128]{1,0:T(8,128)} %refs_12_.1) | copy-start | bytes 43012

commit v5 on v4

--- a/solution.py
+++ b/solution.py
@@ -328,7 +328,9 @@
 
 
 def own_first_kernel(part_ref, flip3, drag_ref, *refs):
-    sends_ref, boxes_ref, rate_ref = refs[-3:]
+    sends_ref, boxes_ref, rate_ref, near_ref, far_ref = refs[-5:]
+    links = part_ref[8:11, :].astype(jnp.int32)
+    near_ref[...], far_ref[...] = near_match(links), far_match(links)
     rate_ref[...] = jnp.full((8, E), drag_ref[0], F32)
     sends_ref[...], boxes_ref[...] = first_boxes(part_ref, flip3, 0)
 
@@ -336,6 +338,19 @@
 def halo_first_kernel(part_ref, flip3, boxes_ref, x_ref, sends_ref):
     sends_ref[...], boxes = first_boxes(part_ref, flip3, 1)
     send(x_ref, neighbours(), [boxes_ref[...], boxes])
+
+
+def near_match(links):
+    rows = lax.broadcasted_iota(jnp.int32, (3 * E, E), 0)
+    return jnp.concatenate(
+        [jnp.where(rows == links[f : f + 1], 1.0, 0.0).astype(BF16) for f in range(3)], axis=1
+    )
+
+
+def far_match(links):
+    rows = lax.broadcasted_iota(jnp.int32, (128, E), 0)
+    found = [rows == far_index(links[f : f + 1]) for f in range(3)]
+    return jnp.concatenate([jnp.where(x, 1.0, 0.0).astype(BF16) for x in found], axis=1)
 
 
 def near_kernel(section, blocks, *refs):
@@ -344,6 +359,7 @@
     rate_ref = refs.pop(0)
     lams = [refs.pop(0) for _ in range(blocks)]
     parts = [refs.pop(0) for _ in range(blocks)]
+    matches = [refs.pop(0) for _ in range(blocks)]
     old_ref = refs.pop(0) if section < 3 else None
     if section == 3:
         state_ref = refs.pop(0)
@@ -426,14 +442,12 @@
         flipped = [[part(88 + 8 * f, 96 + 8 * f, c) for f in range(3)] for c in range(3)]
         hi, lo = halves(traces(flipped, normals))
         pool = jnp.concatenate([hi, lo], axis=0).astype(BF16)
-        links = misc[8:11].astype(jnp.int32)
-        rows = lax.broadcasted_iota(jnp.int32, (3 * E, E), 0)
+        found = dot(pool, matches[b][...])
+        found = found[0:24] + found[24:48]
         opened = []
         sums = [[], [], []]
         for f in range(3):
-            match = jnp.where(rows == links[f : f + 1], 1.0, 0.0).astype(BF16)
-            got = dot(pool, match)
-            got = got[0:24] + got[24:48]
+            got = found[:, 128 * f : 128 * f + 128]
             value = lambda i: at_faces[
                 8 * f : 8 * f + 8, 512 * b + 128 * i : 512 * b + 128 * i + 128
             ]
@@ -526,6 +540,7 @@
     refs = list(refs)
     y_ref, spread3_ref, base_ref, motion_ref = [refs.pop(0) for _ in range(4)]
     parts = [refs.pop(0) for _ in range(blocks)]
+    matches = [refs.pop(0) for _ in range(blocks)]
     if section < 3:
         normal_ref = refs.pop(0)
     if section > 0:
@@ -565,7 +580,6 @@
     if section == 2:
         stacks.append(jnp.transpose(jnp.concatenate(extras, axis=0)))
     left = lax.broadcasted_iota(jnp.int32, (32, 128), 1) < 64
-    rows = lax.broadcasted_iota(jnp.int32, (128, E), 0)
     row = lax.broadcasted_iota(jnp.int32, (8, E), 0)
     face_sums, factors = [], []
     for b in range(blocks):
@@ -579,11 +593,7 @@
         pool = jnp.concatenate(pools, axis=0)
         tall = pool.shape[0]
         pool = jnp.concatenate(halves(pool), axis=0).astype(BF16)
-        links = parts[b][8:11, :].astype(jnp.int32)
-        match = [
-            jnp.where(rows == far_index(links[f : f + 1]), 1.0, 0.0).astype(BF16) for f in range(3)
-        ]
-        got = dot(pool, jnp.concatenate(match, axis=1))
+        got = dot(pool, matches[b][...])
         got = got[0:tall] + got[tall:]
         sums, scales = [[], [], []], [[], [], []]
         for f in range(3):
@@ -676,31 +686,41 @@
 
 
 def round3_kernel(*refs):
-    tables, parts, (state_ref, y_ref) = refs[0:6], refs[6:8], refs[8:10]
-    sends, (lam, halo_lam, x_ref, normal_ref, sum_ref) = refs[10:12], refs[12:17]
-    base, ahead, motion, past = refs[17:]
+    refs = list(refs)
+    take = lambda n: [refs.pop(0) for _ in range(n)]
+    tables, parts, (state_ref, y_ref), sends = take(6), take(2), take(2), take(2)
+    my_near, my_far = take(2)
+    lams, (x_ref, normal_ref, sum_ref, halo_near, halo_far) = take(2), take(5)
+    base, ahead, motion, past = refs
+    links = parts[1][8:11, :].astype(jnp.int32)
+    halo_near[...], halo_far[...] = near_match(links), far_match(links)
     near_kernel(
-        3, 2, *tables, *parts, *parts, state_ref, base, ahead, motion, past, sum_ref
+        3, 2, *tables, *parts, *parts, my_near, halo_near, state_ref,
+        base, ahead, motion, past, sum_ref,
     )
     far_kernel(
-        3, 2, y_ref, tables[4], base, motion, *parts, ahead, *sends, past,
-        lam, halo_lam, x_ref, normal_ref,
+        3, 2, y_ref, tables[4], base, motion, *parts, my_far, halo_far, ahead, *sends, past,
+        *lams, x_ref, normal_ref,
     )
 
 
 def round2_kernel(*refs):
-    tables, lams, parts, (old_ref, state_ref, y_ref) = refs[0:6], refs[6:8], refs[8:10], refs[10:13]
-    normal_ref, sends, (x_ref, base_ref, ahead_ref, motion_ref, sum_ref) = (
-        refs[13], refs[14:16], refs[16:21],
-    )
-    base, ahead, motion, lam, halo_lam, sums = refs[21:]
-    near_kernel(2, 2, *tables, *lams, *parts, old_ref, base, ahead, motion, sums)
+    refs = list(refs)
+    take = lambda n: [refs.pop(0) for _ in range(n)]
+    tables, lams, parts, (old_ref, state_ref, y_ref) = take(6), take(2), take(2), take(3)
+    (normal_ref,), sends, near_matches, far_matches = take(1), take(2), take(2), take(2)
+    x_ref, base_ref, ahead_ref, motion_ref, sum_ref = take(5)
+    base, ahead, motion, lam, halo_lam, sums = refs
+    near_kernel(
+        2, 2, *tables, *lams, *parts, *near_matches, old_ref, base, ahead, motion, sums
+    )
     partial = far_kernel(
-        2, 2, y_ref, tables[4], base, motion, *parts, normal_ref, ahead, *sends,
+        2, 2, y_ref, tables[4], base, motion, *parts, *far_matches, normal_ref, ahead, *sends,
         lam, halo_lam, x_ref,
     )
     near_kernel(
-        1, 2, *tables, lam, halo_lam, *parts, sums, base_ref, ahead_ref, motion_ref, sum_ref
+        1, 2, *tables, lam, halo_lam, *parts, *near_matches, sums,
+        base_ref, ahead_ref, motion_ref, sum_ref,
     )
     flow = state_ref[0, 1] * base_ref[0, 1, 0:28, :] + state_ref[0, 2] * base_ref[0, 2, 0:28, :]
     flow = jnp.concatenate([flow * (HALF / state_ref[0, 0]), jnp.zeros((4, E), F32)], axis=0)
@@ -771,9 +791,10 @@
     halo = lax.ppermute(mine, "dom", pairs)
     both = [mine, halo]
 
-    my_sends, boxes, rate = call(
+    near_out, far_out = ((3 * E, 3 * E), BF16), ((128, 3 * E), BF16)
+    my_sends, boxes, rate, my_near, my_far = call(
         own_first_kernel,
-        [sends_out, ((64, 128), F32), ((8, E), F32)],
+        [sends_out, ((64, 128), F32), ((8, E), F32), near_out, far_out],
         [mine, flip3, drag_rate] + tables,
         smem=(2,),
     )
@@ -787,17 +808,18 @@
     sends = [my_sends, halo_sends]
 
     y = exchange(x)
-    lam3, _, x, normals, sums = got = call(
+    lam3, _, x, normals, sums, halo_near, halo_far = got = call(
         round3_kernel,
-        far_outs + [((2, 3, 8, E), F32), sums_out],
-        tables + both + [saved_states, y] + sends,
+        far_outs + [((2, 3, 8, E), F32), sums_out, near_out, far_out],
+        tables + both + [saved_states, y] + sends + [my_near, my_far],
         scratch=[bases, faces, faces, ((4, 24, E), F32)],
     )
     y = exchange(x)
     x, base, ahead, motion, sums = call(
         round2_kernel,
         [x_out] + near_outs,
-        tables + list(got[0:2]) + both + [sums, saved_states, y, normals] + sends,
+        tables + list(got[0:2]) + both + [sums, saved_states, y, normals] + sends
+        + [my_near, halo_near, my_far, halo_far],
         scratch=[bases, faces, faces, mixed, mixed, sums_out],
     )
     y = exchange(x)
@@ -806,9 +828,9 @@
     lam1, _, x = call(
         lambda *refs: (far_kernel(1, 2, *refs), None)[1],
         far_outs,
-        [y, spread3, base, motion] + both + [normals, ahead] + sends,
-    )
-    args = tables + [lam1, mine, sums, saved_states, lam3, wind_speed, wind_angle]
+        [y, spread3, base, motion] + both + [my_far, halo_far, normals, ahead] + sends,
+    )
+    args = tables + [lam1, mine, my_near, sums, saved_states, lam3, wind_speed, wind_angle]
     base, motion, depth_gradient, speed_gradient, angle_gradient = call(
         lambda *refs: near_kernel(0, 1, *refs),
         [((1, 3, 32, E), F32), ((1, 3, 24, E), F32)] + [((28, E), F32)] * 3,
@@ -819,7 +841,7 @@
     initial, drag_gradient = call(
         lambda *refs: (far_kernel(0, 1, *refs), None)[1],
         [((3, 28, E), F32), ((1,), F32)],
-        [y, spread3, base, motion, mine, normals],
+        [y, spread3, base, motion, mine, my_far, normals],
         values=1,
     )
     return (initial, depth_gradient, speed_gradient, angle_gradient, drag_gradient)

time: 86.9 us -> 86.6 us (level)
  no operation moved by 1% of the time
where the time goes in v5:
time: 86.6 us; the launch traced here: 86.3 us
  blocking collectives  68.1 us (79%)
  Pallas kernels  7.91 us (9%)
  starting transfers between devices  7.7 us (9%)
  between operations  1.52 us (2%)
  local copies, waits for them, and re-layouts  1.05 us (1%)
    all_to_all x4, blocking collectives, exchange(): return lax.all_to_all(x, 'dom', 0, 0, tiled=True, axis_index_groups=groups)  68.1 us
    pallas_call x10, Pallas kernels, call(): pl.pallas_call(kernel, in_specs=[scalar if i in smem else vmem for i in r...  7.91 us
    ppermute x1, starting transfers between devices, local(): within = lax.ppermute(within, 'dom', spread_pairs(devices))  7.03 us
  transfers between devices with their start and end apart: 2, of which 0 were waited for; matrix products, arithmetic and copies ran while one was open for 0% of the time, Pallas kernels for 3%

profile of v5, /device:TPU:1, one launch (start us, length us, event | category | flops | bytes accessed | tf_op | source)
XLA Modules:
  0.0 86.3 jit_solution(18110241579274053496)
XLA Ops:
  0.7 1.0 %copy.20.q_ref.refs_8_.refs_11_.refs_10_ = f32[4,3,28,128]{3,2,1,0:T(8,128)S(1)} copy(f32[4,3,28,128]{3,0,2,1:T(4,128)} %param.15) | data formatting | bytes 344064 | tf_op args[0]
  1.7 0.0 copy-start
  1.7 0.0 copy-start.1
  1.8 0.0 copy-start.2
  1.8 0.0 copy-start.3
  1.8 0.0 copy-start.4
  1.8 0.7 collective-permute-start
  3.2 0.6 shard_map.183
  3.8 0.0 collective-permute-done.part_ref.refs_7_.refs_9_.refs_5_
  3.8 0.6 shard_map.184
  4.4 28.3 %all_to_all.44 = f32[32,8,128]{2,1,0:T(8,128)S(1)} all-to-all(f32[32,8,128]{2,1,0:T(8,128)S(1)} %bitcast.16), channel_id=1, replica_groups={{0,1,2,3,4,5,6,7,8,9,10,11,12,13,14,15,16,17,18,19,20,21,22,23,24,25,26..., dimensions={0} | all-to-all | bytes 262144 | tf_op jit(solution)/shard_map/all_to_all | solution.py:804
  32.7 1.4 %shard_map.185 = (f32[3,32,128]{2,1,0:T(8,128)S(1)}, f32[3,32,128]{2,1,0:T(8,128)S(1)}, f32[256,128]{1,0:T(8,128)S(1)}, f32[2,3,8,128]{3,2,1,0:T(8,128)S(1)}, f3...) custom-call(bf16[112,96]{1,0:T(8,128)(2,1)S(1)} %copy-done.1, ...), custom_call_target="tpu_custom_call" | custom-call | tf_op jit(solution)/shard_map/pallas_call | solution.py:755
  34.1 12.5 %all_to_all.45 = f32[32,8,128]{2,1,0:T(8,128)S(1)} all-to-all(f32[32,8,128]{2,1,0:T(8,128)S(1)} %bitcast.15), channel_id=1, replica_groups={{0,1,2,3,4,5,6,7,8,9,10,11,12,13,14,15,16,17,18,19,20,21,22,23,24,25,26..., dimensions={0} | all-to-all | bytes 262144 | tf_op jit(solution)/shard_map/all_to_all | solution.py:804
  46.7 1.7 %shard_map.186 = (f32[256,128]{1,0:T(8,128)S(1)}, f32[2,3,32,128]{3,2,1,0:T(8,128)S(1)}, f32[2,3,24,128]{3,2,1,0:T(8,128)S(1)}, f32[2,3,24,128]{3,2,1,0:T(8,128)S(1)}, f32[5,32,128]{2,1,0:T(8,128)S(1)}) custom-call(bf16[112,96]{1,0:T(8,128)(2,1)S(1)} %copy-done.1, bf16[24,96]{1,0:T(8,128)(2,1)S(1)} %copy-done.3, bf16[64,96]{1,0:T(8,128)(2,1)S(1)} %copy-done.2, ...), custom_call_target="tpu_custom_call" | custom-call | tf_op jit(solution)/shard_map/pallas_call | solution.py:755
  48.4 12.5 %all_to_all.46 = f32[32,8,128]{2,1,0:T(8,128)S(1)} all-to-all(f32[32,8,128]{2,1,0:T(8,128)S(1)} %bitcast.14), channel_id=1, replica_groups={{0,1,2,3,4,5,6,7,8,9,10,11,12,13,14,15,16,17,18,19,20,21,22,23,24,25,26..., dimensions={0} | all-to-all | bytes 262144 | tf_op jit(solution)/shard_map/all_to_all | solution.py:804
  60.9 0.1 shard_map.189
  61.0 7.0 %collective-permute-start.1 = (f32[8,128]{1,0:T(8,128)S(1)}, f32[8,128]{1,0:T(8,128)S(1)}, u32[]{:S(2)}, u32[]{:S(2)}) collective-permute-start(f32[8,128]{1,0:T(8,128)S(1)} %shard_map.189), channel_id=1, source_target_pairs={{6,6},{32,16},{68,20},{112,0},{150,22},{161,17},{212,4},{241,1},{2... | collective-permute-start | bytes 12296 | tf_op jit(solution)/shard_map/ppermute | solution.py:827
  68.0 0.0 copy-start.6
  68.1 0.0 copy-start.7
  68.1 1.2 %shard_map.187 = (f32[3,32,128]{2,1,0:T(8,128)S(1)}, f32[3,32,128]{2,1,0:T(8,128)}, f32[256,128]{1,0:T(8,128)S(1)}) custom-call(f32[256,128]{1,0:T(8,128)S(1)} %bitcast.9, bf16[56,80]{1,0:T(8,128)(2,1)S(1)} %copy-done, f32[2,3,32,128]{3,2,1,0:T(8,128)S(1)} %get-tuple-element.50.refs_2_, f32[2,3,24,128]{3,2,1,0:T(8,128)S(1)} %get-tuple-element.51.refs_3_, ...), custom_call_target="tpu_custom_call" | custom-call | tf_op jit(solution)/shard_map/pallas_call | solution.py:755
  69.3 1.2 %shard_map.188 = (f32[1,3,32,128]{3,2,1,0:T(8,128)S(1)}, f32[1,3,24,128]{3,2,1,0:T(8,128)S(1)}, f32[28,128]{1,0:T(8,128)}, f32[28,128]{1,0:T(8,128)}, f32[28,128]{1,0:T(8,128)}) custom-call(bf16[112,96]{1,0:T(8,128)(2,1)S(1)} %copy-done.1, bf16[24,96]{1,0:T(8,128)(2,1)S(1)} %copy-done.3, bf16[64,96]{1,0:T(8,128)(2,1)S(1)} %copy-done.2, ...), custom_call_target="tpu_custom_call" | custom-call | tf_op jit(solution)/shard_map/pallas_call | solution.py:755
  70.4 0.0 collective-permute-done.1.value_ref
  70.4 14.7 %all_to_all.47 = f32[32,8,128]{2,1,0:T(8,128)S(1)} all-to-all(f32[32,8,128]{2,1,0:T(8,128)S(1)} %bitcast.11), channel_id=1, replica_groups={{0,1,2,3,4,5,6,7,8,9,10,11,12,13,14,15,16,17,18,19,20,21,22,23,24,25,26..., dimensions={0} | all-to-all | bytes 262144 | tf_op jit(solution)/shard_map/all_to_all | solution.py:804
  85.1 1.1 %shard_map.191 = (f32[3,28,128]{2,1,0:T(8,128)}, f32[1]{0:T(128)}) custom-call(f32[256,128]{1,0:T(8,128)S(1)} %bitcast.12, bf16[56,80]{1,0:T(8,128)(2,1)S(1)} %copy-done, f32[1,3,32,128]{3,2,1,0:T(8,128)S(1)} %get-tuple-element.58.refs_2_, f32[1,3,24,128]{3,2,1,0:T(8,128)S(1)} %get-tuple-element.59.refs_3_, ...), custom_call_target="tpu_custom_call" | custom-call | tf_op jit(solution)/shard_map/pallas_call | solution.py:755
  (21 shorter events, 0.1 us)
Async XLA Ops:
  0.6 1.0 %copy-start.9 = (s32[8,16]{1,0:T(8,128)S(1)}, s32[8,16]{1,0:T(8,128)}, u32[]{:S(2)}) copy-start(s32[8,16]{1,0:T(8,128)} %face_ref.1) | copy-start | bytes 1540
  0.6 1.0 %copy-start.11 = (s32[3,128]{1,0:T(4,128)S(1)}, s32[3,128]{1,0:T(4,128)}, u32[]{:S(2)}) copy-start(s32[3,128]{1,0:T(4,128)} %tag_ref.1) | copy-start | bytes 4612
  0.7 1.0 %copy-start.12 = (s32[3,128]{1,0:T(4,128)S(1)}, s32[3,128]{1,0:T(4,128)}, u32[]{:S(2)}) copy-start(s32[3,128]{1,0:T(4,128)} %link_ref.1) | copy-start | bytes 4612
  0.7 1.0 %copy-start.10 = (f32[4,128]{1,0:T(4,128)S(1)}, f32[4,128]{1,0:T(4,128)}, u32[]{:S(2)}) copy-start(f32[4,128]{1,0:T(4,128)} %metric_ref.1) | copy-start | bytes 6148
  0.7 1.0 %copy-start.8 = (f32[28,128]{1,0:T(8,128)S(1)}, f32[28,128]{1,0:T(8,128)}, u32[]{:S(2)}) copy-start(f32[28,128]{1,0:T(8,128)} %depth_ref.1) | copy-start | bytes 43012
  0.7 1.0 %copy-start.5 = (f32[3,28,128]{2,1,0:T(8,128)S(1)}, f32[3,28,128]{2,1,0:T(8,128)}, u32[]{:S(2)}) copy-start(f32[3,28,128]{2,1,0:T(8,128)} %lam_ref.1) | copy-start | bytes 129028
  1.7 1.4 %copy-start = (bf16[56,80]{1,0:T(8,128)(2,1)S(1)}, bf16[56,80]{1,0:T(8,128)(2,1)}, u32[]{:S(2)}) copy-start(bf16[56,80]{1,0:T(8,128)(2,1)} %constant.14.clone.refs_4_.refs_1_) | copy-start | bytes 26884
  1.7 1.4 %copy-start.1 = (bf16[112,96]{1,0:T(8,128)(2,1)S(1)}, bf16[112,96]{1,0:T(8,128)(2,1)}, u32[]{:S(2)}) copy-start(bf16[112,96]{1,0:T(8,128)(2,1)} %constant.10.clone.refs_0_) | copy-start | bytes 64516
  1.8 1.4 %copy-start.2 = (bf16[64,96]{1,0:T(8,128)(2,1)S(1)}, bf16[64,96]{1,0:T(8,128)(2,1)}, u32[]{:S(2)}) copy-start(bf16[64,96]{1,0:T(8,128)(2,1)} %constant.12.clone.refs_2_) | copy-start | bytes 36868
  1.8 1.4 %copy-start.3 = (bf16[24,96]{1,0:T(8,128)(2,1)S(1)}, bf16[24,96]{1,0:T(8,128)(2,1)}, u32[]{:S(2)}) copy-start(bf16[24,96]{1,0:T(8,128)(2,1)} %constant.11.clone.flip3.refs_1_) | copy-start | bytes 13828
  1.8 1.4 %copy-start.4 = (bf16[24,64]{1,0:T(8,128)(2,1)S(1)}, bf16[24,64]{1,0:T(8,128)(2,1)}, u32[]{:S(2)}) copy-start(bf16[24,64]{1,0:T(8,128)(2,1)} %constant.13.clone.refs_3_) | copy-start | bytes 9220
  1.8 2.0 %collective-permute-start = (f32[392,128]{1,0:T(8,128)S(1)}, f32[392,128]{1,0:T(8,128)S(1)}, u32[]{:S(2)}, u32[]{:S(2)}) collective-permute-start(f32[392,128]{1,0:T(8,128)S(1)} %shard_map.182.part_ref.refs_6_.refs_8_.refs_4_.refs_7_), channel_id=1, source_target_pairs={{0,0},{1,1},{2,2},{3,3},{4,4},{5,5},{6,6},{7,7},{8,8},{9,9},{10,10... | collective-permute-start | bytes 602120 | tf_op jit(solution)/shard_map/ppermute | solution.py:791
  61.0 9.4 %collective-permute-start.1 = (f32[8,128]{1,0:T(8,128)S(1)}, f32[8,128]{1,0:T(8,128)S(1)}, u32[]{:S(2)}, u32[]{:S(2)}) collective-permute-start(f32[8,128]{1,0:T(8,128)S(1)} %shard_map.189), channel_id=1, source_target_pairs={{6,6},{32,16},{68,20},{112,0},{150,22},{161,17},{212,4},{241,1},{2... | collective-permute-start | bytes 12296 | tf_op jit(solution)/shard_map/ppermute | solution.py:827
  68.0 1.2 %copy-start.6 = (f32[28,128]{1,0:T(8,128)S(1)}, f32[28,128]{1,0:T(8,128)}, u32[]{:S(2)}) copy-start(f32[28,128]{1,0:T(8,128)} %refs_12_.1) | copy-start | bytes 43012
  68.1 1.2 %copy-start.7 = (f32[28,128]{1,0:T(8,128)S(1)}, f32[28,128]{1,0:T(8,128)}, u32[]{:S(2)}) copy-start(f32[28,128]{1,0:T(8,128)} %refs_13_.1) | copy-start | bytes 43012

commit v6 on v5

--- a/solution.py
+++ b/solution.py
@@ -245,11 +245,12 @@
     return jnp.concatenate(rows, axis=0)
 
 
-def far_index(link):
+def far_index(link, width=8):
     v = link - 3 * E
     j = lax.shift_right_arithmetic(v, 4)
     c = jnp.bitwise_and(v, 15)
-    row = lax.shift_right_arithmetic(c, 3) * 64 + j * 8 + jnp.bitwise_and(c, 7)
+    part = lax.shift_right_arithmetic(c, width.bit_length() - 1)
+    row = part * (DIRS * width) + j * width + jnp.bitwise_and(c, width - 1)
     return jnp.where(v >= 0, row, -1)
 
 
@@ -266,6 +267,28 @@
     return out[0:64] + pltpu.roll(out[64:128], 32, 1)
 
 
+def quarter_rows(sends, v):
+    hi, lo = halves(v)
+    rest = jnp.zeros((8, v.shape[1]), F32)
+    stack = jnp.concatenate([hi, rest, lo, rest, jnp.zeros((64, v.shape[1]), F32)], axis=0)
+    out = dot_nt(sends, stack.astype(BF16))
+    lane = lax.broadcasted_iota(jnp.int32, (128, 128), 1)
+    out = jnp.where(lane < 32, out + pltpu.roll(out, 96, 1), 0.0)
+    total = out[0:32]
+    for h in range(1, 4):
+        total = total + pltpu.roll(out[32 * h : 32 * h + 32], 32 * h, 1)
+    return total
+
+
+def send_quarters(x_ref, near_by, boxes):
+    x_ref[...] = jnp.zeros(x_ref.shape, F32)
+    for b in range(2):
+        for j in range(DIRS):
+            device, second, exists = near_by[DIRS * b + j]
+            box = jnp.where(exists & (second == 0), boxes[b][4 * j : 4 * j + 4], 0.0)
+            x_ref[device] = x_ref[device] + box
+
+
 def send(x_ref, near_by, boxes):
     x_ref[...] = jnp.zeros(x_ref.shape, F32)
     for b in range(2):
@@ -276,16 +299,17 @@
             x_ref[rows, :] = x_ref[rows, :] + box
 
 
-def send_matrix(misc):
+def send_matrix(misc, width=8):
     faces = misc[16:24]
     lane = lax.broadcasted_iota(jnp.int32, (8, 128), 1)
-    low = jnp.where(lane < 8, faces, 0.0)
-    high = jnp.where((lane >= 8) & (lane < 16), faces, 0.0)
-    both = low + pltpu.roll(high, 56, 1)
+    both = jnp.zeros((8, 128), F32)
+    for h in range(SLOTS // width):
+        part = jnp.where((lane >= width * h) & (lane < width * h + width), faces, 0.0)
+        both = both + (pltpu.roll(part, (DIRS - 1) * width * h, 1) if h else part)
     row = lax.broadcasted_iota(jnp.int32, (8, 128), 0)
     lined = jnp.zeros((8, 128), F32)
     for j in range(DIRS):
-        moved = both if j == 0 else pltpu.roll(both, 8 * j, 1)
+        moved = both if j == 0 else pltpu.roll(both, width * j, 1)
         lined = lined + jnp.where(row == j, moved, 0.0)
     line = jnp.sum(lined, axis=0, keepdims=True)
     column = jnp.transpose(jnp.broadcast_to(line, (128, 128)))
@@ -328,9 +352,10 @@
 
 
 def own_first_kernel(part_ref, flip3, drag_ref, *refs):
-    sends_ref, boxes_ref, rate_ref, near_ref, far_ref = refs[-5:]
+    sends_ref, boxes_ref, rate_ref, near_ref, far_ref, last_ref = refs[-6:]
     links = part_ref[8:11, :].astype(jnp.int32)
     near_ref[...], far_ref[...] = near_match(links), far_match(links)
+    last_ref[...] = far_match(links, 4)
     rate_ref[...] = jnp.full((8, E), drag_ref[0], F32)
     sends_ref[...], boxes_ref[...] = first_boxes(part_ref, flip3, 0)
 
@@ -347,9 +372,9 @@
     )
 
 
-def far_match(links):
+def far_match(links, width=8):
     rows = lax.broadcasted_iota(jnp.int32, (128, E), 0)
-    found = [rows == far_index(links[f : f + 1]) for f in range(3)]
+    found = [rows == far_index(links[f : f + 1], width) for f in range(3)]
     return jnp.concatenate([jnp.where(x, 1.0, 0.0).astype(BF16) for x in found], axis=1)
 
 
@@ -545,6 +570,7 @@
         normal_ref = refs.pop(0)
     if section > 0:
         ahead_ref = refs.pop(0)
+    if section > 1:
         sends_refs = [refs.pop(0), refs.pop(0)]
     if section == 3:
         past_ref = refs.pop(0)
@@ -566,6 +592,9 @@
         for j in range(DIRS):
             if b < blocks:
                 device, second, exists = near_by[DIRS * b + j]
+                if section == 0:
+                    boxes.append(jnp.where(exists, y_ref[device], 0.0))
+                    continue
                 raw = y_ref[pl.ds(pl.multiple_of(device * 8, 8), 8), :]
                 turned = pltpu.roll(raw, 64, 1)
                 if section == 2:
@@ -574,8 +603,10 @@
                 else:
                     box = jnp.where(second == 1, turned, raw)
                 boxes.append(jnp.where(exists, box, 0.0))
-            else:
+            elif section > 0:
                 boxes.append(jnp.zeros((8, 128), F32))
+    if section == 0:
+        boxes.append(jnp.zeros((96, 128), F32))
     stacks = [jnp.transpose(jnp.concatenate(boxes, axis=0))]
     if section == 2:
         stacks.append(jnp.transpose(jnp.concatenate(extras, axis=0)))
@@ -586,7 +617,12 @@
         pools = []
         for turned in stacks:
             low, high = turned[0:32], turned[32:64]
-            if b == 0:
+            if section == 0:
+                pool = low
+                for h in range(1, 4):
+                    pool = pool + pltpu.roll(turned[32 * h : 32 * h + 32], 32 * h, 1)
+                pools.append(pool)
+            elif b == 0:
                 pools.append(jnp.where(left, low, pltpu.roll(high, 64, 1)))
             else:
                 pools.append(jnp.where(left, pltpu.roll(low, 64, 1), high))
@@ -659,6 +695,8 @@
                     slot_rows(sends_refs[0][...], trace, 0)
                     + slot_rows(sends_refs[0][...], jnp.concatenate(extra, axis=0), 1)
                 )
+            elif section == 1:
+                slots.append(quarter_rows(send_matrix(parts[b][0:MISC, :], 4), trace))
             else:
                 slots.append(slot_rows(sends_refs[b][...], trace, b))
             if section == 2:
@@ -669,10 +707,10 @@
             for c in range(3):
                 lam_refs[b][c] = lam[c][0:28]
     if section > 0:
-        send(x_ref, near_by, slots)
+        (send_quarters if section == 1 else send)(x_ref, near_by, slots)
     else:
         group = lax.shift_right_logical(lax.axis_index("dom"), 5)
-        total = jnp.zeros((8, 128), F32)
+        total = jnp.zeros((4, 128), F32)
         for g in range(STRIDE):
             dx = jnp.bitwise_and(g // 4 - lax.shift_right_logical(group, 2), 3)
             dy = jnp.bitwise_and(g % 4 - jnp.bitwise_and(group, 3), 3)
@@ -680,8 +718,8 @@
             for x in range(4):
                 for y in range(4):
                     device = jnp.where((dx == x) & (dy == y), spread_place(x, y), device)
-            total = total + y_ref[pl.ds(pl.multiple_of(device * 8, 8), 8), :]
-        drag_ref[0] = jnp.sum(jnp.where(lane == 127, total, 0.0))
+            total = total + y_ref[device]
+        drag_ref[0] = jnp.sum(jnp.where(lane[0:4] == 127, total, 0.0))
     return partial
 
 
@@ -744,10 +782,10 @@
 
 
 def insert_kernel(x_ref, value_ref, out_ref):
-    lane = lax.broadcasted_iota(jnp.int32, (8, 128), 1)
+    lane = lax.broadcasted_iota(jnp.int32, (4, 128), 1)
+    value = value_ref[0:4, :] + value_ref[4:8, :]
     for e in range(GROUP):
-        part = x_ref[8 * e : 8 * e + 8, :]
-        out_ref[8 * e : 8 * e + 8, :] = jnp.where(lane == 127, value_ref[...], part)
+        out_ref[e] = jnp.where(lane == 127, value, x_ref[e])
 
 
 def call(kernel, outs, args, values=0, scratch=(), smem=()):
@@ -792,9 +830,9 @@
     both = [mine, halo]
 
     near_out, far_out = ((3 * E, 3 * E), BF16), ((128, 3 * E), BF16)
-    my_sends, boxes, rate, my_near, my_far = call(
+    my_sends, boxes, rate, my_near, my_far, my_last = call(
         own_first_kernel,
-        [sends_out, ((64, 128), F32), ((8, E), F32), near_out, far_out],
+        [sends_out, ((64, 128), F32), ((8, E), F32), near_out, far_out, far_out],
         [mine, flip3, drag_rate] + tables,
         smem=(2,),
     )
@@ -825,10 +863,11 @@
     y = exchange(x)
     within = call(fold_kernel, [((8, 128), F32)], (y,))[0]
     within = lax.ppermute(within, "dom", spread_pairs(devices))
+    last_out = ((GROUP, 4, 128), F32)
     lam1, _, x = call(
         lambda *refs: (far_kernel(1, 2, *refs), None)[1],
-        far_outs,
-        [y, spread3, base, motion] + both + [my_far, halo_far, normals, ahead] + sends,
+        [mixed, mixed, last_out],
+        [y, spread3, base, motion] + both + [my_far, halo_far, normals, ahead],
     )
     args = tables + [lam1, mine, my_near, sums, saved_states, lam3, wind_speed, wind_angle]
     base, motion, depth_gradient, speed_gradient, angle_gradient = call(
@@ -837,11 +876,11 @@
         args,
     )
     x, base = lax.optimization_barrier((x, base))
-    y = exchange(call(insert_kernel, [x_out], (x, within))[0])
+    y = exchange(call(insert_kernel, [last_out], (x, within))[0])
     initial, drag_gradient = call(
         lambda *refs: (far_kernel(0, 1, *refs), None)[1],
         [((3, 28, E), F32), ((1,), F32)],
-        [y, spread3, base, motion, mine, my_far, normals],
+        [y, spread3, base, motion, mine, my_last, normals],
         values=1,
     )
     return (initial, depth_gradient, speed_gradient, angle_gradient, drag_gradient)

time: 86.6 us -> 86 us (level)
  blocking collectives: 68.1 us -> 67.1 us
    all_to_all x4, blocking collectives: 68.1 us -> 67.1 us  [exchange(): return lax.all_to_all(x, 'dom', 0, 0, tiled=True, axis_index_groups=groups)]
  transfers between devices with their start and end apart: 2 -> 2, of which waited for: 0 -> 0; matrix products, arithmetic and copies ran while one was open for 0% -> 0% of each run, Pallas kernels for 3% -> 4%
where the time goes in v6:
time: 86 us; the launch traced here: 85.6 us
  blocking collectives  67.1 us (78%)
  Pallas kernels  8.25 us (10%)
  starting transfers between devices  7.7 us (9%)
  between operations  1.52 us (2%)
  local copies, waits for them, and re-layouts  1.05 us (1%)
    all_to_all x4, blocking collectives, exchange(): return lax.all_to_all(x, 'dom', 0, 0, tiled=True, axis_index_groups=groups)  67.1 us
    pallas_call x10, Pallas kernels, call(): pl.pallas_call(kernel, in_specs=[scalar if i in smem else vmem for i in r...  8.25 us
    ppermute x1, starting transfers between devices, local(): within = lax.ppermute(within, 'dom', spread_pairs(devices))  7.03 us
  transfers between devices with their start and end apart: 2, of which 0 were waited for; matrix products, arithmetic and copies ran while one was open for 0% of the time, Pallas kernels for 4%

profile of v6, /device:TPU:1, one launch (start us, length us, event | category | flops | bytes accessed | tf_op | source)
XLA Modules:
  0.0 85.6 jit_solution(13456223903025661697)
XLA Ops:
  0.7 1.0 %copy.20.q_ref.refs_8_.refs_11_.refs_10_ = f32[4,3,28,128]{3,2,1,0:T(8,128)S(1)} copy(f32[4,3,28,128]{3,0,2,1:T(4,128)} %param.15) | data formatting | bytes 344064 | tf_op args[0]
  1.7 0.0 copy-start
  1.7 0.0 copy-start.1
  1.8 0.0 copy-start.2
  1.8 0.0 copy-start.3
  1.8 0.0 copy-start.4
  1.8 0.7 collective-permute-start
  3.2 0.6 shard_map.183
  3.9 0.0 collective-permute-done.part_ref.refs_7_.refs_9_.refs_5_
  3.9 0.6 shard_map.184
  4.4 28.3 %all_to_all.38 = f32[32,8,128]{2,1,0:T(8,128)S(1)} all-to-all(f32[32,8,128]{2,1,0:T(8,128)S(1)} %bitcast.12), channel_id=1, replica_groups={{0,1,2,3,4,5,6,7,8,9,10,11,12,13,14,15,16,17,18,19,20,21,22,23,24,25,26..., dimensions={0} | all-to-all | bytes 262144 | tf_op jit(solution)/shard_map/all_to_all | solution.py:842
  32.7 1.4 %shard_map.185 = (f32[3,32,128]{2,1,0:T(8,128)S(1)}, f32[3,32,128]{2,1,0:T(8,128)S(1)}, f32[256,128]{1,0:T(8,128)S(1)}, f32[2,3,8,128]{3,2,1,0:T(8,128)S(1)}, f3...) custom-call(bf16[112,96]{1,0:T(8,128)(2,1)S(1)} %copy-done.1, ...), custom_call_target="tpu_custom_call" | custom-call | tf_op jit(solution)/shard_map/pallas_call | solution.py:793
  34.1 12.5 %all_to_all.39 = f32[32,8,128]{2,1,0:T(8,128)S(1)} all-to-all(f32[32,8,128]{2,1,0:T(8,128)S(1)} %bitcast.11), channel_id=1, replica_groups={{0,1,2,3,4,5,6,7,8,9,10,11,12,13,14,15,16,17,18,19,20,21,22,23,24,25,26..., dimensions={0} | all-to-all | bytes 262144 | tf_op jit(solution)/shard_map/all_to_all | solution.py:842
  46.7 1.7 %shard_map.186 = (f32[256,128]{1,0:T(8,128)S(1)}, f32[2,3,32,128]{3,2,1,0:T(8,128)S(1)}, f32[2,3,24,128]{3,2,1,0:T(8,128)S(1)}, f32[2,3,24,128]{3,2,1,0:T(8,128)S(1)}, f32[5,32,128]{2,1,0:T(8,128)S(1)}) custom-call(bf16[112,96]{1,0:T(8,128)(2,1)S(1)} %copy-done.1, bf16[24,96]{1,0:T(8,128)(2,1)S(1)} %copy-done.3, bf16[64,96]{1,0:T(8,128)(2,1)S(1)} %copy-done.2, ...), custom_call_target="tpu_custom_call" | custom-call | tf_op jit(solution)/shard_map/pallas_call | solution.py:793
  48.4 12.5 %all_to_all.40 = f32[32,8,128]{2,1,0:T(8,128)S(1)} all-to-all(f32[32,8,128]{2,1,0:T(8,128)S(1)} %bitcast.10), channel_id=1, replica_groups={{0,1,2,3,4,5,6,7,8,9,10,11,12,13,14,15,16,17,18,19,20,21,22,23,24,25,26..., dimensions={0} | all-to-all | bytes 262144 | tf_op jit(solution)/shard_map/all_to_all | solution.py:842
  60.9 0.1 shard_map.189
  61.0 7.0 %collective-permute-start.1 = (f32[8,128]{1,0:T(8,128)S(1)}, f32[8,128]{1,0:T(8,128)S(1)}, u32[]{:S(2)}, u32[]{:S(2)}) collective-permute-start(f32[8,128]{1,0:T(8,128)S(1)} %shard_map.189), channel_id=1, source_target_pairs={{6,6},{32,16},{68,20},{112,0},{150,22},{161,17},{212,4},{241,1},{2... | collective-permute-start | bytes 12296 | tf_op jit(solution)/shard_map/ppermute | solution.py:865
  68.0 0.0 copy-start.6
  68.0 0.0 copy-start.7
  68.1 1.5 %shard_map.187 = (f32[3,32,128]{2,1,0:T(8,128)S(1)}, f32[3,32,128]{2,1,0:T(8,128)}, f32[32,4,128]{2,1,0:T(4,128)S(1)}) custom-call(f32[256,128]{1,0:T(8,128)S(1)} %bitcast.7, bf16[56,80]{1,0:T(8,128)(2,1)S(1)} %copy-done, f32[2,3,32,128]{3,2,1,0:T(8,128)S(1)} %get-tuple-element.51.refs_2_, f32[2,3,24,128]{3,2,1,0:T(8,128)S(1)} %get-tuple-element.52.refs_3_, ...), custom_call_target="tpu_custom_call" | custom-call | tf_op jit(solution)/shard_map/pallas_call | solution.py:793
  69.6 1.2 %shard_map.188 = (f32[1,3,32,128]{3,2,1,0:T(8,128)S(1)}, f32[1,3,24,128]{3,2,1,0:T(8,128)S(1)}, f32[28,128]{1,0:T(8,128)}, f32[28,128]{1,0:T(8,128)}, f32[28,128]{1,0:T(8,128)}) custom-call(bf16[112,96]{1,0:T(8,128)(2,1)S(1)} %copy-done.1, bf16[24,96]{1,0:T(8,128)(2,1)S(1)} %copy-done.3, bf16[64,96]{1,0:T(8,128)(2,1)S(1)} %copy-done.2, ...), custom_call_target="tpu_custom_call" | custom-call | tf_op jit(solution)/shard_map/pallas_call | solution.py:793
  70.7 0.0 collective-permute-done.1.value_ref
  70.8 13.8 %all_to_all.41.refs_0_ = f32[32,4,128]{2,1,0:T(4,128)S(1)} all-to-all(f32[32,4,128]{2,1,0:T(4,128)S(1)} %shard_map.190), channel_id=1, replica_groups={{0,1,2,3,4,5,6,7,8,9,10,11,12,13,14,15,16,17,18,19,20,21,22,23,24,25,26..., dimensions={0} | all-to-all | bytes 131072 | tf_op jit(solution)/shard_map/all_to_all | solution.py:842
  84.5 1.1 %shard_map.191 = (f32[3,28,128]{2,1,0:T(8,128)}, f32[1]{0:T(128)}) custom-call(f32[32,4,128]{2,1,0:T(4,128)S(1)} %all_to_all.41.refs_0_, bf16[56,80]{1,0:T(8,128)(2,1)S(1)} %copy-done, f32[1,3,32,128]{3,2,1,0:T(8,128)S(1)} %get-tuple-element.59.refs_2_, f32[1,3,24,128]{3,2,1,0:T(8,128)S(1)} %get-tuple-element.60.refs_3_, ...), custom_call_target="tpu_custom_call" | custom-call | tf_op jit(solution)/shard_map/pallas_call | solution.py:793
  (21 shorter events, 0.1 us)
Async XLA Ops:
  0.6 1.0 %copy-start.9 = (s32[8,16]{1,0:T(8,128)S(1)}, s32[8,16]{1,0:T(8,128)}, u32[]{:S(2)}) copy-start(s32[8,16]{1,0:T(8,128)} %face_ref.1) | copy-start | bytes 1540
  0.6 1.0 %copy-start.11 = (s32[3,128]{1,0:T(4,128)S(1)}, s32[3,128]{1,0:T(4,128)}, u32[]{:S(2)}) copy-start(s32[3,128]{1,0:T(4,128)} %tag_ref.1) | copy-start | bytes 4612
  0.7 1.0 %copy-start.12 = (s32[3,128]{1,0:T(4,128)S(1)}, s32[3,128]{1,0:T(4,128)}, u32[]{:S(2)}) copy-start(s32[3,128]{1,0:T(4,128)} %link_ref.1) | copy-start | bytes 4612
  0.7 1.0 %copy-start.10 = (f32[4,128]{1,0:T(4,128)S(1)}, f32[4,128]{1,0:T(4,128)}, u32[]{:S(2)}) copy-start(f32[4,128]{1,0:T(4,128)} %metric_ref.1) | copy-start | bytes 6148
  0.7 1.0 %copy-start.8 = (f32[28,128]{1,0:T(8,128)S(1)}, f32[28,128]{1,0:T(8,128)}, u32[]{:S(2)}) copy-start(f32[28,128]{1,0:T(8,128)} %depth_ref.1) | copy-start | bytes 43012
  0.7 1.0 %copy-start.5 = (f32[3,28,128]{2,1,0:T(8,128)S(1)}, f32[3,28,128]{2,1,0:T(8,128)}, u32[]{:S(2)}) copy-start(f32[3,28,128]{2,1,0:T(8,128)} %lam_ref.1) | copy-start | bytes 129028
  1.7 1.4 %copy-start = (bf16[56,80]{1,0:T(8,128)(2,1)S(1)}, bf16[56,80]{1,0:T(8,128)(2,1)}, u32[]{:S(2)}) copy-start(bf16[56,80]{1,0:T(8,128)(2,1)} %constant.14.clone.refs_4_.refs_1_) | copy-start | bytes 26884
  1.7 1.4 %copy-start.1 = (bf16[112,96]{1,0:T(8,128)(2,1)S(1)}, bf16[112,96]{1,0:T(8,128)(2,1)}, u32[]{:S(2)}) copy-start(bf16[112,96]{1,0:T(8,128)(2,1)} %constant.10.clone.refs_0_) | copy-start | bytes 64516
  1.8 1.4 %copy-start.2 = (bf16[64,96]{1,0:T(8,128)(2,1)S(1)}, bf16[64,96]{1,0:T(8,128)(2,1)}, u32[]{:S(2)}) copy-start(bf16[64,96]{1,0:T(8,128)(2,1)} %constant.12.clone.refs_2_) | copy-start | bytes 36868
  1.8 1.4 %copy-start.3 = (bf16[24,96]{1,0:T(8,128)(2,1)S(1)}, bf16[24,96]{1,0:T(8,128)(2,1)}, u32[]{:S(2)}) copy-start(bf16[24,96]{1,0:T(8,128)(2,1)} %constant.11.clone.flip3.refs_1_) | copy-start | bytes 13828
  1.8 1.4 %copy-start.4 = (bf16[24,64]{1,0:T(8,128)(2,1)S(1)}, bf16[24,64]{1,0:T(8,128)(2,1)}, u32[]{:S(2)}) copy-start(bf16[24,64]{1,0:T(8,128)(2,1)} %constant.13.clone.refs_3_) | copy-start | bytes 9220
  1.8 2.0 %collective-permute-start = (f32[392,128]{1,0:T(8,128)S(1)}, f32[392,128]{1,0:T(8,128)S(1)}, u32[]{:S(2)}, u32[]{:S(2)}) collective-permute-start(f32[392,128]{1,0:T(8,128)S(1)} %shard_map.182.part_ref.refs_6_.refs_8_.refs_4_.refs_7_), channel_id=1, source_target_pairs={{0,0},{1,1},{2,2},{3,3},{4,4},{5,5},{6,6},{7,7},{8,8},{9,9},{10,10... | collective-permute-start | bytes 602120 | tf_op jit(solution)/shard_map/ppermute | solution.py:829
  61.0 9.7 %collective-permute-start.1 = (f32[8,128]{1,0:T(8,128)S(1)}, f32[8,128]{1,0:T(8,128)S(1)}, u32[]{:S(2)}, u32[]{:S(2)}) collective-permute-start(f32[8,128]{1,0:T(8,128)S(1)} %shard_map.189), channel_id=1, source_target_pairs={{6,6},{32,16},{68,20},{112,0},{150,22},{161,17},{212,4},{241,1},{2... | collective-permute-start | bytes 12296 | tf_op jit(solution)/shard_map/ppermute | solution.py:865
  68.0 1.5 %copy-start.6 = (f32[28,128]{1,0:T(8,128)S(1)}, f32[28,128]{1,0:T(8,128)}, u32[]{:S(2)}) copy-start(f32[28,128]{1,0:T(8,128)} %refs_12_.1) | copy-start | bytes 43012
  68.0 1.5 %copy-start.7 = (f32[28,128]{1,0:T(8,128)S(1)}, f32[28,128]{1,0:T(8,128)}, u32[]{:S(2)}) copy-start(f32[28,128]{1,0:T(8,128)} %refs_13_.1) | copy-start | bytes 43012

commit v7 on v6

--- a/solution.py
+++ b/solution.py
@@ -352,11 +352,13 @@
 
 
 def own_first_kernel(part_ref, flip3, drag_ref, *refs):
-    sends_ref, boxes_ref, rate_ref, near_ref, far_ref, last_ref = refs[-6:]
+    tables, state_ref = refs[0:5], refs[5]
+    sends_ref, boxes_ref, rate_ref, near_ref, far_ref, last_ref = refs[6:12]
     links = part_ref[8:11, :].astype(jnp.int32)
     near_ref[...], far_ref[...] = near_match(links), far_match(links)
     last_ref[...] = far_match(links, 4)
     rate_ref[...] = jnp.full((8, E), drag_ref[0], F32)
+    near_kernel(3, 1, *tables, rate_ref, part_ref, part_ref, near_ref, state_ref, *refs[12:])
     sends_ref[...], boxes_ref[...] = first_boxes(part_ref, flip3, 0)
 
 
@@ -378,7 +380,7 @@
     return jnp.concatenate([jnp.where(x, 1.0, 0.0).astype(BF16) for x in found], axis=1)
 
 
-def near_kernel(section, blocks, *refs):
+def near_kernel(section, blocks, *refs, light=False):
     refs = list(refs)
     back3, flip3, grad3, take2, spread3 = [refs.pop(0)[...] for _ in range(5)]
     rate_ref = refs.pop(0)
@@ -386,7 +388,7 @@
     parts = [refs.pop(0) for _ in range(blocks)]
     matches = [refs.pop(0) for _ in range(blocks)]
     old_ref = refs.pop(0) if section < 3 else None
-    if section == 3:
+    if section == 3 and not light:
         state_ref = refs.pop(0)
     if section == 0:
         state_ref, lam3_ref = refs.pop(0), refs.pop(0)
@@ -395,9 +397,11 @@
     if section > 0:
         ahead_ref = refs.pop(0)
     motion_ref = refs.pop(0)
-    if section == 3:
+    if section == 3 and not light:
         past_ref = refs.pop(0)
-    if section > 0:
+    if light:
+        pass
+    elif section > 0:
         sum_ref = refs.pop(0)
     else:
         depth_out, speed_out, angle_out = refs.pop(0), refs.pop(0), refs.pop(0)
@@ -422,7 +426,7 @@
     hi, lo = halves(fields)
     at_faces = dot(take2, jnp.concatenate([hi, lo], axis=0).astype(BF16))
 
-    if section == 3:
+    if section == 3 and not light:
         fields = [jnp.concatenate([state_ref[0, c], pad], axis=0) for c in range(3)]
         fields += [field(parts[0], 9 + c, 1.0) for c in range(3)]
         hi, lo = halves(jnp.concatenate(fields, axis=1))
@@ -531,6 +535,8 @@
             ahead = times3(flip3, later * jnp.concatenate(bases, axis=1))
             for c in range(3):
                 ahead_ref[b, c] = ahead[:, 128 * c : 128 * c + 128]
+    if light:
+        return
     w1, w2 = w[0][1], w[0][2]
     g1, g2 = height * w1, height * w2
     if section == 3:
@@ -726,16 +732,16 @@
 def round3_kernel(*refs):
     refs = list(refs)
     take = lambda n: [refs.pop(0) for _ in range(n)]
-    tables, parts, (state_ref, y_ref), sends = take(6), take(2), take(2), take(2)
-    my_near, my_far = take(2)
-    lams, (x_ref, normal_ref, sum_ref, halo_near, halo_far) = take(2), take(5)
-    base, ahead, motion, past = refs
+    tables, parts, (y_ref,), sends = take(6), take(2), take(1), take(2)
+    (my_far,), done, (past,) = take(1), take(3), take(1)
+    lams, (x_ref, normal_ref, halo_near, halo_far) = take(2), take(4)
+    base, ahead, motion, *theirs = refs
     links = parts[1][8:11, :].astype(jnp.int32)
     halo_near[...], halo_far[...] = near_match(links), far_match(links)
-    near_kernel(
-        3, 2, *tables, *parts, *parts, my_near, halo_near, state_ref,
-        base, ahead, motion, past, sum_ref,
-    )
+    near_kernel(3, 1, *tables, parts[1], parts[1], halo_near, *theirs, light=True)
+    for both, ours, other in zip((base, ahead, motion), done, theirs):
+        both[0] = ours[0]
+        both[1] = other[0]
     far_kernel(
         3, 2, y_ref, tables[4], base, motion, *parts, my_far, halo_far, ahead, *sends, past,
         *lams, x_ref, normal_ref,
@@ -830,10 +836,11 @@
     both = [mine, halo]
 
     near_out, far_out = ((3 * E, 3 * E), BF16), ((128, 3 * E), BF16)
-    my_sends, boxes, rate, my_near, my_far, my_last = call(
+    my_sends, boxes, rate, my_near, my_far, my_last, *near3, past, sums = call(
         own_first_kernel,
-        [sends_out, ((64, 128), F32), ((8, E), F32), near_out, far_out, far_out],
-        [mine, flip3, drag_rate] + tables,
+        [sends_out, ((64, 128), F32), ((8, E), F32), near_out, far_out, far_out]
+        + [((1, 3, 32, E), F32), ((1, 3, 24, E), F32), ((1, 3, 24, E), F32), ((4, 24, E), F32), sums_out],
+        [mine, flip3, drag_rate] + tables + [saved_states],
         smem=(2,),
     )
     tables.append(rate)
@@ -846,11 +853,11 @@
     sends = [my_sends, halo_sends]
 
     y = exchange(x)
-    lam3, _, x, normals, sums, halo_near, halo_far = got = call(
+    lam3, _, x, normals, halo_near, halo_far = got = call(
         round3_kernel,
-        far_outs + [((2, 3, 8, E), F32), sums_out, near_out, far_out],
-        tables + both + [saved_states, y] + sends + [my_near, my_far],
-        scratch=[bases, faces, faces, ((4, 24, E), F32)],
+        far_outs + [((2, 3, 8, E), F32), near_out, far_out],
+        tables + both + [y] + sends + [my_far] + near3 + [past],
+        scratch=[bases, faces, faces] + [((1,) + shape[1:], F32) for shape, _ in (bases, faces, faces)],
     )
     y = exchange(x)
     x, base, ahead, motion, sums = call(

time: 86 us -> 85.8 us (level)
  no operation moved by 1% of the time
where the time goes in v7:
time: 85.8 us; the launch traced here: 85.4 us
  blocking collectives  66.7 us (78%)
  Pallas kernels  8.42 us (10%)
  starting transfers between devices  7.71 us (9%)
  between operations  1.53 us (2%)
  local copies, waits for them, and re-layouts  1.05 us (1%)
    all_to_all x4, blocking collectives, exchange(): return lax.all_to_all(x, 'dom', 0, 0, tiled=True, axis_index_groups=groups)  66.7 us
    pallas_call x10, Pallas kernels, call(): pl.pallas_call(kernel, in_specs=[scalar if i in smem else vmem for i in r...  8.42 us
    ppermute x1, starting transfers between devices, local(): within = lax.ppermute(within, 'dom', spread_pairs(devices))  7.04 us
  transfers between devices with their start and end apart: 2, of which 0 were waited for; matrix products, arithmetic and copies ran while one was open for 0% of the time, Pallas kernels for 4%

profile of v7, /device:TPU:1, one launch (start us, length us, event | category | flops | bytes accessed | tf_op | source)
XLA Modules:
  0.0 85.4 jit_solution(9843006199725316405)
XLA Ops:
  0.7 1.0 %copy.20.q_ref.refs_5_.refs_11_.refs_10_ = f32[4,3,28,128]{3,2,1,0:T(8,128)S(1)} copy(f32[4,3,28,128]{3,0,2,1:T(4,128)} %param.15) | data formatting | bytes 344064 | tf_op args[0]
  1.7 0.0 copy-start
  1.7 0.0 copy-start.1
  1.8 0.0 copy-start.2
  1.8 0.0 copy-start.3
  1.8 0.0 copy-start.4
  1.8 0.7 collective-permute-start
  3.2 1.0 %shard_map.183 = (bf16[128,384]{1,0:T(8,128)(2,1)S(1)}, f32[64,128]{1,0:T(8,128)S(1)}, f32[8,128]{1,0:T(8,128)S(1)}, bf16[384,384]{1,0:T(8,128)(2,1)S(1)}, bf16[...) custom-call(f32[392,128]{1,0:T(8,128)S(1)} %shard_map.182.part_ref.r, ...), custom_call_target="tpu_custom_call" | custom-call | tf_op jit(solution)/shard_map/pallas_call | solution.py:799
  4.2 0.0 collective-permute-done.part_ref.refs_7_.refs_9_.refs_5_
  4.2 0.6 shard_map.184
  4.8 27.9 %all_to_all.38 = f32[32,8,128]{2,1,0:T(8,128)S(1)} all-to-all(f32[32,8,128]{2,1,0:T(8,128)S(1)} %bitcast.12), channel_id=1, replica_groups={{0,1,2,3,4,5,6,7,8,9,10,11,12,13,14,15,16,17,18,19,20,21,22,23,24,25,26..., dimensions={0} | all-to-all | bytes 262144 | tf_op jit(solution)/shard_map/all_to_all | solution.py:849
  32.7 1.3 %shard_map.185 = (f32[3,32,128]{2,1,0:T(8,128)S(1)}, f32[3,32,128]{2,1,0:T(8,128)S(1)}, f32[256,128]{1,0:T(8,128)S(1)}, f32[2,3,8,128]{3,2,1,0:T(8,128)S(1)}, bf...) custom-call(bf16[112,96]{1,0:T(8,128)(2,1)S(1)} %copy-done.1, bf16[24,96]{1,0:T(8,128)(2,1)S(1)} %copy-done.3, ...), custom_call_target="tpu_custom_call" | custom-call | tf_op jit(solution)/shard_map/pallas_call | solution.py:799
  34.0 12.5 %all_to_all.39 = f32[32,8,128]{2,1,0:T(8,128)S(1)} all-to-all(f32[32,8,128]{2,1,0:T(8,128)S(1)} %bitcast.10), channel_id=1, replica_groups={{0,1,2,3,4,5,6,7,8,9,10,11,12,13,14,15,16,17,18,19,20,21,22,23,24,25,26..., dimensions={0} | all-to-all | bytes 262144 | tf_op jit(solution)/shard_map/all_to_all | solution.py:849
  46.5 1.7 %shard_map.186 = (f32[256,128]{1,0:T(8,128)S(1)}, f32[2,3,32,128]{3,2,1,0:T(8,128)S(1)}, f32[2,3,24,128]{3,2,1,0:T(8,128)S(1)}, f32[2,3,24,128]{3,2,1,0:T(8,128)S(1)}, f32[5,32,128]{2,1,0:T(8,128)S(1)}) custom-call(bf16[112,96]{1,0:T(8,128)(2,1)S(1)} %copy-done.1, bf16[24,96]{1,0:T(8,128)(2,1)S(1)} %copy-done.3, bf16[64,96]{1,0:T(8,128)(2,1)S(1)} %copy-done.2, ...), custom_call_target="tpu_custom_call" | custom-call | tf_op jit(solution)/shard_map/pallas_call | solution.py:799
  48.2 12.5 %all_to_all.40 = f32[32,8,128]{2,1,0:T(8,128)S(1)} all-to-all(f32[32,8,128]{2,1,0:T(8,128)S(1)} %bitcast.11), channel_id=1, replica_groups={{0,1,2,3,4,5,6,7,8,9,10,11,12,13,14,15,16,17,18,19,20,21,22,23,24,25,26..., dimensions={0} | all-to-all | bytes 262144 | tf_op jit(solution)/shard_map/all_to_all | solution.py:849
  60.7 0.1 shard_map.189
  60.8 7.0 %collective-permute-start.1 = (f32[8,128]{1,0:T(8,128)S(1)}, f32[8,128]{1,0:T(8,128)S(1)}, u32[]{:S(2)}, u32[]{:S(2)}) collective-permute-start(f32[8,128]{1,0:T(8,128)S(1)} %shard_map.189), channel_id=1, source_target_pairs={{6,6},{32,16},{68,20},{112,0},{150,22},{161,17},{212,4},{241,1},{2... | collective-permute-start | bytes 12296 | tf_op jit(solution)/shard_map/ppermute | solution.py:872
  67.9 0.0 copy-start.6
  67.9 0.0 copy-start.7
  67.9 1.5 %shard_map.187 = (f32[3,32,128]{2,1,0:T(8,128)S(1)}, f32[3,32,128]{2,1,0:T(8,128)}, f32[32,4,128]{2,1,0:T(4,128)S(1)}) custom-call(f32[256,128]{1,0:T(8,128)S(1)} %bitcast.7, bf16[56,80]{1,0:T(8,128)(2,1)S(1)} %copy-done, f32[2,3,32,128]{3,2,1,0:T(8,128)S(1)} %get-tuple-element.59.refs_2_, f32[2,3,24,128]{3,2,1,0:T(8,128)S(1)} %get-tuple-element.60.refs_3_, ...), custom_call_target="tpu_custom_call" | custom-call | tf_op jit(solution)/shard_map/pallas_call | solution.py:799
  69.4 1.2 %shard_map.188 = (f32[1,3,32,128]{3,2,1,0:T(8,128)S(1)}, f32[1,3,24,128]{3,2,1,0:T(8,128)S(1)}, f32[28,128]{1,0:T(8,128)}, f32[28,128]{1,0:T(8,128)}, f32[28,128]{1,0:T(8,128)}) custom-call(bf16[112,96]{1,0:T(8,128)(2,1)S(1)} %copy-done.1, bf16[24,96]{1,0:T(8,128)(2,1)S(1)} %copy-done.3, bf16[64,96]{1,0:T(8,128)(2,1)S(1)} %copy-done.2, ...), custom_call_target="tpu_custom_call" | custom-call | tf_op jit(solution)/shard_map/pallas_call | solution.py:799
  70.6 0.0 collective-permute-done.1.value_ref
  70.6 13.8 %all_to_all.41.refs_0_ = f32[32,4,128]{2,1,0:T(4,128)S(1)} all-to-all(f32[32,4,128]{2,1,0:T(4,128)S(1)} %shard_map.190), channel_id=1, replica_groups={{0,1,2,3,4,5,6,7,8,9,10,11,12,13,14,15,16,17,18,19,20,21,22,23,24,25,26..., dimensions={0} | all-to-all | bytes 131072 | tf_op jit(solution)/shard_map/all_to_all | solution.py:849
  84.3 1.1 %shard_map.191 = (f32[3,28,128]{2,1,0:T(8,128)}, f32[1]{0:T(128)}) custom-call(f32[32,4,128]{2,1,0:T(4,128)S(1)} %all_to_all.41.refs_0_, bf16[56,80]{1,0:T(8,128)(2,1)S(1)} %copy-done, f32[1,3,32,128]{3,2,1,0:T(8,128)S(1)} %get-tuple-element.67.refs_2_, f32[1,3,24,128]{3,2,1,0:T(8,128)S(1)} %get-tuple-element.68.refs_3_, ...), custom_call_target="tpu_custom_call" | custom-call | tf_op jit(solution)/shard_map/pallas_call | solution.py:799
  (21 shorter events, 0.1 us)
Async XLA Ops:
  0.6 1.0 %copy-start.9 = (s32[8,16]{1,0:T(8,128)S(1)}, s32[8,16]{1,0:T(8,128)}, u32[]{:S(2)}) copy-start(s32[8,16]{1,0:T(8,128)} %face_ref.1) | copy-start | bytes 1540
  0.6 1.0 %copy-start.11 = (s32[3,128]{1,0:T(4,128)S(1)}, s32[3,128]{1,0:T(4,128)}, u32[]{:S(2)}) copy-start(s32[3,128]{1,0:T(4,128)} %tag_ref.1) | copy-start | bytes 4612
  0.7 1.0 %copy-start.12 = (s32[3,128]{1,0:T(4,128)S(1)}, s32[3,128]{1,0:T(4,128)}, u32[]{:S(2)}) copy-start(s32[3,128]{1,0:T(4,128)} %link_ref.1) | copy-start | bytes 4612
  0.7 1.0 %copy-start.10 = (f32[4,128]{1,0:T(4,128)S(1)}, f32[4,128]{1,0:T(4,128)}, u32[]{:S(2)}) copy-start(f32[4,128]{1,0:T(4,128)} %metric_ref.1) | copy-start | bytes 6148
  0.7 1.0 %copy-start.8 = (f32[28,128]{1,0:T(8,128)S(1)}, f32[28,128]{1,0:T(8,128)}, u32[]{:S(2)}) copy-start(f32[28,128]{1,0:T(8,128)} %depth_ref.1) | copy-start | bytes 43012
  0.7 1.0 %copy-start.5 = (f32[3,28,128]{2,1,0:T(8,128)S(1)}, f32[3,28,128]{2,1,0:T(8,128)}, u32[]{:S(2)}) copy-start(f32[3,28,128]{2,1,0:T(8,128)} %lam_ref.1) | copy-start | bytes 129028
  1.7 1.4 %copy-start = (bf16[56,80]{1,0:T(8,128)(2,1)S(1)}, bf16[56,80]{1,0:T(8,128)(2,1)}, u32[]{:S(2)}) copy-start(bf16[56,80]{1,0:T(8,128)(2,1)} %constant.14.clone.refs_4_.refs_1_) | copy-start | bytes 26884
  1.7 1.4 %copy-start.1 = (bf16[112,96]{1,0:T(8,128)(2,1)S(1)}, bf16[112,96]{1,0:T(8,128)(2,1)}, u32[]{:S(2)}) copy-start(bf16[112,96]{1,0:T(8,128)(2,1)} %constant.10.clone.refs_0_) | copy-start | bytes 64516
  1.8 1.4 %copy-start.2 = (bf16[64,96]{1,0:T(8,128)(2,1)S(1)}, bf16[64,96]{1,0:T(8,128)(2,1)}, u32[]{:S(2)}) copy-start(bf16[64,96]{1,0:T(8,128)(2,1)} %constant.12.clone.refs_2_) | copy-start | bytes 36868
  1.8 1.4 %copy-start.3 = (bf16[24,96]{1,0:T(8,128)(2,1)S(1)}, bf16[24,96]{1,0:T(8,128)(2,1)}, u32[]{:S(2)}) copy-start(bf16[24,96]{1,0:T(8,128)(2,1)} %constant.11.clone.flip3.refs_1_) | copy-start | bytes 13828
  1.8 1.4 %copy-start.4 = (bf16[24,64]{1,0:T(8,128)(2,1)S(1)}, bf16[24,64]{1,0:T(8,128)(2,1)}, u32[]{:S(2)}) copy-start(bf16[24,64]{1,0:T(8,128)(2,1)} %constant.13.clone.refs_3_) | copy-start | bytes 9220
  1.8 2.4 %collective-permute-start = (f32[392,128]{1,0:T(8,128)S(1)}, f32[392,128]{1,0:T(8,128)S(1)}, u32[]{:S(2)}, u32[]{:S(2)}) collective-permute-start(f32[392,128]{1,0:T(8,128)S(1)} %shard_map.182.part_ref.refs_6_.refs_8_.refs_4_.refs_7_), channel_id=1, source_target_pairs={{0,0},{1,1},{2,2},{3,3},{4,4},{5,5},{6,6},{7,7},{8,8},{9,9},{10,10... | collective-permute-start | bytes 602120 | tf_op jit(solution)/shard_map/ppermute | solution.py:835
  60.8 9.7 %collective-permute-start.1 = (f32[8,128]{1,0:T(8,128)S(1)}, f32[8,128]{1,0:T(8,128)S(1)}, u32[]{:S(2)}, u32[]{:S(2)}) collective-permute-start(f32[8,128]{1,0:T(8,128)S(1)} %shard_map.189), channel_id=1, source_target_pairs={{6,6},{32,16},{68,20},{112,0},{150,22},{161,17},{212,4},{241,1},{2... | collective-permute-start | bytes 12296 | tf_op jit(solution)/shard_map/ppermute | solution.py:872
  67.9 1.5 %copy-start.6 = (f32[28,128]{1,0:T(8,128)S(1)}, f32[28,128]{1,0:T(8,128)}, u32[]{:S(2)}) copy-start(f32[28,128]{1,0:T(8,128)} %refs_12_.1) | copy-start | bytes 43012
  67.9 1.5 %copy-start.7 = (f32[28,128]{1,0:T(8,128)S(1)}, f32[28,128]{1,0:T(8,128)}, u32[]{:S(2)}) copy-start(f32[28,128]{1,0:T(8,128)} %refs_13_.1) | copy-start | bytes 43012

commit v8 on v7

--- a/solution.py
+++ b/solution.py
@@ -871,10 +871,11 @@
     within = call(fold_kernel, [((8, 128), F32)], (y,))[0]
     within = lax.ppermute(within, "dom", spread_pairs(devices))
     last_out = ((GROUP, 4, 128), F32)
-    lam1, _, x = call(
-        lambda *refs: (far_kernel(1, 2, *refs), None)[1],
-        [mixed, mixed, last_out],
+    lam1, x = call(
+        lambda *refs: (far_kernel(1, 2, *refs[:-2], refs[-1], refs[-2]), None)[1],
+        [mixed, last_out],
         [y, spread3, base, motion] + both + [my_far, halo_far, normals, ahead],
+        scratch=[mixed],
     )
     args = tables + [lam1, mine, my_near, sums, saved_states, lam3, wind_speed, wind_angle]
     base, motion, depth_gradient, speed_gradient, angle_gradient = call(

time: 85.8 us -> 85.3 us (level)
  no operation moved by 1% of the time
where the time goes in v8:
time: 85.3 us; the launch traced here: 84.9 us
  blocking collectives  66.7 us (78%)
  Pallas kernels  7.91 us (9%)
  starting transfers between devices  7.71 us (9%)
  between operations  1.53 us (2%)
  local copies, waits for them, and re-layouts  1.05 us (1%)
    all_to_all x4, blocking collectives, exchange(): return lax.all_to_all(x, 'dom', 0, 0, tiled=True, axis_index_groups=groups)  66.7 us
    pallas_call x10, Pallas kernels, call(): pl.pallas_call(kernel, in_specs=[scalar if i in smem else vmem for i in r...  7.91 us
    ppermute x1, starting transfers between devices, local(): within = lax.ppermute(within, 'dom', spread_pairs(devices))  7.04 us
  transfers between devices with their start and end apart: 2, of which 0 were waited for; matrix products, arithmetic and copies ran while one was open for 0% of the time, Pallas kernels for 4%

profile of v8, /device:TPU:1, one launch (start us, length us, event | category | flops | bytes accessed | tf_op | source)
XLA Modules:
  0.0 84.9 jit_solution(2246279979869719844)
XLA Ops:
  0.7 1.0 %copy.20.q_ref.refs_5_.refs_11_.refs_10_ = f32[4,3,28,128]{3,2,1,0:T(8,128)S(1)} copy(f32[4,3,28,128]{3,0,2,1:T(4,128)} %param.15) | data formatting | bytes 344064 | tf_op args[0]
  1.7 0.0 copy-start
  1.7 0.0 copy-start.1
  1.8 0.0 copy-start.2
  1.8 0.0 copy-start.3
  1.8 0.0 copy-start.4
  1.8 0.7 collective-permute-start
  3.2 1.0 %shard_map.183 = (bf16[128,384]{1,0:T(8,128)(2,1)S(1)}, f32[64,128]{1,0:T(8,128)S(1)}, f32[8,128]{1,0:T(8,128)S(1)}, bf16[384,384]{1,0:T(8,128)(2,1)S(1)}, bf16[...) custom-call(f32[392,128]{1,0:T(8,128)S(1)} %shard_map.182.part_ref.r, ...), custom_call_target="tpu_custom_call" | custom-call | tf_op jit(solution)/shard_map/pallas_call | solution.py:799
  4.2 0.0 collective-permute-done.part_ref.refs_7_.refs_9_.refs_5_
  4.2 0.6 shard_map.184
  4.8 27.9 %all_to_all.38 = f32[32,8,128]{2,1,0:T(8,128)S(1)} all-to-all(f32[32,8,128]{2,1,0:T(8,128)S(1)} %bitcast.12), channel_id=1, replica_groups={{0,1,2,3,4,5,6,7,8,9,10,11,12,13,14,15,16,17,18,19,20,21,22,23,24,25,26..., dimensions={0} | all-to-all | bytes 262144 | tf_op jit(solution)/shard_map/all_to_all | solution.py:849
  32.7 1.3 %shard_map.185 = (f32[3,32,128]{2,1,0:T(8,128)S(1)}, f32[3,32,128]{2,1,0:T(8,128)S(1)}, f32[256,128]{1,0:T(8,128)S(1)}, f32[2,3,8,128]{3,2,1,0:T(8,128)S(1)}, bf...) custom-call(bf16[112,96]{1,0:T(8,128)(2,1)S(1)} %copy-done.1, bf16[24,96]{1,0:T(8,128)(2,1)S(1)} %copy-done.3, ...), custom_call_target="tpu_custom_call" | custom-call | tf_op jit(solution)/shard_map/pallas_call | solution.py:799
  34.0 12.5 %all_to_all.39 = f32[32,8,128]{2,1,0:T(8,128)S(1)} all-to-all(f32[32,8,128]{2,1,0:T(8,128)S(1)} %bitcast.10), channel_id=1, replica_groups={{0,1,2,3,4,5,6,7,8,9,10,11,12,13,14,15,16,17,18,19,20,21,22,23,24,25,26..., dimensions={0} | all-to-all | bytes 262144 | tf_op jit(solution)/shard_map/all_to_all | solution.py:849
  46.5 1.7 %shard_map.186 = (f32[256,128]{1,0:T(8,128)S(1)}, f32[2,3,32,128]{3,2,1,0:T(8,128)S(1)}, f32[2,3,24,128]{3,2,1,0:T(8,128)S(1)}, f32[2,3,24,128]{3,2,1,0:T(8,128)S(1)}, f32[5,32,128]{2,1,0:T(8,128)S(1)}) custom-call(bf16[112,96]{1,0:T(8,128)(2,1)S(1)} %copy-done.1, bf16[24,96]{1,0:T(8,128)(2,1)S(1)} %copy-done.3, bf16[64,96]{1,0:T(8,128)(2,1)S(1)} %copy-done.2, ...), custom_call_target="tpu_custom_call" | custom-call | tf_op jit(solution)/shard_map/pallas_call | solution.py:799
  48.2 12.5 %all_to_all.40 = f32[32,8,128]{2,1,0:T(8,128)S(1)} all-to-all(f32[32,8,128]{2,1,0:T(8,128)S(1)} %bitcast.11), channel_id=1, replica_groups={{0,1,2,3,4,5,6,7,8,9,10,11,12,13,14,15,16,17,18,19,20,21,22,23,24,25,26..., dimensions={0} | all-to-all | bytes 262144 | tf_op jit(solution)/shard_map/all_to_all | solution.py:849
  60.7 0.1 shard_map.189
  60.8 7.0 %collective-permute-start.1 = (f32[8,128]{1,0:T(8,128)S(1)}, f32[8,128]{1,0:T(8,128)S(1)}, u32[]{:S(2)}, u32[]{:S(2)}) collective-permute-start(f32[8,128]{1,0:T(8,128)S(1)} %shard_map.189), channel_id=1, source_target_pairs={{6,6},{32,16},{68,20},{112,0},{150,22},{161,17},{212,4},{241,1},{2... | collective-permute-start | bytes 12296 | tf_op jit(solution)/shard_map/ppermute | solution.py:872
  67.9 0.0 copy-start.6
  67.9 0.0 copy-start.7
  67.9 1.0 %shard_map.187 = (f32[3,32,128]{2,1,0:T(8,128)S(1)}, f32[32,4,128]{2,1,0:T(4,128)S(1)}) custom-call(f32[256,128]{1,0:T(8,128)S(1)} %bitcast.7, bf16[56,80]{1,0:T(8,128)(2,1)S(1)} %copy-done, f32[2,3,32,128]{3,2,1,0:T(8,128)S(1)} %get-tuple-element.59.refs_2_, f32[2,3,24,128]{3,2,1,0:T(8,128)S(1)} %get-tuple-element.60.refs_3_, ...), custom_call_target="tpu_custom_call" | custom-call | tf_op jit(solution)/shard_map/pallas_call | solution.py:799
  68.9 1.2 %shard_map.188 = (f32[1,3,32,128]{3,2,1,0:T(8,128)S(1)}, f32[1,3,24,128]{3,2,1,0:T(8,128)S(1)}, f32[28,128]{1,0:T(8,128)}, f32[28,128]{1,0:T(8,128)}, f32[28,128]{1,0:T(8,128)}) custom-call(bf16[112,96]{1,0:T(8,128)(2,1)S(1)} %copy-done.1, bf16[24,96]{1,0:T(8,128)(2,1)S(1)} %copy-done.3, bf16[64,96]{1,0:T(8,128)(2,1)S(1)} %copy-done.2, ...), custom_call_target="tpu_custom_call" | custom-call | tf_op jit(solution)/shard_map/pallas_call | solution.py:799
  70.0 0.0 collective-permute-done.1.value_ref
  70.1 13.8 %all_to_all.41.refs_0_ = f32[32,4,128]{2,1,0:T(4,128)S(1)} all-to-all(f32[32,4,128]{2,1,0:T(4,128)S(1)} %shard_map.190), channel_id=1, replica_groups={{0,1,2,3,4,5,6,7,8,9,10,11,12,13,14,15,16,17,18,19,20,21,22,23,24,25,26..., dimensions={0} | all-to-all | bytes 131072 | tf_op jit(solution)/shard_map/all_to_all | solution.py:849
  83.8 1.1 %shard_map.191 = (f32[3,28,128]{2,1,0:T(8,128)}, f32[1]{0:T(128)}) custom-call(f32[32,4,128]{2,1,0:T(4,128)S(1)} %all_to_all.41.refs_0_, bf16[56,80]{1,0:T(8,128)(2,1)S(1)} %copy-done, f32[1,3,32,128]{3,2,1,0:T(8,128)S(1)} %get-tuple-element.67.refs_2_, f32[1,3,24,128]{3,2,1,0:T(8,128)S(1)} %get-tuple-element.68.refs_3_, ...), custom_call_target="tpu_custom_call" | custom-call | tf_op jit(solution)/shard_map/pallas_call | solution.py:799
  (21 shorter events, 0.1 us)
Async XLA Ops:
  0.6 1.0 %copy-start.9 = (s32[8,16]{1,0:T(8,128)S(1)}, s32[8,16]{1,0:T(8,128)}, u32[]{:S(2)}) copy-start(s32[8,16]{1,0:T(8,128)} %face_ref.1) | copy-start | bytes 1540
  0.6 1.0 %copy-start.11 = (s32[3,128]{1,0:T(4,128)S(1)}, s32[3,128]{1,0:T(4,128)}, u32[]{:S(2)}) copy-start(s32[3,128]{1,0:T(4,128)} %tag_ref.1) | copy-start | bytes 4612
  0.7 1.0 %copy-start.12 = (s32[3,128]{1,0:T(4,128)S(1)}, s32[3,128]{1,0:T(4,128)}, u32[]{:S(2)}) copy-start(s32[3,128]{1,0:T(4,128)} %link_ref.1) | copy-start | bytes 4612
  0.7 1.0 %copy-start.10 = (f32[4,128]{1,0:T(4,128)S(1)}, f32[4,128]{1,0:T(4,128)}, u32[]{:S(2)}) copy-start(f32[4,128]{1,0:T(4,128)} %metric_ref.1) | copy-start | bytes 6148
  0.7 1.0 %copy-start.8 = (f32[28,128]{1,0:T(8,128)S(1)}, f32[28,128]{1,0:T(8,128)}, u32[]{:S(2)}) copy-start(f32[28,128]{1,0:T(8,128)} %depth_ref.1) | copy-start | bytes 43012
  0.7 1.0 %copy-start.5 = (f32[3,28,128]{2,1,0:T(8,128)S(1)}, f32[3,28,128]{2,1,0:T(8,128)}, u32[]{:S(2)}) copy-start(f32[3,28,128]{2,1,0:T(8,128)} %lam_ref.1) | copy-start | bytes 129028
  1.7 1.4 %copy-start = (bf16[56,80]{1,0:T(8,128)(2,1)S(1)}, bf16[56,80]{1,0:T(8,128)(2,1)}, u32[]{:S(2)}) copy-start(bf16[56,80]{1,0:T(8,128)(2,1)} %constant.14.clone.refs_4_.refs_1_) | copy-start | bytes 26884
  1.7 1.4 %copy-start.1 = (bf16[112,96]{1,0:T(8,128)(2,1)S(1)}, bf16[112,96]{1,0:T(8,128)(2,1)}, u32[]{:S(2)}) copy-start(bf16[112,96]{1,0:T(8,128)(2,1)} %constant.10.clone.refs_0_) | copy-start | bytes 64516
  1.8 1.4 %copy-start.2 = (bf16[64,96]{1,0:T(8,128)(2,1)S(1)}, bf16[64,96]{1,0:T(8,128)(2,1)}, u32[]{:S(2)}) copy-start(bf16[64,96]{1,0:T(8,128)(2,1)} %constant.12.clone.refs_2_) | copy-start | bytes 36868
  1.8 1.4 %copy-start.3 = (bf16[24,96]{1,0:T(8,128)(2,1)S(1)}, bf16[24,96]{1,0:T(8,128)(2,1)}, u32[]{:S(2)}) copy-start(bf16[24,96]{1,0:T(8,128)(2,1)} %constant.11.clone.flip3.refs_1_) | copy-start | bytes 13828
  1.8 1.4 %copy-start.4 = (bf16[24,64]{1,0:T(8,128)(2,1)S(1)}, bf16[24,64]{1,0:T(8,128)(2,1)}, u32[]{:S(2)}) copy-start(bf16[24,64]{1,0:T(8,128)(2,1)} %constant.13.clone.refs_3_) | copy-start | bytes 9220
  1.8 2.4 %collective-permute-start = (f32[392,128]{1,0:T(8,128)S(1)}, f32[392,128]{1,0:T(8,128)S(1)}, u32[]{:S(2)}, u32[]{:S(2)}) collective-permute-start(f32[392,128]{1,0:T(8,128)S(1)} %shard_map.182.part_ref.refs_6_.refs_8_.refs_4_.refs_7_), channel_id=1, source_target_pairs={{0,0},{1,1},{2,2},{3,3},{4,4},{5,5},{6,6},{7,7},{8,8},{9,9},{10,10... | collective-permute-start | bytes 602120 | tf_op jit(solution)/shard_map/ppermute | solution.py:835
  60.8 9.2 %collective-permute-start.1 = (f32[8,128]{1,0:T(8,128)S(1)}, f32[8,128]{1,0:T(8,128)S(1)}, u32[]{:S(2)}, u32[]{:S(2)}) collective-permute-start(f32[8,128]{1,0:T(8,128)S(1)} %shard_map.189), channel_id=1, source_target_pairs={{6,6},{32,16},{68,20},{112,0},{150,22},{161,17},{212,4},{241,1},{2... | collective-permute-start | bytes 12296 | tf_op jit(solution)/shard_map/ppermute | solution.py:872
  67.9 1.0 %copy-start.6 = (f32[28,128]{1,0:T(8,128)S(1)}, f32[28,128]{1,0:T(8,128)}, u32[]{:S(2)}) copy-start(f32[28,128]{1,0:T(8,128)} %refs_12_.1) | copy-start | bytes 43012
  67.9 1.0 %copy-start.7 = (f32[28,128]{1,0:T(8,128)S(1)}, f32[28,128]{1,0:T(8,128)}, u32[]{:S(2)}) copy-start(f32[28,128]{1,0:T(8,128)} %refs_13_.1) | copy-start | bytes 43012
